TPU v7x, 32 devices: a whole 2x2x4 slice. The times are simulated.
32 devices in a mesh: groups: 2 (over x), space: 16 (over z, y, core).
Axes of the slice: x: 2, y: 2, z: 4, core: 2. Of those that a mesh axis runs over, the one named last changes fastest.
Arguments:
- model: float32 [128, 64, 128], P(('groups', 'space')), parts along dimension 0, may hold values from -3.35 to 3.35
- forward: bfloat16 [8, 128, 64, 128], P(None, ('groups', 'space')), parts along dimension 1, may hold values from -6 to 6
- warm_start: bfloat16 [8, 128, 64, 128], P(None, ('groups', 'space')), parts along dimension 1, may hold values from -6 to 6
- residual_data: float32 [16, 8, 256], P('groups'), parts along dimension 0, may hold values from -6 to 6
- electrodes: int32 [512], P('groups'), parts along dimension 0, may hold values from 0 to 65535
- survey_order: int32 [16], P('groups'), parts along dimension 0, may hold values from 0 to 7, each once
Outputs:
- adjoint: bfloat16 [8, 128, 64, 128], P(None, ('groups', 'space')), parts along dimension 1
- gradient: float32 [128, 64, 128], P(('groups', 'space')), parts along dimension 0
There are 2 independent parts, one for each index of `groups`. A program takes and returns all parts, laid end to end along the dimension named above; each array names one. Nothing has to cross between parts.
All inputs are finite; a program needn't handle non-finite values.
Results may differ from a plain program's by a relative error of at most 0.001.
Values sent between devices are 32-bit elements; how exact they have to be, the bound alone decides.
No kernel may reach another device: no remote copies, remote signals or barrier semaphores. Data moves between devices by JAX's collectives and lax.ppermute only.
A program may use at most 128 MiB of HBM per device.

v0:
```python
import jax
import jax.numpy as jnp
from jax import lax
from jax.sharding import PartitionSpec as P

SURVEYS = 8
ITERS = 4


GROUND = 0.5
CENTER = 1.0
HALF_WIDTH = 0.99


def padded(shard, sides, width):
    for axis, dim in sides:
        devices, length = (lax.axis_size(axis), shard.shape[dim])
        up = [(i, (i + 1) % devices) for i in range(devices)]
        down = [(j, i) for i, j in up]
        last = lax.slice_in_dim(shard, length - width, length, axis=dim)
        leading = lax.slice_in_dim(shard, 0, width, axis=dim)
        before = lax.ppermute(last, axis, up)
        after = lax.ppermute(leading, axis, down)
        shard = jnp.concatenate([before, shard, after], axis=dim)
    return shard


def swapped(value, axis, bit):
    mask = 2**bit
    pairs = [(source, source ^ mask) for source in range(lax.axis_size(axis))]
    return lax.ppermute(value, axis, pairs)


def face_diff(field, axis):
    count = field.shape[axis]
    return lax.slice_in_dim(field, 0, count - 1, axis=axis) - lax.slice_in_dim(
        field, 1, count, axis=axis
    )


def edge_zeros(field, axis):
    shape = list(field.shape)
    shape[axis] = 1
    return jnp.zeros(shape, jnp.float32)


def pad_diff(faces, axis):
    zeros = edge_zeros(faces, axis)
    return jnp.concatenate([faces, zeros], axis=axis) - jnp.concatenate([zeros, faces], axis=axis)


def pad_sum(faces, axis):
    zeros = edge_zeros(faces, axis)
    return jnp.concatenate([faces, zeros], axis=axis) + jnp.concatenate([zeros, faces], axis=axis)


def extend(field):
    return padded(field, (("space", 1),), 1)


def body(model, forward, warm_start, residual_data, electrodes, survey_order):
    sources, layers, rows_y, rows_z = forward.shape
    position = lax.axis_index("space")
    devices = lax.axis_size("space")
    tiles = devices // SURVEYS
    half_tiles = tiles // 2
    shifted = position + half_tiles
    tile = shifted % tiles
    survey = shifted // tiles % SURVEYS
    block = position // tiles
    rotation = jnp.where(position % tiles >= half_tiles, 1, 0).astype(jnp.int32)
    valid = jnp.ones((layers + 1,), jnp.float32)
    valid = valid.at[0].set(jnp.where(tile == 0, 0.0, 1.0))
    valid = valid.at[layers].set(jnp.where(tile == tiles - 1, 0.0, 1.0))
    valid_faces = valid[:, None, None]
    model_pad = padded(model, (("space", 0),), 1)
    sigma_pad = jnp.exp(model_pad)
    sigma = sigma_pad[1:-1]
    conduct_x = 0.5 * (sigma_pad[:-1] + sigma_pad[1:]) * valid_faces
    conduct_y = 0.5 * (sigma[:, :-1] + sigma[:, 1:])
    conduct_z = 0.5 * (sigma[:, :, :-1] + sigma[:, :, 1:])
    diagonal = (
        conduct_x[1:]
        + conduct_x[:-1]
        + pad_sum(conduct_y, 1)
        + pad_sum(conduct_z, 2)
        + GROUND * sigma
    )
    inverse_diag = (1.0 / diagonal)[None]

    def operate(field_pad):
        field = field_pad[:, 1:-1]
        flux_x = conduct_x[None] * (field_pad[:, :-1] - field_pad[:, 1:])
        total = flux_x[:, 1:] - flux_x[:, :-1]
        total = total + pad_diff(conduct_y[None] * face_diff(field, 2), 2)
        total = total + pad_diff(conduct_z[None] * face_diff(field, 3), 3)
        return total + GROUND * sigma[None] * field

    cells = layers * rows_y * rows_z
    residual = lax.dynamic_index_in_dim(residual_data, survey, 0, keepdims=False)
    local_index = electrodes - tile * cells
    inside = (local_index >= 0) & (local_index < cells)
    target = jnp.where(inside, local_index, 0)
    amount = jnp.where(inside[None, :], residual, 0.0)
    rhs = jnp.zeros((sources, cells), jnp.float32).at[:, target].add(amount)
    rhs = rhs.reshape(sources, layers, rows_y, rows_z)
    iterate = warm_start.astype(jnp.float32)
    remain = rhs - operate(extend(iterate))
    direction = remain * inverse_diag / CENTER
    weight_now = HALF_WIDTH / CENTER
    for sweep_index in range(ITERS):
        iterate = iterate + direction
        if sweep_index + 1 < ITERS:
            remain = remain - operate(extend(direction))
            weight_new = 1.0 / (2.0 * CENTER / HALF_WIDTH - weight_now)
            direction = weight_new * weight_now * direction + 2.0 * weight_new / HALF_WIDTH * (
                remain * inverse_diag
            )
            weight_now = weight_new
    both = padded(
        jnp.concatenate([forward.astype(jnp.float32), iterate], axis=0), (("space", 1),), 1
    )
    forward_pad = both[:sources]
    adjoint_pad = both[sources:]
    potential = forward_pad[:, 1:-1]
    product_x = (
        jnp.sum(
            (forward_pad[:, :-1] - forward_pad[:, 1:]) * (adjoint_pad[:, :-1] - adjoint_pad[:, 1:]),
            axis=0,
        )
        * valid_faces
    )
    terms = product_x[1:] + product_x[:-1]
    terms = terms + pad_sum(jnp.sum(face_diff(potential, 2) * face_diff(iterate, 2), axis=0), 1)
    terms = terms + pad_sum(jnp.sum(face_diff(potential, 3) * face_diff(iterate, 3), axis=0), 2)
    data_term = -sigma * (0.5 * terms + GROUND * jnp.sum(potential * iterate, axis=0))
    model_x = (model_pad[:-1] - model_pad[1:]) * valid_faces
    space_term = (
        model_x[1:]
        - model_x[:-1]
        + pad_diff(face_diff(model, 1), 1)
        + pad_diff(face_diff(model, 2), 2)
    )
    base_bit = tiles.bit_length() - 1
    collected = model
    for level in range(SURVEYS.bit_length() - 1):
        partner = swapped(collected, "space", base_bit + level)
        upper = block >> level & 1 == 1
        lower_half = jnp.where(upper, partner, collected)
        upper_half = jnp.where(upper, collected, partner)
        collected = jnp.concatenate([lower_half, upper_half], axis=0)
    all_blocks = collected.reshape(SURVEYS, layers, rows_y, rows_z)
    ranks = jnp.arange(SURVEYS, dtype=jnp.int32)
    placed = (survey_order[:, None] == ranks[None, :]).astype(jnp.float32)
    apart = jnp.abs(ranks[:, None] - ranks[None, :])
    degree = jnp.where((ranks == 0) | (ranks == SURVEYS - 1), 1.0, 2.0)
    path = jnp.where(apart == 0, degree[:, None], 0.0) - jnp.where(apart == 1, 1.0, 0.0)
    coupling = jnp.dot(
        placed.T,
        jnp.dot(path, placed, precision=lax.Precision.HIGHEST),
        precision=lax.Precision.HIGHEST,
    )
    row_weights = lax.dynamic_index_in_dim(coupling, survey, 0, keepdims=False)
    block_survey = (ranks + rotation) % SURVEYS
    picker = (block_survey[:, None] == ranks[None, :]).astype(jnp.float32)
    block_weights = jnp.dot(picker, row_weights, precision=lax.Precision.HIGHEST)
    time_term = jnp.sum(block_weights[:, None, None, None] * all_blocks, axis=0)
    return (iterate.astype(jnp.bfloat16), data_term + space_term + time_term)


def solution(mesh):
    in_specs = (
        P(("groups", "space"), None, None),
        P(None, ("groups", "space"), None, None),
        P(None, ("groups", "space"), None, None),
        P("groups", None, None),
        P("groups"),
        P("groups"),
    )
    out_specs = (P(None, ("groups", "space"), None, None), P(("groups", "space"), None, None))
    return jax.shard_map(body, mesh=mesh, in_specs=in_specs, out_specs=out_specs, check_vma=False)
```

profile of v0, /device:TPU:14, one launch (start us, length us, event | category | flops | bytes accessed | tf_op | source)
XLA Modules:
  0.0 97.1 jit_solution(17605388691630219357)
XLA Ops:
  0.7 0.6 collective-permute-start.12
  1.2 1.4 %fusion.89 = (f32[1,64,128]{2,1,0:T(8,128)}, f32[1,64,128]{2,1,0:T(8,128)}) fusion(f32[4,64,128]{2,1,0:T(8,128)} %param.10), kind=kLoop, calls=%fused_computation.150 | loop fusion | bytes 131072 | tf_op jit(solution)/shard_map/slice | solution.py:20
  2.7 1.7 %collective-permute-start.1 = (f32[1,64,128]{2,1,0:T(8,128)}, f32[1,64,128]{2,1,0:T(8,128)}, u32[]{:S(2)}, u32[]{:S(2)}) collective-permute-start(f32[1,64,128]{2,1,0:T(8,128)} %get-tuple-element.55), channel_id=1, source_target_pairs={{1,0},{2,1},{3,2},{4,3},{5,4},{6,5},{7,6},{8,7},{9,8},{10,9},{11,1... | collective-permute-start | bytes 98312 | tf_op jit(solution)/shard_map/ppermute | solution.py:23
  4.4 1.8 %fusion.88 = (f32[8,1,64,128]{3,2,1,0:T(8,128)}, f32[8,1,64,128]{3,2,1,0:T(8,128)}) fusion(bf16[8,4,64,128]{3,2,1,0:T(8,128)(2,1)} %param.12), kind=kLoop, calls=%fused_computation.149 | loop fusion | bytes 1048576 | tf_op jit(solution)/shard_map/slice | solution.py:21
  6.2 0.9 collective-permute-start.2
  7.1 0.8 collective-permute-start.3
  8.0 0.7 compare_and_fusion
  8.6 0.7 compare_select_fusion
  9.5 0.2 fusion.58
  9.7 0.3 fusion.64
  10.0 0.7 fusion.57
  10.7 0.2 convolution_bitcast_fusion
  11.2 8.4 %scatter_custom_fusion = f32[8,32768]{0,1:T(8,128)} fusion(s32[256]{0:T(256)S(1)} %compare_select_fusion, f32[256,8]{1,0:T(8,128)S(1)} %copy.9, f32[]{:T(128)} %constant.135.clone.1), kind=kCustom, calls=%fused_computation.1 | custom fusion | flops 2048 | bytes 1048580 | tf_op jit(solution)/shard_map/scatter-add | solution.py:105
  19.5 10.7 %copy.10 = f32[8,4,64,128]{3,2,1,0:T(8,128)} copy(f32[8,4,64,128]{0,3,2,1:T(8,128)} %bitcast.17) | data formatting | bytes 2097152 | tf_op jit(solution)/shard_map/reshape | solution.py:106
  30.3 0.8 maximum_exponential_fusion
  31.4 0.3 fusion.34
  32.0 0.9 broadcast_select_fusion.5
  33.0 0.5 collective-permute-start.13
  33.5 1.2 %fusion.4 = f32[8,5,64,128]{3,2,1,0:T(8,128)S(1)} fusion(f32[8,4,64,128]{3,2,1,0:T(8,128)S(1)} %convert_element_type.11, f32[8,1,64,128]{3,2,1,0:T(8,128)} %collective-permute-done.2, f32[8,1,64,128]{3,2,1,0:T(8,128)} %collective-permute-done.3, f32[5,64,128]{2,1,0:T(8,128)S(1)} %fusion.40), kind=kLoop, calls=%fused_computation.10 | loop fusion | flops 1310720 | bytes 3047424 | tf_op jit(solution)/shard_map/mul | solution.py:93
  34.7 0.7 broadcast_multiply_fusion
  35.7 1.6 %collective-permute-start.4 = (f32[8,1,64,128]{3,2,1,0:T(8,128)S(1)}, f32[8,1,64,128]{3,2,1,0:T(8,128)S(1)}, u32[]{:S(2)}, u32[]{:S(2)}) collective-permute-start(f32[8,1,64,128]{3,2,1,0:T(8,128)S(1)} %get-tuple-element.45), channel_id=1, source_target_pairs={{0,1},{1,2},{2,3},{3,4},{4,5},{5,6},{6,7},{7,8},{8,9},{9,10},{10,1... | collective-permute-start | bytes 786440 | tf_op jit(solution)/shard_map/ppermute | solution.py:22
  37.3 0.8 collective-permute-start.5
  38.1 0.3 fusion.28
  38.4 3.0 %collective-permute-done.13 = f32[8,64,128]{2,1,0:T(8,128)S(1)} collective-permute-done((f32[8,64,128]{2,1,0:T(8,128)S(1)}, f32[8,64,128]{2,1,0:T(8,128)S(1)}, u32[]{:S(2)}, u32[]{:S(2)}) %collective-permute-start.13) | collective-permute-done | bytes 262176 | tf_op jit(solution)/shard_map/ppermute | solution.py:31
  41.5 2.1 %collective-permute-start.14 = (f32[16,64,128]{2,1,0:T(8,128)S(1)}, f32[16,64,128]{2,1,0:T(8,128)S(1)}, u32[]{:S(2)}, u32[]{:S(2)}) collective-permute-start(f32[16,64,128]{2,1,0:T(8,128)S(1)} %pad_maximum_fusion.4), channel_id=1, source_target_pairs={{0,8},{1,9},{2,10},{3,11},{4,12},{5,13},{6,14},{7,15},{8,0},{9,1},... | collective-permute-start | bytes 1572872 | tf_op jit(solution)/shard_map/ppermute | solution.py:31
  43.8 0.8 multiply_add_fusion.1
  44.7 0.2 fusion.23
  44.9 18.4 %collective-permute-start.6 = (f32[8,1,64,128]{3,2,1,0:T(8,128)S(1)}, f32[8,1,64,128]{3,2,1,0:T(8,128)S(1)}, u32[]{:S(2)}, u32[]{:S(2)}) collective-permute-start(f32[8,1,64,128]{3,2,1,0:T(8,128)S(1)} %get-tuple-element.43), channel_id=1, source_target_pairs={{0,1},{1,2},{2,3},{3,4},{4,5},{5,6},{6,7},{7,8},{8,9},{9,10},{10,1... | collective-permute-start | bytes 786440 | tf_op jit(solution)/shard_map/ppermute | solution.py:22
  63.3 0.3 fusion.22
  63.6 0.8 collective-permute-done.6
  64.4 5.5 %collective-permute-done.7 = f32[8,1,64,128]{3,2,1,0:T(8,128)S(1)} collective-permute-done((f32[8,1,64,128]{3,2,1,0:T(8,128)S(1)}, f32[8,1,64,128]{3,2,1,0:T(8,128)S(1)}, u32[]{:S(2)}, u32[]{:S(2)}) %collective-permute-start.7) | collective-permute-done | bytes 262176 | tf_op jit(solution)/shard_map/ppermute | solution.py:23
  70.0 0.2 fusion.6
  70.2 0.9 multiply_add_fusion
  71.1 3.3 %collective-permute-start.8 = (f32[8,1,64,128]{3,2,1,0:T(8,128)S(1)}, f32[8,1,64,128]{3,2,1,0:T(8,128)S(1)}, u32[]{:S(2)}, u32[]{:S(2)}) collective-permute-start(f32[8,1,64,128]{3,2,1,0:T(8,128)S(1)} %get-tuple-element.41), channel_id=1, source_target_pairs={{0,1},{1,2},{2,3},{3,4},{4,5},{5,6},{6,7},{7,8},{8,9},{9,10},{10,1... | collective-permute-start | bytes 786440 | tf_op jit(solution)/shard_map/ppermute | solution.py:22
  74.4 0.2 fusion.13
  74.6 0.3 fusion.12
  75.1 2.0 %collective-permute-done.8 = f32[8,1,64,128]{3,2,1,0:T(8,128)S(1)} collective-permute-done((f32[8,1,64,128]{3,2,1,0:T(8,128)S(1)}, f32[8,1,64,128]{3,2,1,0:T(8,128)S(1)}, u32[]{:S(2)}, u32[]{:S(2)}) %collective-permute-start.8) | collective-permute-done | bytes 262176 | tf_op jit(solution)/shard_map/ppermute | solution.py:22
  77.1 1.2 %collective-permute-done.9 = f32[8,1,64,128]{3,2,1,0:T(8,128)S(1)} collective-permute-done((f32[8,1,64,128]{3,2,1,0:T(8,128)S(1)}, f32[8,1,64,128]{3,2,1,0:T(8,128)S(1)}, u32[]{:S(2)}, u32[]{:S(2)}) %collective-permute-start.9) | collective-permute-done | bytes 262176 | tf_op jit(solution)/shard_map/ppermute | solution.py:23
  78.4 1.1 %multiply_reduce_fusion.1 = (f32[4,64,128]{2,1,0:T(8,128)S(1)}, f32[8,4,64,128]{3,2,1,0:T(8,128)S(1)}) fusion(bf16[8,4,64,128]{3,2,1,0:T(8,128)(2,1)S(1)} %copy-done.3, f32[8,4,64,128]{3,2,1,0:T(8,128)S(1)} %get-tuple-element.29, f32[4,64,128]{2,1,0:T(8,128)S(1)} %get-tuple-element.52, f32[8,4,64,127]{3,2,1,0:T(8,128)S(1)} %fusion.12, ...), kind=kLoop, calls=%fused_computation.68 | loop fusion | flops 6520832 | bytes 9805824 | tf_op jit(solution)/shard_map/reduce_sum | solution.py:136
  79.7 3.4 %collective-permute-start.10 = (f32[16,1,64,128]{3,2,1,0:T(8,128)S(1)}, f32[16,1,64,128]{3,2,1,0:T(8,128)S(1)}, u32[]{:S(2)}, u32[]{:S(2)}) collective-permute-start(f32[16,1,64,128]{3,2,1,0:T(8,128)S(1)} %get-tuple-element.36), channel_id=1, source_target_pairs={{0,1},{1,2},{2,3},{3,4},{4,5},{5,6},{6,7},{7,8},{8,9},{9,10},{10,1... | collective-permute-start | bytes 1572872 | tf_op jit(solution)/shard_map/ppermute | solution.py:22
  83.2 0.9 convert_element_type.12
  84.0 0.6 fusion.9
  84.7 0.3 fusion.11
  85.0 9.1 %collective-permute-done.10 = f32[16,1,64,128]{3,2,1,0:T(8,128)S(1)} collective-permute-done((f32[16,1,64,128]{3,2,1,0:T(8,128)S(1)}, f32[16,1,64,128]{3,2,1,0:T(8,128)S(1)}, u32[]{:S(2)}, u32[]{:S(2)}) %collective-permute-start.10) | collective-permute-done | bytes 524320 | tf_op jit(solution)/shard_map/ppermute | solution.py:22
  94.1 0.7 maximum_maximum_fusion
  94.8 0.6 fusion.3
  95.4 0.9 broadcast_multiply_fusion.1
  96.3 0.8 fusion.45
  (51 shorter events, 2.1 us)
Async XLA Ops:
  0.6 8.7 %copy-start.1 = (f32[4,64,128]{2,1,0:T(8,128)S(1)}, f32[4,64,128]{2,1,0:T(8,128)}, u32[]{:S(2)}) copy-start(f32[4,64,128]{2,1,0:T(8,128)} %param.10) | copy-start | bytes 393220
  0.6 10.3 %copy-start = (bf16[8,4,64,128]{3,2,1,0:T(8,128)(2,1)S(1)}, bf16[8,4,64,128]{3,2,1,0:T(8,128)(2,1)}, u32[]{:S(2)}) copy-start(bf16[8,4,64,128]{3,2,1,0:T(8,128)(2,1)} %param.12) | copy-start | bytes 1572868
  0.7 8.9 %copy-start.4 = (s32[8]{0:T(128)S(1)}, s32[8]{0:T(128)}, u32[]{:S(2)}) copy-start(s32[8]{0:T(128)} %param.15) | copy-start | bytes 100
  0.7 31.3 %collective-permute-start.12 = (f32[4,64,128]{2,1,0:T(8,128)}, f32[4,64,128]{2,1,0:T(8,128)}, u32[]{:S(2)}, u32[]{:S(2)}) collective-permute-start(f32[4,64,128]{2,1,0:T(8,128)} %param.10), channel_id=1, source_target_pairs={{0,2},{1,3},{2,0},{3,1},{4,6},{5,7},{6,4},{7,5},{8,10},{9,11},{10,... | collective-permute-start | bytes 393224 | tf_op jit(solution)/shard_map/ppermute | solution.py:31
  2.6 27.7 %collective-permute-start = (f32[1,64,128]{2,1,0:T(8,128)}, f32[1,64,128]{2,1,0:T(8,128)}, u32[]{:S(2)}, u32[]{:S(2)}) collective-permute-start(f32[1,64,128]{2,1,0:T(8,128)} %get-tuple-element.54), channel_id=1, source_target_pairs={{0,1},{1,2},{2,3},{3,4},{4,5},{5,6},{6,7},{7,8},{8,9},{9,10},{10,1... | collective-permute-start | bytes 98312 | tf_op jit(solution)/shard_map/ppermute | solution.py:22
  2.7 27.7 %collective-permute-start.1 = (f32[1,64,128]{2,1,0:T(8,128)}, f32[1,64,128]{2,1,0:T(8,128)}, u32[]{:S(2)}, u32[]{:S(2)}) collective-permute-start(f32[1,64,128]{2,1,0:T(8,128)} %get-tuple-element.55), channel_id=1, source_target_pairs={{1,0},{2,1},{3,2},{4,3},{5,4},{6,5},{7,6},{8,7},{9,8},{10,9},{11,1... | collective-permute-start | bytes 98312 | tf_op jit(solution)/shard_map/ppermute | solution.py:23
  6.2 27.3 %collective-permute-start.2 = (f32[8,1,64,128]{3,2,1,0:T(8,128)}, f32[8,1,64,128]{3,2,1,0:T(8,128)}, u32[]{:S(2)}, u32[]{:S(2)}) collective-permute-start(f32[8,1,64,128]{3,2,1,0:T(8,128)} %get-tuple-element.49), channel_id=1, source_target_pairs={{0,1},{1,2},{2,3},{3,4},{4,5},{5,6},{6,7},{7,8},{8,9},{9,10},{10,1... | collective-permute-start | bytes 786440 | tf_op jit(solution)/shard_map/ppermute | solution.py:22
  7.1 26.4 %collective-permute-start.3 = (f32[8,1,64,128]{3,2,1,0:T(8,128)}, f32[8,1,64,128]{3,2,1,0:T(8,128)}, u32[]{:S(2)}, u32[]{:S(2)}) collective-permute-start(f32[8,1,64,128]{3,2,1,0:T(8,128)} %get-tuple-element.48), channel_id=1, source_target_pairs={{1,0},{2,1},{3,2},{4,3},{5,4},{6,5},{7,6},{8,7},{9,8},{10,9},{11,1... | collective-permute-start | bytes 786440 | tf_op jit(solution)/shard_map/ppermute | solution.py:23
  19.5 10.7 %copy-start.3 = (bf16[8,4,64,128]{3,2,1,0:T(8,128)(2,1)S(1)}, bf16[8,4,64,128]{3,2,1,0:T(8,128)(2,1)}, u32[]{:S(2)}) copy-start(bf16[8,4,64,128]{3,2,1,0:T(8,128)(2,1)} %param.11) | copy-start | bytes 1572868
  33.0 1.7 %copy-start.2 = (f32[8,4,64,128]{3,2,1,0:T(8,128)S(1)}, f32[8,4,64,128]{3,2,1,0:T(8,128)}, u32[]{:S(2)}) copy-start(f32[8,4,64,128]{3,2,1,0:T(8,128)} %copy.10) | copy-start | bytes 3145732
  33.0 8.5 %collective-permute-start.13 = (f32[8,64,128]{2,1,0:T(8,128)S(1)}, f32[8,64,128]{2,1,0:T(8,128)S(1)}, u32[]{:S(2)}, u32[]{:S(2)}) collective-permute-start(f32[8,64,128]{2,1,0:T(8,128)S(1)} %pad_maximum_fusion.5), channel_id=1, source_target_pairs={{0,4},{1,5},{2,6},{3,7},{4,0},{5,1},{6,2},{7,3},{8,12},{9,13},{10,... | collective-permute-start | bytes 786440 | tf_op jit(solution)/shard_map/ppermute | solution.py:31
  35.7 8.0 %collective-permute-start.4 = (f32[8,1,64,128]{3,2,1,0:T(8,128)S(1)}, f32[8,1,64,128]{3,2,1,0:T(8,128)S(1)}, u32[]{:S(2)}, u32[]{:S(2)}) collective-permute-start(f32[8,1,64,128]{3,2,1,0:T(8,128)S(1)} %get-tuple-element.45), channel_id=1, source_target_pairs={{0,1},{1,2},{2,3},{3,4},{4,5},{5,6},{6,7},{7,8},{8,9},{9,10},{10,1... | collective-permute-start | bytes 786440 | tf_op jit(solution)/shard_map/ppermute | solution.py:22
  37.3 6.4 %collective-permute-start.5 = (f32[8,1,64,128]{3,2,1,0:T(8,128)S(1)}, f32[8,1,64,128]{3,2,1,0:T(8,128)S(1)}, u32[]{:S(2)}, u32[]{:S(2)}) collective-permute-start(f32[8,1,64,128]{3,2,1,0:T(8,128)S(1)} %get-tuple-element.44), channel_id=1, source_target_pairs={{1,0},{2,1},{3,2},{4,3},{5,4},{6,5},{7,6},{8,7},{9,8},{10,9},{11,1... | collective-permute-start | bytes 786440 | tf_op jit(solution)/shard_map/ppermute | solution.py:23
  41.5 33.4 %collective-permute-start.14 = (f32[16,64,128]{2,1,0:T(8,128)S(1)}, f32[16,64,128]{2,1,0:T(8,128)S(1)}, u32[]{:S(2)}, u32[]{:S(2)}) collective-permute-start(f32[16,64,128]{2,1,0:T(8,128)S(1)} %pad_maximum_fusion.4), channel_id=1, source_target_pairs={{0,8},{1,9},{2,10},{3,11},{4,12},{5,13},{6,14},{7,15},{8,0},{9,1},... | collective-permute-start | bytes 1572872 | tf_op jit(solution)/shard_map/ppermute | solution.py:31
  44.9 19.6 %collective-permute-start.6 = (f32[8,1,64,128]{3,2,1,0:T(8,128)S(1)}, f32[8,1,64,128]{3,2,1,0:T(8,128)S(1)}, u32[]{:S(2)}, u32[]{:S(2)}) collective-permute-start(f32[8,1,64,128]{3,2,1,0:T(8,128)S(1)} %get-tuple-element.43), channel_id=1, source_target_pairs={{0,1},{1,2},{2,3},{3,4},{4,5},{5,6},{6,7},{7,8},{8,9},{9,10},{10,1... | collective-permute-start | bytes 786440 | tf_op jit(solution)/shard_map/ppermute | solution.py:22
  63.2 6.7 %collective-permute-start.7 = (f32[8,1,64,128]{3,2,1,0:T(8,128)S(1)}, f32[8,1,64,128]{3,2,1,0:T(8,128)S(1)}, u32[]{:S(2)}, u32[]{:S(2)}) collective-permute-start(f32[8,1,64,128]{3,2,1,0:T(8,128)S(1)} %get-tuple-element.42), channel_id=1, source_target_pairs={{1,0},{2,1},{3,2},{4,3},{5,4},{6,5},{7,6},{8,7},{9,8},{10,9},{11,1... | collective-permute-start | bytes 786440 | tf_op jit(solution)/shard_map/ppermute | solution.py:23
  71.1 6.0 %collective-permute-start.8 = (f32[8,1,64,128]{3,2,1,0:T(8,128)S(1)}, f32[8,1,64,128]{3,2,1,0:T(8,128)S(1)}, u32[]{:S(2)}, u32[]{:S(2)}) collective-permute-start(f32[8,1,64,128]{3,2,1,0:T(8,128)S(1)} %get-tuple-element.41), channel_id=1, source_target_pairs={{0,1},{1,2},{2,3},{3,4},{4,5},{5,6},{6,7},{7,8},{8,9},{9,10},{10,1... | collective-permute-start | bytes 786440 | tf_op jit(solution)/shard_map/ppermute | solution.py:22
  74.4 3.9 %collective-permute-start.9 = (f32[8,1,64,128]{3,2,1,0:T(8,128)S(1)}, f32[8,1,64,128]{3,2,1,0:T(8,128)S(1)}, u32[]{:S(2)}, u32[]{:S(2)}) collective-permute-start(f32[8,1,64,128]{3,2,1,0:T(8,128)S(1)} %get-tuple-element.40), channel_id=1, source_target_pairs={{1,0},{2,1},{3,2},{4,3},{5,4},{6,5},{7,6},{8,7},{9,8},{10,9},{11,1... | collective-permute-start | bytes 786440 | tf_op jit(solution)/shard_map/ppermute | solution.py:23
  79.7 14.4 %collective-permute-start.10 = (f32[16,1,64,128]{3,2,1,0:T(8,128)S(1)}, f32[16,1,64,128]{3,2,1,0:T(8,128)S(1)}, u32[]{:S(2)}, u32[]{:S(2)}) collective-permute-start(f32[16,1,64,128]{3,2,1,0:T(8,128)S(1)} %get-tuple-element.36), channel_id=1, source_target_pairs={{0,1},{1,2},{2,3},{3,4},{4,5},{5,6},{6,7},{7,8},{8,9},{9,10},{10,1... | collective-permute-start | bytes 1572872 | tf_op jit(solution)/shard_map/ppermute | solution.py:22
  83.0 11.1 %collective-permute-start.11 = (f32[16,1,64,128]{3,2,1,0:T(8,128)S(1)}, f32[16,1,64,128]{3,2,1,0:T(8,128)S(1)}, u32[]{:S(2)}, u32[]{:S(2)}) collective-permute-start(f32[16,1,64,128]{3,2,1,0:T(8,128)S(1)} %get-tuple-element.37), channel_id=1, source_target_pairs={{1,0},{2,1},{3,2},{4,3},{5,4},{6,5},{7,6},{8,7},{9,8},{10,9},{11,1... | collective-permute-start | bytes 1572872 | tf_op jit(solution)/shard_map/ppermute | solution.py:23
where the time goes:
time: 97.7 us; the launch traced here: 97.1 us
  starting transfers between devices  34.2 us (35%)
  other arithmetic  25.4 us (26%)
  waiting for transfers between devices  21.7 us (22%)
  local copies, waits for them, and re-layouts  14.2 us (15%)
  between operations  1.06 us (1%)
    ppermute x6, starting transfers between devices, padded(): before = lax.ppermute(last, axis, up)  27.6 us
    ppermute x6, waiting for transfers between devices, padded(): before = lax.ppermute(last, axis, up)  12 us
    reshape x1, local copies, waits for them, and re-layouts, body(): rhs = rhs.reshape(sources, layers, rows_y, rows_z)  10.7 us
    scatter-add x1, other arithmetic, body(): rhs = jnp.zeros((sources, cells), jnp.float32).at[:, target].add(amount)  8.35 us
    ppermute x6, waiting for transfers between devices, padded(): after = lax.ppermute(leading, axis, down)  6.72 us
    ppermute x6, starting transfers between devices, padded(): after = lax.ppermute(leading, axis, down)  3.38 us
    ppermute x3, starting transfers between devices, swapped(): return lax.ppermute(value, axis, pairs)  3.24 us
    ppermute x3, waiting for transfers between devices, swapped(): return lax.ppermute(value, axis, pairs)  3.04 us
  transfers between devices with their start and end apart: 15, of which 6 were waited for; matrix products, arithmetic and copies ran while one was open for 37% of the time, Pallas kernels for 0%

commit v1 on v0

--- a/solution.py
+++ b/solution.py
@@ -1,6 +1,8 @@
 import jax
 import jax.numpy as jnp
 from jax import lax
+from jax.experimental import pallas as pl
+from jax.experimental.pallas import tpu as pltpu
 from jax.sharding import PartitionSpec as P
 
 SURVEYS = 8
@@ -58,7 +60,7 @@
     return padded(field, (("space", 1),), 1)
 
 
-def body(model, forward, warm_start, residual_data, electrodes, survey_order):
+def layered(model, forward, warm_start, residual_data, electrodes, survey_order):
     sources, layers, rows_y, rows_z = forward.shape
     position = lax.axis_index("space")
     devices = lax.axis_size("space")
@@ -168,7 +170,449 @@
     return (iterate.astype(jnp.bfloat16), data_term + space_term + time_term)
 
 
+def weights():
+    now = HALF_WIDTH / CENTER
+    steps = []
+    for _ in range(ITERS - 1):
+        new = 1.0 / (2.0 * CENTER / HALF_WIDTH - now)
+        steps.append((new * now, 2.0 * new / HALF_WIDTH))
+        now = new
+    return steps
+
+
+def after(x, axis):
+    return pltpu.roll(x, x.shape[axis] - 1, axis)
+
+
+def before(x, axis):
+    return pltpu.roll(x, 1, axis)
+
+
+def inner(shape, axis):
+    return lax.broadcasted_iota(jnp.int32, shape, axis) < shape[axis] - 1
+
+
+def face_prod(field, other, axis):
+    return (field - after(field, axis)) * (other - after(other, axis))
+
+
+def pack_first(info, model, warm, out):
+    layers = model.shape[0]
+    out[:layers] = model[...]
+    for q in range(warm.shape[0]):
+        out[layers * (q + 1) : layers * (q + 2)] = warm[q].astype(jnp.float32)
+
+
+def pack_second(info, warm, forward, out):
+    count, layers = warm.shape[:2]
+    for q in range(count):
+        out[layers * q : layers * (q + 1)] = warm[q].astype(jnp.float32)
+    for q in range(forward.shape[0]):
+        out[count * layers + q] = forward[q, 0].astype(jnp.float32)
+
+
+def inject(info, residual, electrodes, out):
+    tile = info[0]
+    sources, _, rows_y, rows_z = out.shape
+    half = residual.shape[1] // 2
+    cells = out.shape[1] * rows_y * rows_z
+    where_cell = lax.rem(electrodes[...] + tile * (cells // 2), cells)
+    row = where_cell // rows_z
+    lane = lax.rem(where_cell, rows_z)
+    count = row.shape[1]
+    rows = cells // rows_z
+    at_row = lax.broadcasted_iota(jnp.int32, (rows, count), 0) == row
+    at_row = jnp.where(at_row, 1.0, 0.0).astype(jnp.bfloat16)
+    at_lane = lax.broadcasted_iota(jnp.int32, (rows_z, count), 0) == lane
+    mine = jnp.where(tile == 0, residual[0, :half], residual[0, half:])
+    total = None
+    for _ in range(3):
+        part = mine.astype(jnp.bfloat16).astype(jnp.float32)
+        mine = mine - part
+        right = jnp.concatenate(
+            [jnp.where(at_lane, part[q : q + 1], 0.0) for q in range(sources)], axis=0
+        ).astype(jnp.bfloat16)
+        term = lax.dot_general(
+            at_row, right, (((1,), (1,)), ((), ())), preferred_element_type=jnp.float32
+        )
+        total = term if total is None else total + term
+    for q in range(sources):
+        out[q] = total[:, q * rows_z : (q + 1) * rows_z].reshape(out.shape[1:])
+
+
+def find_coefs(tile, model, other, sigma, coefs):
+    layers = model.shape[0]
+    full = 2 * layers
+    shape = model.shape[1:]
+    for i in range(layers):
+        sigma[i] = jnp.exp(model[i])
+        sigma[layers + i] = jnp.exp(other[i])
+    in_y, in_z = inner(shape, 0), inner(shape, 1)
+    middle = jnp.where(tile == 0, 1.0, 0.0)
+    for i in range(full):
+        mine = sigma[i]
+        up = 0.5 * (mine + sigma[(i + 1) % full])
+        down = 0.5 * (mine + sigma[(i - 1) % full])
+        if i == layers - 1:
+            up = up * middle
+        if i == full - 1:
+            up = up * (1.0 - middle)
+        if i == layers:
+            down = down * middle
+        if i == 0:
+            down = down * (1.0 - middle)
+        right_y = jnp.where(in_y, 0.5 * (mine + after(mine, 0)), 0.0)
+        right_z = jnp.where(in_z, 0.5 * (mine + after(mine, 1)), 0.0)
+        left_y = before(right_y, 0)
+        left_z = before(right_z, 1)
+        scale = 1.0 / (up + down + right_y + left_y + right_z + left_z + GROUND * mine)
+        for k, face in enumerate((up, down, right_y, left_y, right_z, left_z)):
+            coefs[k, i] = face * scale
+        coefs[6, i] = scale
+
+
+def sweeps(coefs, rhs, start, rest, lam, mine, sent):
+    count, full = start.shape[:2]
+
+    def around(field, q, i, weight):
+        here = field[q, i]
+        total = weight[0] * field[q, (i + 1) % full] + weight[1] * field[q, (i + full - 1) % full]
+        total = total + (weight[2] * after(here, 0) + weight[3] * before(here, 0))
+        total = total + (weight[4] * after(here, 1) + weight[5] * before(here, 1))
+        return here, total
+
+    def first(i, carry):
+        weight = [coefs[k, i] for k in range(7)]
+        for q in range(count):
+            here, total = around(start, q, i, weight)
+            step = rhs[q, i] * weight[6] - here + total
+            mine[0, q, i] = step
+            lam[q, i] = here + step
+        return carry
+
+    lax.fori_loop(0, full, first, 0)
+    for index, (keep, gain) in enumerate(weights()):
+        source, target = mine.at[index % 2], mine.at[1 - index % 2]
+        last = index == ITERS - 2
+
+        def later(i, carry):
+            weight = [coefs[k, i] for k in range(6)]
+            for q in range(count):
+                here, total = around(source, q, i, weight)
+                if index > 0:
+                    total = rest[q, i] - here + total
+                step = keep * here + gain * total
+                if not last:
+                    rest[q, i] = total
+                    target[q, i] = step
+                lam[q, i] = lam[q, i] + step
+            return carry
+
+        lax.fori_loop(0, full, later, 0)
+
+
+def solve_first(info, model, got, warm, rhs, coefs, own, sent, sigma, start, rest, lam, mine):
+    layers = model.shape[0]
+    count = warm.shape[0]
+    find_coefs(info[0], model, got.at[:layers], sigma, coefs)
+    for q in range(count):
+        start[q, :layers] = warm[q].astype(jnp.float32)
+        start[q, layers:] = got[layers * (q + 1) : layers * (q + 2)]
+    sweeps(coefs, rhs, start, rest, lam, mine, None)
+    for q in range(count):
+        own[q] = lam[q, :layers]
+        sent[layers * q : layers * (q + 1)] = lam[q, layers:]
+
+
+def solve_second(info, coefs, got, warm, rhs, face, own_first, sent_first, own, sent, start, rest, lam, mine):
+    count, layers = warm.shape[:2]
+    for q in range(count):
+        start[q, :layers] = warm[q].astype(jnp.float32)
+        start[q, layers:] = got[layers * q : layers * (q + 1)]
+    sweeps(coefs, rhs, start, rest, lam, mine, None)
+    near = (layers - 1) * (1 - info[0])
+    far = (layers - 1) * info[0]
+    total = None
+    for q in range(2 * count):
+        slope = face[q, 0].astype(jnp.float32) - got[count * layers + q]
+        if q < count:
+            drop = own_first[q, near] - sent_first[layers * q + far]
+        else:
+            drop = lam[q - count, near] - lam[q - count, layers + far]
+        total = slope * drop if total is None else total + slope * drop
+    for q in range(count):
+        own[q] = lam[q, :layers]
+        sent[layers * q : layers * (q + 1)] = lam[q, layers:]
+    sent[count * layers] = total
+
+
+def data_sums(pairs, layers, along_x, along_y, along_z, mass):
+    def add(ref, i, value, first):
+        ref[i] = value if first else ref[i] + value
+
+    for i in range(layers):
+        totals = [None] * 4
+        for forward, lam in pairs:
+            here, other = forward(i), lam(i)
+            terms = [None, face_prod(here, other, 0), face_prod(here, other, 1), here * other]
+            if i + 1 < layers:
+                terms[0] = (here - forward(i + 1)) * (other - lam(i + 1))
+            totals = [t if a is None else (a if t is None else a + t) for a, t in zip(totals, terms)]
+        if i + 1 < layers:
+            along_x[i] = along_x[i] + totals[0]
+        along_y[i] = along_y[i] + totals[1]
+        along_z[i] = along_z[i] + totals[2]
+        mass[i] = mass[i] + totals[3]
+
+
+def gather_terms(info, forward_a, forward_b, forward_c, own_first, own_second, back, sums, adjoint):
+    count, layers = own_first.shape[:2]
+    sums[...] = jnp.zeros(sums.shape, jnp.float32)
+    pairs = []
+    for forward, lam in ((forward_a, own_first), (forward_b, own_second)):
+        for q in range(count):
+            pairs.append((
+                lambda i, f=forward, q=q: f[q, i].astype(jnp.float32),
+                lambda i, l=lam, q=q: l[q, i],
+            ))
+    for q in range(count):
+        pairs.append((
+            lambda i, q=q: forward_c[q, i].astype(jnp.float32),
+            lambda i, q=q: back[layers * q + i],
+        ))
+    data_sums(pairs, layers, sums.at[0], sums.at[1], sums.at[2], sums.at[3])
+    for q in range(count):
+        adjoint[q] = own_first[q].astype(jnp.bfloat16)
+        adjoint[count + q] = own_second[q].astype(jnp.bfloat16)
+        adjoint[2 * count + q] = back[layers * q : layers * (q + 1)].astype(jnp.bfloat16)
+
+
+def finish(info, sums, back, sent, forward, model, other, times, near_a, near_b, near_c, three, adjoint, gradient):
+    tile = info[0]
+    count, layers = forward.shape[:2]
+    shape = model.shape[1:]
+    pairs = []
+    for q in range(count):
+        pairs.append((
+            lambda i, q=q: forward[q, i].astype(jnp.float32),
+            lambda i, q=q: back[layers * q + i],
+        ))
+    in_y, in_z = inner(shape, 0), inner(shape, 1)
+    low = jnp.where(tile == 0, 0.0, 1.0)
+    high = 1.0 - low
+    cross = back[count * layers] + sent[0]
+    bridge = other[(layers - 1) * tile]
+    products, falls = [low * cross], [low * (bridge - model[0])]
+    for i in range(layers):
+        if i + 1 < layers:
+            total = sums[0, i]
+            for f, l in pairs:
+                total = total + (f(i) - f(i + 1)) * (l(i) - l(i + 1))
+            products.append(total)
+            falls.append(model[i] - model[i + 1])
+        else:
+            products.append(high * cross)
+            falls.append(high * (model[i] - bridge))
+    for i in range(layers):
+        total_y, total_z, mass = sums[1, i], sums[2, i], sums[3, i]
+        for f, l in pairs:
+            here, there = f(i), l(i)
+            total_y = total_y + face_prod(here, there, 0)
+            total_z = total_z + face_prod(here, there, 1)
+            mass = mass + here * there
+        total_y = jnp.where(in_y, total_y, 0.0)
+        total_z = jnp.where(in_z, total_z, 0.0)
+        terms = products[i] + products[i + 1]
+        terms = terms + (total_y + before(total_y, 0)) + (total_z + before(total_z, 1))
+        value = model[i]
+        fall_y = jnp.where(in_y, value - after(value, 0), 0.0)
+        fall_z = jnp.where(in_z, value - after(value, 1), 0.0)
+        space = falls[i + 1] - falls[i] + (fall_y - before(fall_y, 0)) + (fall_z - before(fall_z, 1))
+        time = times[i] + near_a[i] + near_b[i] + near_c[i]
+        gradient[i] = space + time - jnp.exp(value) * (0.5 * terms + GROUND * mass)
+    spot = count * 2 * tile
+    for q in range(2 * count):
+        adjoint[spot + q] = three[q]
+    spot = count * 2 * (1 - tile)
+    for q in range(count):
+        adjoint[spot + q] = three[2 * count + q]
+        adjoint[spot + count + q] = back[layers * q : layers * (q + 1)].astype(jnp.bfloat16)
+
+
+def time_parts(info, order, model, beside, times, part_a, part_b, part_c):
+    surveys = order.shape[0]
+
+    def rank(survey):
+        found = 0
+        for i in range(surveys):
+            found = found + jnp.where(order[i] == survey, i, 0)
+        return found
+
+    def couple(first, second):
+        a, b = rank(first), rank(second)
+        ends = jnp.where(a == 0, 1, 0) + jnp.where(a == surveys - 1, 1, 0)
+        value = jnp.where(a == b, 2 - ends, jnp.where(jnp.abs(a - b) == 1, -1, 0))
+        return value.astype(jnp.float32)
+
+    mine, sibling = info[1], info[2]
+    for k, out in enumerate((times, part_a, part_b, part_c)):
+        target = info[3 + k]
+        out[...] = couple(target, mine) * model[...] + couple(target, sibling) * beside[...]
+
+
+def call(kernel, info, operands, specs, out_shapes, out_specs=None, scratch=()):
+    if out_specs is None:
+        out_specs = [whole(s.shape) for s in out_shapes]
+    several = len(out_shapes) > 1
+    return pl.pallas_call(
+        kernel,
+        out_shape=out_shapes if several else out_shapes[0],
+        grid_spec=pltpu.PrefetchScalarGridSpec(
+            num_scalar_prefetch=1,
+            grid=(1,),
+            in_specs=specs,
+            out_specs=out_specs if several else out_specs[0],
+            scratch_shapes=list(scratch),
+        ),
+        compiler_params=pltpu.CompilerParams(vmem_limit_bytes=48 * 2**20),
+    )(info, *operands)
+
+
+def whole(shape):
+    zeros = (0,) * len(shape)
+    return pl.BlockSpec(tuple(shape), lambda g, info: zeros)
+
+
+def f32(*shape):
+    return jax.ShapeDtypeStruct(shape, jnp.float32)
+
+
+def paired(model, forward, warm_start, residual_data, electrodes, survey_order):
+    sources, layers, ny, nz = forward.shape
+    half, count = sources // 2, sources // 4
+    full = 2 * layers
+    devices = lax.axis_size("space")
+    position = lax.axis_index("space")
+    tile = (position + 1) % 2
+    survey = (position + 1) // 2 % SURVEYS
+    sibling = (position ^ 1) + 1
+    sibling = sibling // 2 % SURVEYS
+    targets = [((position ^ (4 * k)) + 1) // 2 % SURVEYS for k in range(4)]
+    info = jnp.stack([tile, survey, sibling] + targets).astype(jnp.int32)
+    pairs = []
+    for p in range(1, devices, 2):
+        pairs += [(p, (p + 1) % devices), ((p + 1) % devices, p)]
+
+    def swap(x, mask=None):
+        links = pairs if mask is None else [(p, p ^ mask) for p in range(devices)]
+        return lax.ppermute(x, "space", links)
+
+    block = (count, layers, ny, nz)
+    mine_a = pl.BlockSpec(block, lambda g, info: (2 * info[0], 0, 0, 0))
+    mine_b = pl.BlockSpec(block, lambda g, info: (2 * info[0] + 1, 0, 0, 0))
+    theirs_a = pl.BlockSpec(block, lambda g, info: (2 - 2 * info[0], 0, 0, 0))
+    theirs_b = pl.BlockSpec(block, lambda g, info: (3 - 2 * info[0], 0, 0, 0))
+    edge = (half, 1, ny, nz)
+    my_edge = pl.BlockSpec(edge, lambda g, info: (info[0], (layers - 1) * (1 - info[0]), 0, 0))
+    their_edge = pl.BlockSpec(edge, lambda g, info: (1 - info[0], (layers - 1) * (1 - info[0]), 0, 0))
+
+    slab = (layers, ny, nz)
+    first = call(
+        pack_first, info, (model, warm_start), [whole(slab), theirs_a], [f32((count + 1) * layers, ny, nz)]
+    )
+    got_first = swap(first)
+    second = call(
+        pack_second, info, (warm_start, forward), [theirs_b, their_edge], [f32(count * layers + half, ny, nz)]
+    )
+    got_second = swap(second)
+    electrodes_row = electrodes.reshape(1, -1)
+    rhs = call(
+        inject,
+        info,
+        (residual_data, electrodes_row),
+        [
+            pl.BlockSpec((1,) + residual_data.shape[1:], lambda g, info: (info[1], 0, 0)),
+            whole(electrodes_row.shape),
+        ],
+        [f32(half, full, ny, nz)],
+    )
+    other = got_first[:layers]
+    beside = swap(other, 1)
+    fields = [
+        pltpu.VMEM((count, full, ny, nz), jnp.float32),
+        pltpu.VMEM((count, full, ny, nz), jnp.float32),
+        pltpu.VMEM((count, full, ny, nz), jnp.float32),
+        pltpu.VMEM((2, count, full, ny, nz), jnp.float32),
+    ]
+    rhs_block = (count, full, ny, nz)
+    coefs, own_first, sent_first = call(
+        solve_first,
+        info,
+        (model, got_first, warm_start, rhs),
+        [whole(slab), whole(got_first.shape), mine_a, pl.BlockSpec(rhs_block, lambda g, info: (0, 0, 0, 0))],
+        [f32(7, full, ny, nz), f32(*block), f32(count * layers, ny, nz)],
+        scratch=[pltpu.VMEM((full, ny, nz), jnp.float32)] + fields,
+    )
+    back_first = swap(sent_first)
+    times, part_a, part_b, part_c = pl.pallas_call(
+        time_parts,
+        out_shape=[f32(*slab)] * 4,
+        grid_spec=pltpu.PrefetchScalarGridSpec(
+            num_scalar_prefetch=2,
+            grid=(1,),
+            in_specs=[pl.BlockSpec(slab, lambda g, info, order: (0, 0, 0))] * 2,
+            out_specs=[pl.BlockSpec(slab, lambda g, info, order: (0, 0, 0))] * 4,
+        ),
+    )(info, survey_order, model, beside)
+    near = [swap(part, 4 * (k + 1)) for k, part in enumerate((part_a, part_b, part_c))]
+    own_second, sent_second = call(
+        solve_second,
+        info,
+        (coefs, got_second, warm_start, rhs, forward, own_first, sent_first),
+        [
+            whole(coefs.shape),
+            whole(got_second.shape),
+            mine_b,
+            pl.BlockSpec(rhs_block, lambda g, info: (1, 0, 0, 0)),
+            my_edge,
+            whole(own_first.shape),
+            whole(sent_first.shape),
+        ],
+        [f32(*block), f32(count * layers + 1, ny, nz)],
+        scratch=fields,
+    )
+    back_second = swap(sent_second)
+    sums, three = call(
+        gather_terms,
+        info,
+        (forward, forward, forward, own_first, own_second, back_first),
+        [mine_a, mine_b, theirs_a, whole(own_first.shape), whole(own_second.shape), whole(back_first.shape)],
+        [f32(4, *slab), jax.ShapeDtypeStruct((3 * count, layers, ny, nz), jnp.bfloat16)],
+    )
+    adjoint, gradient = call(
+        finish,
+        info,
+        (sums, back_second, sent_second, forward, model, got_first, times, *near, three),
+        [
+            whole(sums.shape),
+            whole(back_second.shape),
+            pl.BlockSpec((1, ny, nz), lambda g, info: (count * layers, 0, 0)),
+            theirs_b,
+            whole(slab),
+            whole(slab),
+            whole(slab),
+            whole(slab),
+            whole(slab),
+            whole(slab),
+            whole(three.shape),
+        ],
+        [jax.ShapeDtypeStruct(forward.shape, jnp.bfloat16), f32(*slab)],
+    )
+    return adjoint, gradient
+
+
 def solution(mesh):
+    body = paired if mesh.shape["space"] == 2 * SURVEYS else layered
     in_specs = (
         P(("groups", "space"), None, None),
         P(None, ("groups", "space"), None, None),

time: 97.7 us -> 52.6 us (0.54)
  the two profiles are of different devices: /device:TPU:14 before, /device:TPU:0 now
where the time goes in v1:
time: 52.6 us; the launch traced here: 52.3 us
  starting transfers between devices  18.2 us (35%)
  Pallas kernels  16.5 us (31%)
  waiting for transfers between devices  11.3 us (21%)
  local copies, waits for them, and re-layouts  5.44 us (10%)
  between operations  0.92 us (2%)
    ppermute x8, starting transfers between devices, swap(): return lax.ppermute(x, 'space', links)  18.2 us
    pallas_call x7, Pallas kernels, call(): pl.pallas_call(kernel, out_shape=out_shapes if several else out_shapes[0]...  14 us
    ppermute x8, waiting for transfers between devices, swap(): return lax.ppermute(x, 'space', links)  11.3 us
    unnamed x28, local copies, waits for them, and re-layouts  5.34 us
    pallas_call x1, Pallas kernels, paired(): pl.pallas_call(time_parts, out_shape=[f32(*slab)] * 4, grid_spec=pltpu.Pr...  2.49 us
  transfers between devices with their start and end apart: 8, of which 4 were waited for; matrix products, arithmetic and copies ran while one was open for 0% of the time, Pallas kernels for 19%

profile of v1, /device:TPU:0, one launch (start us, length us, event | category | flops | bytes accessed | tf_op | source)
XLA Modules:
  0.0 52.3 jit_solution(8902512584305175317)
XLA Ops:
  0.6 0.0 copy-start.12
  0.6 0.0 copy-start.9
  0.8 0.1 stack.28.info
  0.9 0.0 copy-start.2
  0.9 1.0 %copy-done.2 = bf16[8,4,64,128]{3,2,1,0:T(8,128)(2,1)S(1)} copy-done((bf16[8,4,64,128]{3,2,1,0:T(8,128)(2,1)S(1)}, bf16[8,4,64,128]{3,2,1,0:T(8,128)(2,1)}, u32[]{:S(2)}) %copy-start.2) | copy-done | bytes 524312
  1.9 0.0 copy-start.5
  2.0 0.9 %copy-done.5 = f32[4,64,128]{2,1,0:T(8,128)S(1)} copy-done((f32[4,64,128]{2,1,0:T(8,128)S(1)}, f32[4,64,128]{2,1,0:T(8,128)}, u32[]{:S(2)}) %copy-start.5) | copy-done | bytes 131096
  2.9 0.0 copy-start.10
  2.9 0.0 copy-start.4
  2.9 0.0 copy-start.6
  2.9 0.6 %shard_map.77 = f32[12,64,128]{2,1,0:T(8,128)S(1)} custom-call(s32[7]{0:T(128)S(1)} %stack.28.info, f32[4,64,128]{2,1,0:T(8,128)S(1)} %copy-done.5, bf16[8,4,64,128]{3,2,1,0:T(8,128)(2,1)S(1)} %copy-done.2), custom_call_target="tpu_custom_call" | custom-call | tf_op jit(solution)/shard_map/pallas_call | solution.py:467
  3.4 5.5 %collective-permute-start = (f32[12,64,128]{2,1,0:T(8,128)S(1)}, f32[12,64,128]{2,1,0:T(8,128)S(1)}, u32[]{:S(2)}, u32[]{:S(2)}) collective-permute-start(f32[12,64,128]{2,1,0:T(8,128)S(1)} %shard_map.77), channel_id=1, source_target_pairs={{1,2},{2,1},{3,4},{4,3},{5,6},{6,5},{7,8},{8,7},{9,10},{10,9},{11,... | collective-permute-start | bytes 1179656 | tf_op jit(solution)/shard_map/ppermute | solution.py:508
  8.9 1.0 %copy-done = bf16[8,4,64,128]{3,2,1,0:T(8,128)(2,1)S(1)} copy-done((bf16[8,4,64,128]{3,2,1,0:T(8,128)(2,1)S(1)}, bf16[8,4,64,128]{3,2,1,0:T(8,128)(2,1)}, u32[]{:S(2)}) %copy-start) | copy-done | bytes 524312
  10.0 1.0 %copy-done.3 = bf16[8,4,64,128]{3,2,1,0:T(8,128)(2,1)S(1)} copy-done((bf16[8,4,64,128]{3,2,1,0:T(8,128)(2,1)S(1)}, bf16[8,4,64,128]{3,2,1,0:T(8,128)(2,1)}, u32[]{:S(2)}) %copy-start.3) | copy-done | bytes 524312
  11.0 0.6 %shard_map.80 = f32[12,64,128]{2,1,0:T(8,128)S(1)} custom-call(s32[7]{0:T(128)S(1)} %stack.28.info, bf16[8,4,64,128]{3,2,1,0:T(8,128)(2,1)S(1)} %copy-done.3, bf16[8,4,64,128]{3,2,1,0:T(8,128)(2,1)S(1)} %copy-done), custom_call_target="tpu_custom_call" | custom-call | tf_op jit(solution)/shard_map/pallas_call | solution.py:467
  11.6 0.0 copy-start.1
  11.6 0.1 collective-permute-start.1
  11.7 0.0 copy-done.12
  11.7 0.0 copy-done.9
  11.7 1.2 %shard_map.78.rhs = f32[4,8,64,128]{3,2,1,0:T(8,128)S(1)} custom-call(s32[7]{0:T(128)S(1)} %stack.28.info, f32[8,8,256]{2,1,0:T(8,128)S(1)} %copy-done.9, s32[1,256]{1,0:T(1,128)S(1)} %bitcast.7), custom_call_target="tpu_custom_call" | custom-call | tf_op jit(solution)/shard_map/pallas_call | solution.py:467
  12.9 1.6 %collective-permute-done.got.other = f32[12,64,128]{2,1,0:T(8,128)S(1)} collective-permute-done((f32[12,64,128]{2,1,0:T(8,128)S(1)}, f32[12,64,128]{2,1,0:T(8,128)S(1)}, u32[]{:S(2)}, u32[]{:S(2)}) %collective-permute-start) | collective-permute-done | bytes 393248 | tf_op jit(solution)/shard_map/ppermute | solution.py:508
  14.5 0.0 copy-done.4
  14.5 0.0 copy-done.6
  14.5 4.5 %shard_map.79 = (f32[7,8,64,128]{3,2,1,0:T(8,128)S(1)}, f32[2,4,64,128]{3,2,1,0:T(8,128)S(1)}, f32[8,64,128]{2,1,0:T(8,128)S(1)}) custom-call(s32[7]{0:T(128)S(1)} %stack.28.info, f32[4,64,128]{2,1,0:T(8,128)S(1)} %copy-done.6, f32[12,64,128]{2,1,0:T(8,128)S(1)} %collective-permute-done.got.other, bf16[8,4,64,128]{3,2,1,0:T(8,128)(2,1)S(1)} %copy-done.4, ...), custom_call_target="tpu_custom_call" | custom-call | tf_op jit(solution)/shard_map/pallas_call | solution.py:467
  19.0 2.7 %collective-permute-done.1.got = f32[12,64,128]{2,1,0:T(8,128)S(1)} collective-permute-done((f32[12,64,128]{2,1,0:T(8,128)S(1)}, f32[12,64,128]{2,1,0:T(8,128)S(1)}, u32[]{:S(2)}, u32[]{:S(2)}) %collective-permute-start.1) | collective-permute-done | bytes 393248 | tf_op jit(solution)/shard_map/ppermute | solution.py:508
  21.7 0.0 copy-done.10
  21.7 0.0 copy-done.1
  21.7 4.2 %shard_map.81 = (f32[2,4,64,128]{3,2,1,0:T(8,128)S(1)}, f32[9,64,128]{2,1,0:T(8,128)S(1)}) custom-call(s32[7]{0:T(128)S(1)} %stack.28.info, f32[7,8,64,128]{3,2,1,0:T(8,128)S(1)} %get-tuple-element.14.coefs, f32[12,64,128]{2,1,0:T(8,128)S(1)} %collective-permute-done.1.got, bf16[8,4,64,128]{3,2,1,0:T(8,128)(2,1)S(1)} %copy-done.4, ...), custom_call_target="tpu_custom_call" | custom-call | tf_op jit(solution)/shard_map/pallas_call | solution.py:467
  25.9 0.0 copy-start.7
  25.9 1.8 %collective-permute-start.3 = (f32[9,64,128]{2,1,0:T(8,128)S(1)}, f32[9,64,128]{2,1,0:T(8,128)S(1)}, u32[]{:S(2)}, u32[]{:S(2)}) collective-permute-start(f32[9,64,128]{2,1,0:T(8,128)S(1)} %get-tuple-element.18.sent), channel_id=1, source_target_pairs={{1,2},{2,1},{3,4},{4,3},{5,6},{6,5},{7,8},{8,7},{9,10},{10,9},{11,... | collective-permute-start | bytes 884744 | tf_op jit(solution)/shard_map/ppermute | solution.py:508
  27.8 3.3 %collective-permute-start.4 = (f32[4,64,128]{2,1,0:T(8,128)S(1)}, f32[4,64,128]{2,1,0:T(8,128)S(1)}, u32[]{:S(2)}, u32[]{:S(2)}) collective-permute-start(f32[4,64,128]{2,1,0:T(8,128)S(1)} %slice.4), channel_id=1, source_target_pairs={{0,1},{1,0},{2,3},{3,2},{4,5},{5,4},{6,7},{7,6},{8,9},{9,8},{10,11... | collective-permute-start | bytes 393224 | tf_op jit(solution)/shard_map/ppermute | solution.py:508
  31.1 3.1 %collective-permute-start.2 = (f32[8,64,128]{2,1,0:T(8,128)S(1)}, f32[8,64,128]{2,1,0:T(8,128)S(1)}, u32[]{:S(2)}, u32[]{:S(2)}) collective-permute-start(f32[8,64,128]{2,1,0:T(8,128)S(1)} %get-tuple-element.15.sent_first), channel_id=1, source_target_pairs={{1,2},{2,1},{3,4},{4,3},{5,6},{6,5},{7,8},{8,7},{9,10},{10,9},{11,... | collective-permute-start | bytes 786440 | tf_op jit(solution)/shard_map/ppermute | solution.py:508
  34.1 0.0 collective-permute-done.4.beside
  34.1 0.7 %copy-done.13 = f32[4,64,128]{2,1,0:T(8,128)} copy-done((f32[4,64,128]{2,1,0:T(8,128)}, f32[4,64,128]{2,1,0:T(8,128)S(1)}, u32[]{:S(2)}) %copy-start.13) | copy-done | bytes 131096
  34.8 2.5 %shard_map.83 = (f32[4,64,128]{2,1,0:T(8,128)}, f32[4,64,128]{2,1,0:T(8,128)}, f32[4,64,128]{2,1,0:T(8,128)}, f32[4,64,128]{2,1,0:T(8,128)}) custom-call(s32[7]{0:T(128)} %copy-done.10, s32[8]{0:T(128)} %order.1, f32[4,64,128]{2,1,0:T(8,128)} %model.7, f32[4,64,128]{2,1,0:T(8,128)} %copy-done.13), custom_call_target="tpu_custom_call" | custom-call | tf_op jit(solution)/shard_map/pallas_call | solution.py:557
  37.3 0.0 collective-permute-start.5
  37.3 2.1 %collective-permute-start.6 = (f32[4,64,128]{2,1,0:T(8,128)}, f32[4,64,128]{2,1,0:T(8,128)S(1)}, u32[]{:S(2)}, u32[]{:S(2)}) collective-permute-start(f32[4,64,128]{2,1,0:T(8,128)} %get-tuple-element.21), channel_id=1, source_target_pairs={{0,8},{1,9},{2,10},{3,11},{4,12},{5,13},{6,14},{7,15},{8,0},{9,1},... | collective-permute-start | bytes 393224 | tf_op jit(solution)/shard_map/ppermute | solution.py:508
  39.4 2.3 %collective-permute-start.7 = (f32[4,64,128]{2,1,0:T(8,128)}, f32[4,64,128]{2,1,0:T(8,128)S(1)}, u32[]{:S(2)}, u32[]{:S(2)}) collective-permute-start(f32[4,64,128]{2,1,0:T(8,128)} %get-tuple-element.22), channel_id=1, source_target_pairs={{0,12},{1,13},{2,14},{3,15},{4,8},{5,9},{6,10},{7,11},{8,4},{9,5},... | collective-permute-start | bytes 393224 | tf_op jit(solution)/shard_map/ppermute | solution.py:508
  41.7 0.0 collective-permute-done.2.back
  41.7 0.6 %copy-done.11 = s32[7]{0:T(128)S(1)} copy-done((s32[7]{0:T(128)S(1)}, s32[7]{0:T(128)}, u32[]{:S(2)}) %copy-start.11) | copy-done | bytes 52
  42.3 1.1 %shard_map.82 = (f32[4,4,64,128]{3,2,1,0:T(8,128)S(1)}, bf16[6,4,64,128]{3,2,1,0:T(8,128)(2,1)S(1)}) custom-call(s32[7]{0:T(128)S(1)} %copy-done.11, bf16[8,4,64,128]{3,2,1,0:T(8,128)(2,1)S(1)} %copy-done.1, bf16[8,4,64,128]{3,2,1,0:T(8,128)(2,1)S(1)} %copy-done.1, bf16[8,4,64,128]{3,2,1,0:T(8,128)(2,1)S(1)} %copy-done.1, ...), custom_call_target="tpu_custom_call" | custom-call | tf_op jit(solution)/shard_map/pallas_call | solution.py:467
  43.4 0.6 %collective-permute-done.5.near_a = f32[4,64,128]{2,1,0:T(8,128)S(1)} collective-permute-done((f32[4,64,128]{2,1,0:T(8,128)}, f32[4,64,128]{2,1,0:T(8,128)S(1)}, u32[]{:S(2)}, u32[]{:S(2)}) %collective-permute-start.5) | collective-permute-done | bytes 131104 | tf_op jit(solution)/shard_map/ppermute | solution.py:508
  44.0 6.4 %collective-permute-done.6.near_b = f32[4,64,128]{2,1,0:T(8,128)S(1)} collective-permute-done((f32[4,64,128]{2,1,0:T(8,128)}, f32[4,64,128]{2,1,0:T(8,128)S(1)}, u32[]{:S(2)}, u32[]{:S(2)}) %collective-permute-start.6) | collective-permute-done | bytes 131104 | tf_op jit(solution)/shard_map/ppermute | solution.py:508
  50.4 0.0 collective-permute-done.7.near_c
  50.4 0.0 collective-permute-done.3.back
  50.4 0.0 copy-done.7
  50.4 0.0 copy-done.8
  50.4 1.9 %shard_map.84 = (bf16[8,4,64,128]{3,2,1,0:T(8,128)(2,1)}, f32[4,64,128]{2,1,0:T(8,128)}) custom-call(s32[7]{0:T(128)S(1)} %copy-done.11, f32[4,4,64,128]{3,2,1,0:T(8,128)S(1)} %get-tuple-element.17.sums, f32[9,64,128]{2,1,0:T(8,128)S(1)} %collective-permute-done.3.back, f32[9,64,128]{2,1,0:T(8,128)S(1)} %get-tuple-element.18.sent, ...), custom_call_target="tpu_custom_call" | custom-call | tf_op jit(solution)/shard_map/pallas_call | solution.py:467
  (6 shorter events, 0.0 us)
Async XLA Ops:
  0.6 11.1 %copy-start.12 = (s32[256]{0:T(256)S(1)}, s32[256]{0:T(256)}, u32[]{:S(2)}) copy-start(s32[256]{0:T(256)} %param.10) | copy-start | bytes 3076
  0.6 11.1 %copy-start.9 = (f32[8,8,256]{2,1,0:T(8,128)S(1)}, f32[8,8,256]{2,1,0:T(8,128)}, u32[]{:S(2)}) copy-start(f32[8,8,256]{2,1,0:T(8,128)} %residual.1) | copy-start | bytes 196612
  0.9 1.0 %copy-start.2 = (bf16[8,4,64,128]{3,2,1,0:T(8,128)(2,1)S(1)}, bf16[8,4,64,128]{3,2,1,0:T(8,128)(2,1)}, u32[]{:S(2)}) copy-start(bf16[8,4,64,128]{3,2,1,0:T(8,128)(2,1)} %warm.7) | copy-start | bytes 1572868
  1.9 0.9 %copy-start.5 = (f32[4,64,128]{2,1,0:T(8,128)S(1)}, f32[4,64,128]{2,1,0:T(8,128)}, u32[]{:S(2)}) copy-start(f32[4,64,128]{2,1,0:T(8,128)} %model.7) | copy-start | bytes 393220
  2.9 18.8 %copy-start.10 = (s32[7]{0:T(128)}, s32[7]{0:T(128)S(1)}, u32[]{:S(2)}) copy-start(s32[7]{0:T(128)S(1)} %stack.28.info) | copy-start | bytes 88
  2.9 11.7 %copy-start.4 = (bf16[8,4,64,128]{3,2,1,0:T(8,128)(2,1)S(1)}, bf16[8,4,64,128]{3,2,1,0:T(8,128)(2,1)}, u32[]{:S(2)}) copy-start(bf16[8,4,64,128]{3,2,1,0:T(8,128)(2,1)} %warm.7) | copy-start | bytes 1572868
  2.9 11.7 %copy-start.6 = (f32[4,64,128]{2,1,0:T(8,128)S(1)}, f32[4,64,128]{2,1,0:T(8,128)}, u32[]{:S(2)}) copy-start(f32[4,64,128]{2,1,0:T(8,128)} %model.7) | copy-start | bytes 393220
  3.4 11.1 %collective-permute-start = (f32[12,64,128]{2,1,0:T(8,128)S(1)}, f32[12,64,128]{2,1,0:T(8,128)S(1)}, u32[]{:S(2)}, u32[]{:S(2)}) collective-permute-start(f32[12,64,128]{2,1,0:T(8,128)S(1)} %shard_map.77), channel_id=1, source_target_pairs={{1,2},{2,1},{3,4},{4,3},{5,6},{6,5},{7,8},{8,7},{9,10},{10,9},{11,... | collective-permute-start | bytes 1179656 | tf_op jit(solution)/shard_map/ppermute | solution.py:508
  8.9 1.0 %copy-start = (bf16[8,4,64,128]{3,2,1,0:T(8,128)(2,1)S(1)}, bf16[8,4,64,128]{3,2,1,0:T(8,128)(2,1)}, u32[]{:S(2)}) copy-start(bf16[8,4,64,128]{3,2,1,0:T(8,128)(2,1)} %forward.3) | copy-start | bytes 1572868
  10.0 1.0 %copy-start.3 = (bf16[8,4,64,128]{3,2,1,0:T(8,128)(2,1)S(1)}, bf16[8,4,64,128]{3,2,1,0:T(8,128)(2,1)}, u32[]{:S(2)}) copy-start(bf16[8,4,64,128]{3,2,1,0:T(8,128)(2,1)} %warm.7) | copy-start | bytes 1572868
  11.6 10.1 %copy-start.1 = (bf16[8,4,64,128]{3,2,1,0:T(8,128)(2,1)S(1)}, bf16[8,4,64,128]{3,2,1,0:T(8,128)(2,1)}, u32[]{:S(2)}) copy-start(bf16[8,4,64,128]{3,2,1,0:T(8,128)(2,1)} %forward.3) | copy-start | bytes 1572868
  11.6 10.1 %collective-permute-start.1 = (f32[12,64,128]{2,1,0:T(8,128)S(1)}, f32[12,64,128]{2,1,0:T(8,128)S(1)}, u32[]{:S(2)}, u32[]{:S(2)}) collective-permute-start(f32[12,64,128]{2,1,0:T(8,128)S(1)} %shard_map.80), channel_id=1, source_target_pairs={{1,2},{2,1},{3,4},{4,3},{5,6},{6,5},{7,8},{8,7},{9,10},{10,9},{11,... | collective-permute-start | bytes 1179656 | tf_op jit(solution)/shard_map/ppermute | solution.py:508
  25.9 24.5 %copy-start.7 = (f32[4,64,128]{2,1,0:T(8,128)S(1)}, f32[4,64,128]{2,1,0:T(8,128)}, u32[]{:S(2)}) copy-start(f32[4,64,128]{2,1,0:T(8,128)} %model.7) | copy-start | bytes 393220
  25.9 24.5 %collective-permute-start.3 = (f32[9,64,128]{2,1,0:T(8,128)S(1)}, f32[9,64,128]{2,1,0:T(8,128)S(1)}, u32[]{:S(2)}, u32[]{:S(2)}) collective-permute-start(f32[9,64,128]{2,1,0:T(8,128)S(1)} %get-tuple-element.18.sent), channel_id=1, source_target_pairs={{1,2},{2,1},{3,4},{4,3},{5,6},{6,5},{7,8},{8,7},{9,10},{10,9},{11,... | collective-permute-start | bytes 884744 | tf_op jit(solution)/shard_map/ppermute | solution.py:508
  27.8 6.4 %collective-permute-start.4 = (f32[4,64,128]{2,1,0:T(8,128)S(1)}, f32[4,64,128]{2,1,0:T(8,128)S(1)}, u32[]{:S(2)}, u32[]{:S(2)}) collective-permute-start(f32[4,64,128]{2,1,0:T(8,128)S(1)} %slice.4), channel_id=1, source_target_pairs={{0,1},{1,0},{2,3},{3,2},{4,5},{5,4},{6,7},{7,6},{8,9},{9,8},{10,11... | collective-permute-start | bytes 393224 | tf_op jit(solution)/shard_map/ppermute | solution.py:508
  31.1 10.6 %collective-permute-start.2 = (f32[8,64,128]{2,1,0:T(8,128)S(1)}, f32[8,64,128]{2,1,0:T(8,128)S(1)}, u32[]{:S(2)}, u32[]{:S(2)}) collective-permute-start(f32[8,64,128]{2,1,0:T(8,128)S(1)} %get-tuple-element.15.sent_first), channel_id=1, source_target_pairs={{1,2},{2,1},{3,4},{4,3},{5,6},{6,5},{7,8},{8,7},{9,10},{10,9},{11,... | collective-permute-start | bytes 786440 | tf_op jit(solution)/shard_map/ppermute | solution.py:508
  34.1 0.7 %copy-start.13 = (f32[4,64,128]{2,1,0:T(8,128)}, f32[4,64,128]{2,1,0:T(8,128)S(1)}, u32[]{:S(2)}) copy-start(f32[4,64,128]{2,1,0:T(8,128)S(1)} %collective-permute-done.4.beside) | copy-start | bytes 393220
  37.3 13.1 %copy-start.8 = (f32[4,64,128]{2,1,0:T(8,128)S(1)}, f32[4,64,128]{2,1,0:T(8,128)}, u32[]{:S(2)}) copy-start(f32[4,64,128]{2,1,0:T(8,128)} %get-tuple-element.19.times) | copy-start | bytes 393220
  37.3 6.7 %collective-permute-start.5 = (f32[4,64,128]{2,1,0:T(8,128)}, f32[4,64,128]{2,1,0:T(8,128)S(1)}, u32[]{:S(2)}, u32[]{:S(2)}) collective-permute-start(f32[4,64,128]{2,1,0:T(8,128)} %get-tuple-element.20), channel_id=1, source_target_pairs={{0,4},{1,5},{2,6},{3,7},{4,0},{5,1},{6,2},{7,3},{8,12},{9,13},{10,... | collective-permute-start | bytes 393224 | tf_op jit(solution)/shard_map/ppermute | solution.py:508
  37.3 13.1 %collective-permute-start.6 = (f32[4,64,128]{2,1,0:T(8,128)}, f32[4,64,128]{2,1,0:T(8,128)S(1)}, u32[]{:S(2)}, u32[]{:S(2)}) collective-permute-start(f32[4,64,128]{2,1,0:T(8,128)} %get-tuple-element.21), channel_id=1, source_target_pairs={{0,8},{1,9},{2,10},{3,11},{4,12},{5,13},{6,14},{7,15},{8,0},{9,1},... | collective-permute-start | bytes 393224 | tf_op jit(solution)/shard_map/ppermute | solution.py:508
  39.4 11.0 %collective-permute-start.7 = (f32[4,64,128]{2,1,0:T(8,128)}, f32[4,64,128]{2,1,0:T(8,128)S(1)}, u32[]{:S(2)}, u32[]{:S(2)}) collective-permute-start(f32[4,64,128]{2,1,0:T(8,128)} %get-tuple-element.22), channel_id=1, source_target_pairs={{0,12},{1,13},{2,14},{3,15},{4,8},{5,9},{6,10},{7,11},{8,4},{9,5},... | collective-permute-start | bytes 393224 | tf_op jit(solution)/shard_map/ppermute | solution.py:508
  41.7 0.6 %copy-start.11 = (s32[7]{0:T(128)S(1)}, s32[7]{0:T(128)}, u32[]{:S(2)}) copy-start(s32[7]{0:T(128)} %copy-done.10) | copy-start | bytes 88

commit v2 on v1

--- a/solution.py
+++ b/solution.py
@@ -196,23 +196,46 @@
     return (field - after(field, axis)) * (other - after(other, axis))
 
 
-def pack_first(info, model, warm, out):
-    layers = model.shape[0]
-    out[:layers] = model[...]
-    for q in range(warm.shape[0]):
-        out[layers * (q + 1) : layers * (q + 2)] = warm[q].astype(jnp.float32)
-
-
-def pack_second(info, warm, forward, out):
-    count, layers = warm.shape[:2]
-    for q in range(count):
-        out[layers * q : layers * (q + 1)] = warm[q].astype(jnp.float32)
-    for q in range(forward.shape[0]):
-        out[count * layers + q] = forward[q, 0].astype(jnp.float32)
-
-
-def inject(info, residual, electrodes, out):
+def pack(info, warm, forward, first, second, held, edges, sems):
     tile = info[0]
+    half, layers = held.shape[:2]
+    count = half // 2
+    theirs = half * (1 - tile)
+    face = (layers - 1) * (1 - tile)
+    copies = [
+        pltpu.make_async_copy(warm.at[pl.ds(theirs, count)], held.at[:count], sems.at[0]),
+        pltpu.make_async_copy(warm.at[pl.ds(theirs + count, count)], held.at[count:], sems.at[1]),
+        pltpu.make_async_copy(forward.at[pl.ds(theirs, half), pl.ds(face, 1)], edges, sems.at[2]),
+    ]
+    for copy in copies:
+        copy.start()
+    copies[0].wait()
+    for q in range(count):
+        first[layers * q : layers * (q + 1)] = held[q].astype(jnp.float32)
+    copies[1].wait()
+    for q in range(count):
+        second[layers * q : layers * (q + 1)] = held[count + q].astype(jnp.float32)
+    copies[2].wait()
+    for q in range(half):
+        second[count * layers + q] = edges[q, 0].astype(jnp.float32)
+
+
+def inject(info, order, residual, electrodes, out, weights):
+    tile = info[0]
+    surveys = order.shape[0]
+    ranks = []
+    for k in range(6):
+        found = 0
+        for i in range(surveys):
+            found = found + jnp.where(order[i] == info[1 + k], i, 0)
+        ranks.append(found)
+    for k in range(4):
+        a = ranks[2 + k]
+        ends = jnp.where(a == 0, 1, 0) + jnp.where(a == surveys - 1, 1, 0)
+        for m in range(2):
+            b = ranks[m]
+            value = jnp.where(a == b, 2 - ends, jnp.where(jnp.abs(a - b) == 1, -1, 0))
+            weights[2 * k + m] = value.astype(jnp.float32)
     sources, _, rows_y, rows_z = out.shape
     half = residual.shape[1] // 2
     cells = out.shape[1] * rows_y * rows_z
@@ -224,7 +247,8 @@
     at_row = lax.broadcasted_iota(jnp.int32, (rows, count), 0) == row
     at_row = jnp.where(at_row, 1.0, 0.0).astype(jnp.bfloat16)
     at_lane = lax.broadcasted_iota(jnp.int32, (rows_z, count), 0) == lane
-    mine = jnp.where(tile == 0, residual[0, :half], residual[0, half:])
+    mine = residual[info[1]]
+    mine = jnp.where(tile == 0, mine[:half], mine[half:])
     total = None
     for _ in range(3):
         part = mine.astype(jnp.bfloat16).astype(jnp.float32)
@@ -240,7 +264,8 @@
         out[q] = total[:, q * rows_z : (q + 1) * rows_z].reshape(out.shape[1:])
 
 
-def find_coefs(tile, model, other, sigma, coefs):
+def find_coefs(info, model, other, coefs, sigma):
+    tile = info[0]
     layers = model.shape[0]
     full = 2 * layers
     shape = model.shape[1:]
@@ -271,7 +296,7 @@
         coefs[6, i] = scale
 
 
-def sweeps(coefs, rhs, start, rest, lam, mine, sent):
+def sweeps(coefs, rhs, base, start, rest, lam, mine):
     count, full = start.shape[:2]
 
     def around(field, q, i, weight):
@@ -285,7 +310,7 @@
         weight = [coefs[k, i] for k in range(7)]
         for q in range(count):
             here, total = around(start, q, i, weight)
-            step = rhs[q, i] * weight[6] - here + total
+            step = rhs[base + q, i] * weight[6] - here + total
             mine[0, q, i] = step
             lam[q, i] = here + step
         return carry
@@ -311,30 +336,34 @@
         lax.fori_loop(0, full, later, 0)
 
 
-def solve_first(info, model, got, warm, rhs, coefs, own, sent, sigma, start, rest, lam, mine):
-    layers = model.shape[0]
-    count = warm.shape[0]
-    find_coefs(info[0], model, got.at[:layers], sigma, coefs)
-    for q in range(count):
-        start[q, :layers] = warm[q].astype(jnp.float32)
-        start[q, layers:] = got[layers * (q + 1) : layers * (q + 2)]
-    sweeps(coefs, rhs, start, rest, lam, mine, None)
+def load_start(warm, source, got, start):
+    count, full = start.shape[:2]
+    layers = full // 2
+    for q in range(count):
+        start[q, :layers] = warm[source + q].astype(jnp.float32)
+        start[q, layers:] = got[layers * q : layers * (q + 1)]
+
+
+def solve_first(info, coefs, got, warm, rhs, own, sent, start, rest, lam, mine):
+    count, layers = own.shape[:2]
+    load_start(warm, 2 * count * info[0], got, start)
+    sweeps(coefs, rhs, 0, start, rest, lam, mine)
     for q in range(count):
         own[q] = lam[q, :layers]
         sent[layers * q : layers * (q + 1)] = lam[q, layers:]
 
 
-def solve_second(info, coefs, got, warm, rhs, face, own_first, sent_first, own, sent, start, rest, lam, mine):
-    count, layers = warm.shape[:2]
-    for q in range(count):
-        start[q, :layers] = warm[q].astype(jnp.float32)
-        start[q, layers:] = got[layers * q : layers * (q + 1)]
-    sweeps(coefs, rhs, start, rest, lam, mine, None)
+def solve_second(info, coefs, got, warm, rhs, forward, own_first, sent_first, times, near_a, near_b, near_c, own, sent, time, start, rest, lam, mine):
+    count, layers = own.shape[:2]
+    time[...] = (times[...] + near_a[...]) + (near_b[...] + near_c[...])
+    source = 2 * count * info[0]
+    load_start(warm, source + count, got, start)
+    sweeps(coefs, rhs, count, start, rest, lam, mine)
     near = (layers - 1) * (1 - info[0])
     far = (layers - 1) * info[0]
     total = None
     for q in range(2 * count):
-        slope = face[q, 0].astype(jnp.float32) - got[count * layers + q]
+        slope = forward[source + q, near].astype(jnp.float32) - got[count * layers + q]
         if q < count:
             drop = own_first[q, near] - sent_first[layers * q + far]
         else:
@@ -365,42 +394,51 @@
         mass[i] = mass[i] + totals[3]
 
 
-def gather_terms(info, forward_a, forward_b, forward_c, own_first, own_second, back, sums, adjoint):
+def gather_terms(info, forward, own_first, own_second, back, sums, adjoint, rounded, sems):
     count, layers = own_first.shape[:2]
+    tile = info[0]
+    mine, theirs = 2 * count * tile, 2 * count * (1 - tile)
+    for q in range(count):
+        rounded[q] = own_first[q].astype(jnp.bfloat16)
+        rounded[count + q] = own_second[q].astype(jnp.bfloat16)
+        rounded[2 * count + q] = back[layers * q : layers * (q + 1)].astype(jnp.bfloat16)
+    copies = [
+        pltpu.make_async_copy(rounded.at[: 2 * count], adjoint.at[pl.ds(mine, 2 * count)], sems.at[0]),
+        pltpu.make_async_copy(rounded.at[2 * count :], adjoint.at[pl.ds(theirs, count)], sems.at[1]),
+    ]
+    for copy in copies:
+        copy.start()
     sums[...] = jnp.zeros(sums.shape, jnp.float32)
     pairs = []
-    for forward, lam in ((forward_a, own_first), (forward_b, own_second)):
-        for q in range(count):
-            pairs.append((
-                lambda i, f=forward, q=q: f[q, i].astype(jnp.float32),
-                lambda i, l=lam, q=q: l[q, i],
-            ))
-    for q in range(count):
-        pairs.append((
-            lambda i, q=q: forward_c[q, i].astype(jnp.float32),
-            lambda i, q=q: back[layers * q + i],
-        ))
+    for q in range(count):
+        pairs.append((mine + q, lambda i, q=q: own_first[q, i]))
+        pairs.append((mine + count + q, lambda i, q=q: own_second[q, i]))
+        pairs.append((theirs + q, lambda i, q=q: back[layers * q + i]))
+    pairs = [(lambda i, s=s: forward[s, i].astype(jnp.float32), lam) for s, lam in pairs]
     data_sums(pairs, layers, sums.at[0], sums.at[1], sums.at[2], sums.at[3])
-    for q in range(count):
-        adjoint[q] = own_first[q].astype(jnp.bfloat16)
-        adjoint[count + q] = own_second[q].astype(jnp.bfloat16)
-        adjoint[2 * count + q] = back[layers * q : layers * (q + 1)].astype(jnp.bfloat16)
-
-
-def finish(info, sums, back, sent, forward, model, other, times, near_a, near_b, near_c, three, adjoint, gradient):
+    for copy in copies:
+        copy.wait()
+
+
+def finish(info, sums, back, sent, forward, model, other, times, kept, adjoint, gradient, rounded, result, sems):
     tile = info[0]
-    count, layers = forward.shape[:2]
+    count, layers = rounded.shape[:2]
+    theirs = 2 * count * (1 - tile) + count
+    for q in range(count):
+        rounded[q] = back[layers * q : layers * (q + 1)].astype(jnp.bfloat16)
+    copies = [pltpu.make_async_copy(rounded, adjoint.at[pl.ds(theirs, count)], sems.at[layers])]
+    copies[0].start()
     shape = model.shape[1:]
     pairs = []
     for q in range(count):
         pairs.append((
-            lambda i, q=q: forward[q, i].astype(jnp.float32),
+            lambda i, q=q: forward[theirs + q, i].astype(jnp.float32),
             lambda i, q=q: back[layers * q + i],
         ))
     in_y, in_z = inner(shape, 0), inner(shape, 1)
     low = jnp.where(tile == 0, 0.0, 1.0)
     high = 1.0 - low
-    cross = back[count * layers] + sent[0]
+    cross = back[count * layers] + sent[count * layers]
     bridge = other[(layers - 1) * tile]
     products, falls = [low * cross], [low * (bridge - model[0])]
     for i in range(layers):
@@ -428,63 +466,45 @@
         fall_y = jnp.where(in_y, value - after(value, 0), 0.0)
         fall_z = jnp.where(in_z, value - after(value, 1), 0.0)
         space = falls[i + 1] - falls[i] + (fall_y - before(fall_y, 0)) + (fall_z - before(fall_z, 1))
-        time = times[i] + near_a[i] + near_b[i] + near_c[i]
-        gradient[i] = space + time - jnp.exp(value) * (0.5 * terms + GROUND * mass)
-    spot = count * 2 * tile
-    for q in range(2 * count):
-        adjoint[spot + q] = three[q]
-    spot = count * 2 * (1 - tile)
-    for q in range(count):
-        adjoint[spot + q] = three[2 * count + q]
-        adjoint[spot + count + q] = back[layers * q : layers * (q + 1)].astype(jnp.bfloat16)
-
-
-def time_parts(info, order, model, beside, times, part_a, part_b, part_c):
-    surveys = order.shape[0]
-
-    def rank(survey):
-        found = 0
-        for i in range(surveys):
-            found = found + jnp.where(order[i] == survey, i, 0)
-        return found
-
-    def couple(first, second):
-        a, b = rank(first), rank(second)
-        ends = jnp.where(a == 0, 1, 0) + jnp.where(a == surveys - 1, 1, 0)
-        value = jnp.where(a == b, 2 - ends, jnp.where(jnp.abs(a - b) == 1, -1, 0))
-        return value.astype(jnp.float32)
-
-    mine, sibling = info[1], info[2]
+        result[i] = space + times[i] - jnp.exp(value) * (0.5 * terms + GROUND * mass)
+        copies.append(pltpu.make_async_copy(result.at[i], gradient.at[i], sems.at[i]))
+        copies[-1].start()
+    for copy in copies:
+        copy.wait()
+
+
+def time_parts(weights, model, beside, times, part_a, part_b, part_c):
     for k, out in enumerate((times, part_a, part_b, part_c)):
-        target = info[3 + k]
-        out[...] = couple(target, mine) * model[...] + couple(target, sibling) * beside[...]
-
-
-def call(kernel, info, operands, specs, out_shapes, out_specs=None, scratch=()):
-    if out_specs is None:
-        out_specs = [whole(s.shape) for s in out_shapes]
+        out[...] = weights[2 * k] * model[...] + weights[2 * k + 1] * beside[...]
+
+
+V, S, H = pltpu.VMEM, pltpu.SMEM, pltpu.HBM
+
+
+def call(kernel, operands, spaces, out_shapes, out_spaces=None, scratch=(), aliases=None, micros=1, room=16):
     several = len(out_shapes) > 1
+    specs = [pl.BlockSpec(memory_space=m) for m in spaces]
+    out_specs = [pl.BlockSpec(memory_space=m) for m in out_spaces or [V] * len(out_shapes)]
     return pl.pallas_call(
         kernel,
         out_shape=out_shapes if several else out_shapes[0],
-        grid_spec=pltpu.PrefetchScalarGridSpec(
-            num_scalar_prefetch=1,
-            grid=(1,),
-            in_specs=specs,
-            out_specs=out_specs if several else out_specs[0],
-            scratch_shapes=list(scratch),
+        in_specs=specs,
+        out_specs=out_specs if several else out_specs[0],
+        scratch_shapes=list(scratch),
+        input_output_aliases=aliases or {},
+        compiler_params=pltpu.CompilerParams(vmem_limit_bytes=room * 2**20),
+        cost_estimate=pl.CostEstimate(
+            flops=micros * 10**9, bytes_accessed=micros * 3 * 10**6, transcendentals=0
         ),
-        compiler_params=pltpu.CompilerParams(vmem_limit_bytes=48 * 2**20),
-    )(info, *operands)
-
-
-def whole(shape):
-    zeros = (0,) * len(shape)
-    return pl.BlockSpec(tuple(shape), lambda g, info: zeros)
+    )(*operands)
 
 
 def f32(*shape):
     return jax.ShapeDtypeStruct(shape, jnp.float32)
+
+
+def bf16(*shape):
+    return jax.ShapeDtypeStruct(shape, jnp.bfloat16)
 
 
 def paired(model, forward, warm_start, residual_data, electrodes, survey_order):
@@ -493,12 +513,9 @@
     full = 2 * layers
     devices = lax.axis_size("space")
     position = lax.axis_index("space")
-    tile = (position + 1) % 2
-    survey = (position + 1) // 2 % SURVEYS
-    sibling = (position ^ 1) + 1
-    sibling = sibling // 2 % SURVEYS
-    targets = [((position ^ (4 * k)) + 1) // 2 % SURVEYS for k in range(4)]
-    info = jnp.stack([tile, survey, sibling] + targets).astype(jnp.int32)
+    places = [position, position ^ 1] + [position ^ (4 * k) for k in range(4)]
+    tile = (position + 1) & 1
+    info = jnp.stack([tile] + [((p + 1) >> 1) & (SURVEYS - 1) for p in places]).astype(jnp.int32)
     pairs = []
     for p in range(1, devices, 2):
         pairs += [(p, (p + 1) % devices), ((p + 1) % devices, p)]
@@ -507,106 +524,76 @@
         links = pairs if mask is None else [(p, p ^ mask) for p in range(devices)]
         return lax.ppermute(x, "space", links)
 
-    block = (count, layers, ny, nz)
-    mine_a = pl.BlockSpec(block, lambda g, info: (2 * info[0], 0, 0, 0))
-    mine_b = pl.BlockSpec(block, lambda g, info: (2 * info[0] + 1, 0, 0, 0))
-    theirs_a = pl.BlockSpec(block, lambda g, info: (2 - 2 * info[0], 0, 0, 0))
-    theirs_b = pl.BlockSpec(block, lambda g, info: (3 - 2 * info[0], 0, 0, 0))
-    edge = (half, 1, ny, nz)
-    my_edge = pl.BlockSpec(edge, lambda g, info: (info[0], (layers - 1) * (1 - info[0]), 0, 0))
-    their_edge = pl.BlockSpec(edge, lambda g, info: (1 - info[0], (layers - 1) * (1 - info[0]), 0, 0))
-
+    dma = pltpu.SemaphoreType.DMA
     slab = (layers, ny, nz)
-    first = call(
-        pack_first, info, (model, warm_start), [whole(slab), theirs_a], [f32((count + 1) * layers, ny, nz)]
+    other = swap(model)
+    first, second = call(
+        pack,
+        (info, warm_start, forward),
+        (S, H, H),
+        [f32(count * layers, ny, nz), f32(count * layers + half, ny, nz)],
+        scratch=[V((half, *slab), jnp.bfloat16), V((half, 1, ny, nz), jnp.bfloat16), dma((3,))],
+        room=60,
     )
     got_first = swap(first)
-    second = call(
-        pack_second, info, (warm_start, forward), [theirs_b, their_edge], [f32(count * layers + half, ny, nz)]
-    )
     got_second = swap(second)
-    electrodes_row = electrodes.reshape(1, -1)
-    rhs = call(
+    rhs, weights_time = call(
         inject,
-        info,
-        (residual_data, electrodes_row),
-        [
-            pl.BlockSpec((1,) + residual_data.shape[1:], lambda g, info: (info[1], 0, 0)),
-            whole(electrodes_row.shape),
-        ],
-        [f32(half, full, ny, nz)],
-    )
-    other = got_first[:layers]
+        (info, survey_order, residual_data, electrodes.reshape(1, -1)),
+        (S, S, V, V),
+        [f32(half, full, ny, nz), f32(8)],
+        [V, S],
+    )
     beside = swap(other, 1)
-    fields = [
-        pltpu.VMEM((count, full, ny, nz), jnp.float32),
-        pltpu.VMEM((count, full, ny, nz), jnp.float32),
-        pltpu.VMEM((count, full, ny, nz), jnp.float32),
-        pltpu.VMEM((2, count, full, ny, nz), jnp.float32),
-    ]
-    rhs_block = (count, full, ny, nz)
-    coefs, own_first, sent_first = call(
+    coefs = call(
+        find_coefs,
+        (info, model, other),
+        (S, V, V),
+        [f32(7, full, ny, nz)],
+        scratch=[V((full, ny, nz), jnp.float32)],
+    )
+    times, part_a, part_b, part_c = call(
+        time_parts, (weights_time, model, beside), (S, V, V), [f32(*slab)] * 4
+    )
+    near = [swap(part, 4 * (k + 1)) for k, part in enumerate((part_a, part_b, part_c))]
+    field = V((count, full, ny, nz), jnp.float32)
+    fields = [field, field, field, V((2, count, full, ny, nz), jnp.float32)]
+    block = f32(count, *slab)
+    own_first, sent_first = call(
         solve_first,
-        info,
-        (model, got_first, warm_start, rhs),
-        [whole(slab), whole(got_first.shape), mine_a, pl.BlockSpec(rhs_block, lambda g, info: (0, 0, 0, 0))],
-        [f32(7, full, ny, nz), f32(*block), f32(count * layers, ny, nz)],
-        scratch=[pltpu.VMEM((full, ny, nz), jnp.float32)] + fields,
+        (info, coefs, got_first, warm_start, rhs),
+        (S, V, V, V, V),
+        [block, f32(count * layers, ny, nz)],
+        scratch=fields,
+        micros=4,
     )
     back_first = swap(sent_first)
-    times, part_a, part_b, part_c = pl.pallas_call(
-        time_parts,
-        out_shape=[f32(*slab)] * 4,
-        grid_spec=pltpu.PrefetchScalarGridSpec(
-            num_scalar_prefetch=2,
-            grid=(1,),
-            in_specs=[pl.BlockSpec(slab, lambda g, info, order: (0, 0, 0))] * 2,
-            out_specs=[pl.BlockSpec(slab, lambda g, info, order: (0, 0, 0))] * 4,
-        ),
-    )(info, survey_order, model, beside)
-    near = [swap(part, 4 * (k + 1)) for k, part in enumerate((part_a, part_b, part_c))]
-    own_second, sent_second = call(
+    own_second, sent_second, time = call(
         solve_second,
-        info,
-        (coefs, got_second, warm_start, rhs, forward, own_first, sent_first),
-        [
-            whole(coefs.shape),
-            whole(got_second.shape),
-            mine_b,
-            pl.BlockSpec(rhs_block, lambda g, info: (1, 0, 0, 0)),
-            my_edge,
-            whole(own_first.shape),
-            whole(sent_first.shape),
-        ],
-        [f32(*block), f32(count * layers + 1, ny, nz)],
+        (info, coefs, got_second, warm_start, rhs, forward, own_first, sent_first, times, *near),
+        (S, V, V, V, V, V, V, V, V, V, V, V),
+        [block, f32(count * layers + 1, ny, nz), f32(*slab)],
         scratch=fields,
+        micros=4,
     )
     back_second = swap(sent_second)
-    sums, three = call(
+    sums, kept = call(
         gather_terms,
-        info,
-        (forward, forward, forward, own_first, own_second, back_first),
-        [mine_a, mine_b, theirs_a, whole(own_first.shape), whole(own_second.shape), whole(back_first.shape)],
-        [f32(4, *slab), jax.ShapeDtypeStruct((3 * count, layers, ny, nz), jnp.bfloat16)],
+        (info, forward, own_first, own_second, back_first),
+        (S, V, V, V, V),
+        [f32(4, *slab), bf16(*forward.shape)],
+        [V, H],
+        scratch=[V((3 * count, *slab), jnp.bfloat16), dma((2,))],
+        micros=2,
     )
     adjoint, gradient = call(
         finish,
-        info,
-        (sums, back_second, sent_second, forward, model, got_first, times, *near, three),
-        [
-            whole(sums.shape),
-            whole(back_second.shape),
-            pl.BlockSpec((1, ny, nz), lambda g, info: (count * layers, 0, 0)),
-            theirs_b,
-            whole(slab),
-            whole(slab),
-            whole(slab),
-            whole(slab),
-            whole(slab),
-            whole(slab),
-            whole(three.shape),
-        ],
-        [jax.ShapeDtypeStruct(forward.shape, jnp.bfloat16), f32(*slab)],
+        (info, sums, back_second, sent_second, forward, model, other, time, kept),
+        (S, V, V, V, V, V, V, V, H),
+        [bf16(*forward.shape), f32(*slab)],
+        [H, H],
+        scratch=[V((count, *slab), jnp.bfloat16), V(slab, jnp.float32), dma((layers + 1,))],
+        aliases={8: 0},
     )
     return adjoint, gradient
 

time: 52.6 us -> 48.6 us (0.924)
  the two profiles are of different devices: /device:TPU:0 before, /device:TPU:12 now
where the time goes in v2:
time: 48.6 us; the launch traced here: 48.5 us
  waiting for transfers between devices  20.7 us (43%)
  Pallas kernels  17.3 us (36%)
  starting transfers between devices  8.94 us (18%)
  between operations  0.77 us (2%)
  local copies, waits for them, and re-layouts  0.7 us (1%)
    ppermute x9, waiting for transfers between devices, swap(): return lax.ppermute(x, 'space', links)  20.7 us
    pallas_call x8, Pallas kernels, call(): pl.pallas_call(kernel, out_shape=out_shapes if several else out_shapes[0]...  17.3 us
    ppermute x9, starting transfers between devices, swap(): return lax.ppermute(x, 'space', links)  8.94 us
  transfers between devices with their start and end apart: 9, of which 5 were waited for; matrix products, arithmetic and copies ran while one was open for 1% of the time, Pallas kernels for 32%

profile of v2, /device:TPU:12, one launch (start us, length us, event | category | flops | bytes accessed | tf_op | source)
XLA Modules:
  0.0 48.5 jit_solution(5882150084770333178)
XLA Ops:
  0.6 0.1 collective-permute-start
  0.7 0.7 %stack.28.info = s32[7]{0:T(128)} concatenate(s32[1]{0:T(128)} %bitcast, s32[1]{0:T(128)} %bitcast.1, s32[1]{0:T(128)} %bitcast.2, s32[1]{0:T(128)} %bitcast.1, s32[1]{0:T(128)} %bitcast.3, s32[1]{0:T(128)} %bitcast.4, s32[1]{0:T(128)} %bitcast.5), dimensions={0} | concatenate | bytes 56 | tf_op jit(solution)/shard_map/stack | solution.py:518
  1.4 0.0 copy-start
  1.4 0.0 copy-start.4
  1.4 0.0 copy-start.5
  1.4 0.0 copy-start.6
  1.4 2.6 %shard_map.78 = (f32[8,64,128]{2,1,0:T(8,128)}, f32[12,64,128]{2,1,0:T(8,128)}) custom-call(s32[7]{0:T(128)} %stack.28.info, bf16[8,4,64,128]{3,2,1,0:T(8,128)(2,1)} %warm.5, bf16[8,4,64,128]{3,2,1,0:T(8,128)(2,1)} %forward.7), custom_call_target="tpu_custom_call" | custom-call | flops 1000000000 | bytes 3000000 | tf_op jit(solution)/shard_map/pallas_call | solution.py:488
  4.1 1.8 %collective-permute-start.1 = (f32[8,64,128]{2,1,0:T(8,128)}, f32[8,64,128]{2,1,0:T(8,128)S(1)}, u32[]{:S(2)}, u32[]{:S(2)}) collective-permute-start(f32[8,64,128]{2,1,0:T(8,128)} %get-tuple-element.17), channel_id=1, source_target_pairs={{1,2},{2,1},{3,4},{4,3},{5,6},{6,5},{7,8},{8,7},{9,10},{10,9},{11,... | collective-permute-start | bytes 786440 | tf_op jit(solution)/shard_map/ppermute | solution.py:525
  5.8 0.1 collective-permute-start.2
  5.9 0.8 %collective-permute-done.other = f32[4,64,128]{2,1,0:T(8,128)S(1)} collective-permute-done((f32[4,64,128]{2,1,0:T(8,128)}, f32[4,64,128]{2,1,0:T(8,128)S(1)}, u32[]{:S(2)}, u32[]{:S(2)}) %collective-permute-start) | collective-permute-done | bytes 131104 | tf_op jit(solution)/shard_map/ppermute | solution.py:525
  6.7 1.7 %collective-permute-start.3 = (f32[4,64,128]{2,1,0:T(8,128)S(1)}, f32[4,64,128]{2,1,0:T(8,128)S(1)}, u32[]{:S(2)}, u32[]{:S(2)}) collective-permute-start(f32[4,64,128]{2,1,0:T(8,128)S(1)} %collective-permute-done.other), channel_id=1, source_target_pairs={{0,1},{1,0},{2,3},{3,2},{4,5},{5,4},{6,7},{7,6},{8,9},{9,8},{10,11... | collective-permute-start | bytes 393224 | tf_op jit(solution)/shard_map/ppermute | solution.py:525
  8.4 0.0 copy-done
  8.4 0.0 copy-done.4
  8.4 0.0 copy-done.5
  8.4 0.0 copy-done.6
  8.4 0.0 copy-start.3
  8.4 1.2 %shard_map.79 = (f32[4,8,64,128]{3,2,1,0:T(8,128)S(1)}, f32[8]{0:T(128)S(1)}) custom-call(s32[7]{0:T(128)S(1)} %copy-done, s32[8]{0:T(128)S(1)} %copy-done.6, f32[8,8,256]{2,1,0:T(8,128)S(1)} %copy-done.4, s32[1,256]{1,0:T(1,128)S(1)} %bitcast.7), custom_call_target="tpu_custom_call" | custom-call | flops 1000000000 | bytes 3000000 | tf_op jit(solution)/shard_map/pallas_call | solution.py:488
  9.6 0.0 copy-done.3
  9.6 0.9 %shard_map.77.coefs = f32[7,8,64,128]{3,2,1,0:T(8,128)S(1)} custom-call(s32[7]{0:T(128)S(1)} %copy-done, f32[4,64,128]{2,1,0:T(8,128)S(1)} %copy-done.3, f32[4,64,128]{2,1,0:T(8,128)S(1)} %collective-permute-done.other), custom_call_target="tpu_custom_call" | custom-call | flops 1000000000 | bytes 3000000 | tf_op jit(solution)/shard_map/pallas_call | solution.py:488
  10.5 0.0 collective-permute-done.3.beside
  10.5 0.0 copy-start.1
  10.5 0.6 %shard_map.81 = (f32[4,64,128]{2,1,0:T(8,128)S(1)}, f32[4,64,128]{2,1,0:T(8,128)S(1)}, f32[4,64,128]{2,1,0:T(8,128)S(1)}, f32[4,64,128]{2,1,0:T(8,128)S(1)}) custom-call(f32[8]{0:T(128)S(1)} %get-tuple-element.22.weights, f32[4,64,128]{2,1,0:T(8,128)S(1)} %copy-done.3, f32[4,64,128]{2,1,0:T(8,128)S(1)} %collective-permute-done.3.beside), custom_call_target="tpu_custom_call" | custom-call | flops 1000000000 | bytes 3000000 | tf_op jit(solution)/shard_map/pallas_call | solution.py:488
  11.1 0.5 %collective-permute-start.4 = (f32[4,64,128]{2,1,0:T(8,128)S(1)}, f32[4,64,128]{2,1,0:T(8,128)S(1)}, u32[]{:S(2)}, u32[]{:S(2)}) collective-permute-start(f32[4,64,128]{2,1,0:T(8,128)S(1)} %get-tuple-element.24), channel_id=1, source_target_pairs={{0,4},{1,5},{2,6},{3,7},{4,0},{5,1},{6,2},{7,3},{8,12},{9,13},{10,... | collective-permute-start | bytes 393224 | tf_op jit(solution)/shard_map/ppermute | solution.py:525
  11.7 2.6 %collective-permute-start.5 = (f32[4,64,128]{2,1,0:T(8,128)S(1)}, f32[4,64,128]{2,1,0:T(8,128)S(1)}, u32[]{:S(2)}, u32[]{:S(2)}) collective-permute-start(f32[4,64,128]{2,1,0:T(8,128)S(1)} %get-tuple-element.25), channel_id=1, source_target_pairs={{0,8},{1,9},{2,10},{3,11},{4,12},{5,13},{6,14},{7,15},{8,0},{9,1},... | collective-permute-start | bytes 393224 | tf_op jit(solution)/shard_map/ppermute | solution.py:525
  14.3 0.5 collective-permute-start.6
  14.7 2.4 %collective-permute-done.1.got = f32[8,64,128]{2,1,0:T(8,128)S(1)} collective-permute-done((f32[8,64,128]{2,1,0:T(8,128)}, f32[8,64,128]{2,1,0:T(8,128)S(1)}, u32[]{:S(2)}, u32[]{:S(2)}) %collective-permute-start.1) | collective-permute-done | bytes 262176 | tf_op jit(solution)/shard_map/ppermute | solution.py:525
  17.2 0.0 copy-done.1
  17.2 0.0 copy-start.2
  17.2 4.2 %shard_map.80 = (f32[2,4,64,128]{3,2,1,0:T(8,128)S(1)}, f32[8,64,128]{2,1,0:T(8,128)S(1)}) custom-call(s32[7]{0:T(128)S(1)} %copy-done, f32[7,8,64,128]{3,2,1,0:T(8,128)S(1)} %shard_map.77.coefs, f32[8,64,128]{2,1,0:T(8,128)S(1)} %collective-permute-done.1.got, bf16[8,4,64,128]{3,2,1,0:T(8,128)(2,1)S(1)} %copy-done.1, ...), custom_call_target="tpu_custom_call" | custom-call | flops 4000000000 | bytes 12000000 | tf_op jit(solution)/shard_map/pallas_call | solution.py:488
  21.3 1.7 %collective-permute-start.7 = (f32[8,64,128]{2,1,0:T(8,128)S(1)}, f32[8,64,128]{2,1,0:T(8,128)S(1)}, u32[]{:S(2)}, u32[]{:S(2)}) collective-permute-start(f32[8,64,128]{2,1,0:T(8,128)S(1)} %get-tuple-element.21.sent_first), channel_id=1, source_target_pairs={{1,2},{2,1},{3,4},{4,3},{5,6},{6,5},{7,8},{8,7},{9,10},{10,9},{11,... | collective-permute-start | bytes 786440 | tf_op jit(solution)/shard_map/ppermute | solution.py:525
  23.0 1.9 %collective-permute-done.4.near_a = f32[4,64,128]{2,1,0:T(8,128)S(1)} collective-permute-done((f32[4,64,128]{2,1,0:T(8,128)S(1)}, f32[4,64,128]{2,1,0:T(8,128)S(1)}, u32[]{:S(2)}, u32[]{:S(2)}) %collective-permute-start.4) | collective-permute-done | bytes 131104 | tf_op jit(solution)/shard_map/ppermute | solution.py:525
  24.9 0.0 collective-permute-done.5.near_b
  24.9 8.2 %collective-permute-done.6.near_c = f32[4,64,128]{2,1,0:T(8,128)S(1)} collective-permute-done((f32[4,64,128]{2,1,0:T(8,128)S(1)}, f32[4,64,128]{2,1,0:T(8,128)S(1)}, u32[]{:S(2)}, u32[]{:S(2)}) %collective-permute-start.6) | collective-permute-done | bytes 131104 | tf_op jit(solution)/shard_map/ppermute | solution.py:525
  33.1 0.0 collective-permute-done.2.got
  33.1 0.0 copy-done.2
  33.1 4.2 %shard_map.82 = (f32[2,4,64,128]{3,2,1,0:T(8,128)S(1)}, f32[9,64,128]{2,1,0:T(8,128)S(1)}, f32[4,64,128]{2,1,0:T(8,128)S(1)}) custom-call(s32[7]{0:T(128)S(1)} %copy-done, f32[7,8,64,128]{3,2,1,0:T(8,128)S(1)} %shard_map.77.coefs, f32[12,64,128]{2,1,0:T(8,128)S(1)} %collective-permute-done.2.got, bf16[8,4,64,128]{3,2,1,0:T(8,128)(2,1)S(1)} %copy-done.1, ...), custom_call_target="tpu_custom_call" | custom-call | flops 4000000000 | bytes 12000000 | tf_op jit(solution)/shard_map/pallas_call | solution.py:488
  37.4 0.1 collective-permute-start.8
  37.4 0.0 collective-permute-done.7.back
  37.4 1.9 %shard_map.83 = (f32[4,4,64,128]{3,2,1,0:T(8,128)S(1)}, bf16[8,4,64,128]{3,2,1,0:T(8,128)(2,1)}) custom-call(s32[7]{0:T(128)S(1)} %copy-done, bf16[8,4,64,128]{3,2,1,0:T(8,128)(2,1)S(1)} %copy-done.2, f32[2,4,64,128]{3,2,1,0:T(8,128)S(1)} %get-tuple-element.19.own_first, f32[2,4,64,128]{3,2,1,0:T(8,128)S(1)} %get-tuple-element.27.own_second, ...), custom_call_target="tpu_custom_call" | custom-call | flops 2000000000 | bytes 6000000 | tf_op jit(solution)/shard_map/pallas_call | solution.py:488
  39.3 7.4 %collective-permute-done.8.back = f32[9,64,128]{2,1,0:T(8,128)S(1)} collective-permute-done((f32[9,64,128]{2,1,0:T(8,128)S(1)}, f32[9,64,128]{2,1,0:T(8,128)S(1)}, u32[]{:S(2)}, u32[]{:S(2)}) %collective-permute-start.8) | collective-permute-done | bytes 294944 | tf_op jit(solution)/shard_map/ppermute | solution.py:525
  46.7 1.7 %shard_map.84 = (bf16[8,4,64,128]{3,2,1,0:T(8,128)(2,1)}, f32[4,64,128]{2,1,0:T(8,128)}) custom-call(s32[7]{0:T(128)S(1)} %copy-done, f32[4,4,64,128]{3,2,1,0:T(8,128)S(1)} %get-tuple-element.28.sums, f32[9,64,128]{2,1,0:T(8,128)S(1)} %collective-permute-done.8.back, f32[9,64,128]{2,1,0:T(8,128)S(1)} %get-tuple-element.29.sent, ...), custom_call_target="tpu_custom_call", output_to_operand_aliasing={{0}: (8, {})} | custom-call | flops 1000000000 | bytes 3000000 | tf_op jit(solution)/shard_map/pallas_call | solution.py:488
Async XLA Ops:
  0.6 6.1 %collective-permute-start = (f32[4,64,128]{2,1,0:T(8,128)}, f32[4,64,128]{2,1,0:T(8,128)S(1)}, u32[]{:S(2)}, u32[]{:S(2)}) collective-permute-start(f32[4,64,128]{2,1,0:T(8,128)} %model.5), channel_id=1, source_target_pairs={{1,2},{2,1},{3,4},{4,3},{5,6},{6,5},{7,8},{8,7},{9,10},{10,9},{11,... | collective-permute-start | bytes 393224 | tf_op jit(solution)/shard_map/ppermute | solution.py:525
  1.4 7.0 %copy-start = (s32[7]{0:T(128)S(1)}, s32[7]{0:T(128)}, u32[]{:S(2)}) copy-start(s32[7]{0:T(128)} %stack.28.info) | copy-start | bytes 88
  1.4 7.0 %copy-start.4 = (f32[8,8,256]{2,1,0:T(8,128)S(1)}, f32[8,8,256]{2,1,0:T(8,128)}, u32[]{:S(2)}) copy-start(f32[8,8,256]{2,1,0:T(8,128)} %residual.1) | copy-start | bytes 196612
  1.4 7.0 %copy-start.5 = (s32[256]{0:T(256)S(1)}, s32[256]{0:T(256)}, u32[]{:S(2)}) copy-start(s32[256]{0:T(256)} %param.10) | copy-start | bytes 3076
  1.4 7.0 %copy-start.6 = (s32[8]{0:T(128)S(1)}, s32[8]{0:T(128)}, u32[]{:S(2)}) copy-start(s32[8]{0:T(128)} %order.1) | copy-start | bytes 100
  4.1 13.1 %collective-permute-start.1 = (f32[8,64,128]{2,1,0:T(8,128)}, f32[8,64,128]{2,1,0:T(8,128)S(1)}, u32[]{:S(2)}, u32[]{:S(2)}) collective-permute-start(f32[8,64,128]{2,1,0:T(8,128)} %get-tuple-element.17), channel_id=1, source_target_pairs={{1,2},{2,1},{3,4},{4,3},{5,6},{6,5},{7,8},{8,7},{9,10},{10,9},{11,... | collective-permute-start | bytes 786440 | tf_op jit(solution)/shard_map/ppermute | solution.py:525
  5.8 27.3 %collective-permute-start.2 = (f32[12,64,128]{2,1,0:T(8,128)}, f32[12,64,128]{2,1,0:T(8,128)S(1)}, u32[]{:S(2)}, u32[]{:S(2)}) collective-permute-start(f32[12,64,128]{2,1,0:T(8,128)} %get-tuple-element.20), channel_id=1, source_target_pairs={{1,2},{2,1},{3,4},{4,3},{5,6},{6,5},{7,8},{8,7},{9,10},{10,9},{11,... | collective-permute-start | bytes 1179656 | tf_op jit(solution)/shard_map/ppermute | solution.py:525
  6.7 3.8 %collective-permute-start.3 = (f32[4,64,128]{2,1,0:T(8,128)S(1)}, f32[4,64,128]{2,1,0:T(8,128)S(1)}, u32[]{:S(2)}, u32[]{:S(2)}) collective-permute-start(f32[4,64,128]{2,1,0:T(8,128)S(1)} %collective-permute-done.other), channel_id=1, source_target_pairs={{0,1},{1,0},{2,3},{3,2},{4,5},{5,4},{6,7},{7,6},{8,9},{9,8},{10,11... | collective-permute-start | bytes 393224 | tf_op jit(solution)/shard_map/ppermute | solution.py:525
  8.4 1.2 %copy-start.3 = (f32[4,64,128]{2,1,0:T(8,128)S(1)}, f32[4,64,128]{2,1,0:T(8,128)}, u32[]{:S(2)}) copy-start(f32[4,64,128]{2,1,0:T(8,128)} %model.5) | copy-start | bytes 393220
  10.5 6.6 %copy-start.1 = (bf16[8,4,64,128]{3,2,1,0:T(8,128)(2,1)S(1)}, bf16[8,4,64,128]{3,2,1,0:T(8,128)(2,1)}, u32[]{:S(2)}) copy-start(bf16[8,4,64,128]{3,2,1,0:T(8,128)(2,1)} %warm.5) | copy-start | bytes 1572868
  11.1 13.8 %collective-permute-start.4 = (f32[4,64,128]{2,1,0:T(8,128)S(1)}, f32[4,64,128]{2,1,0:T(8,128)S(1)}, u32[]{:S(2)}, u32[]{:S(2)}) collective-permute-start(f32[4,64,128]{2,1,0:T(8,128)S(1)} %get-tuple-element.24), channel_id=1, source_target_pairs={{0,4},{1,5},{2,6},{3,7},{4,0},{5,1},{6,2},{7,3},{8,12},{9,13},{10,... | collective-permute-start | bytes 393224 | tf_op jit(solution)/shard_map/ppermute | solution.py:525
  11.7 13.3 %collective-permute-start.5 = (f32[4,64,128]{2,1,0:T(8,128)S(1)}, f32[4,64,128]{2,1,0:T(8,128)S(1)}, u32[]{:S(2)}, u32[]{:S(2)}) collective-permute-start(f32[4,64,128]{2,1,0:T(8,128)S(1)} %get-tuple-element.25), channel_id=1, source_target_pairs={{0,8},{1,9},{2,10},{3,11},{4,12},{5,13},{6,14},{7,15},{8,0},{9,1},... | collective-permute-start | bytes 393224 | tf_op jit(solution)/shard_map/ppermute | solution.py:525
  14.3 18.9 %collective-permute-start.6 = (f32[4,64,128]{2,1,0:T(8,128)S(1)}, f32[4,64,128]{2,1,0:T(8,128)S(1)}, u32[]{:S(2)}, u32[]{:S(2)}) collective-permute-start(f32[4,64,128]{2,1,0:T(8,128)S(1)} %get-tuple-element.26), channel_id=1, source_target_pairs={{0,12},{1,13},{2,14},{3,15},{4,8},{5,9},{6,10},{7,11},{8,4},{9,5},... | collective-permute-start | bytes 393224 | tf_op jit(solution)/shard_map/ppermute | solution.py:525
  17.2 16.0 %copy-start.2 = (bf16[8,4,64,128]{3,2,1,0:T(8,128)(2,1)S(1)}, bf16[8,4,64,128]{3,2,1,0:T(8,128)(2,1)}, u32[]{:S(2)}) copy-start(bf16[8,4,64,128]{3,2,1,0:T(8,128)(2,1)} %forward.7) | copy-start | bytes 1572868
  21.3 16.1 %collective-permute-start.7 = (f32[8,64,128]{2,1,0:T(8,128)S(1)}, f32[8,64,128]{2,1,0:T(8,128)S(1)}, u32[]{:S(2)}, u32[]{:S(2)}) collective-permute-start(f32[8,64,128]{2,1,0:T(8,128)S(1)} %get-tuple-element.21.sent_first), channel_id=1, source_target_pairs={{1,2},{2,1},{3,4},{4,3},{5,6},{6,5},{7,8},{8,7},{9,10},{10,9},{11,... | collective-permute-start | bytes 786440 | tf_op jit(solution)/shard_map/ppermute | solution.py:525
  37.4 9.4 %collective-permute-start.8 = (f32[9,64,128]{2,1,0:T(8,128)S(1)}, f32[9,64,128]{2,1,0:T(8,128)S(1)}, u32[]{:S(2)}, u32[]{:S(2)}) collective-permute-start(f32[9,64,128]{2,1,0:T(8,128)S(1)} %get-tuple-element.29.sent), channel_id=1, source_target_pairs={{1,2},{2,1},{3,4},{4,3},{5,6},{6,5},{7,8},{8,7},{9,10},{10,9},{11,... | collective-permute-start | bytes 884744 | tf_op jit(solution)/shard_map/ppermute | solution.py:525

commit v3 on v2

--- a/solution.py
+++ b/solution.py
@@ -196,38 +196,23 @@
     return (field - after(field, axis)) * (other - after(other, axis))
 
 
-def pack(info, warm, forward, first, second, held, edges, sems):
-    tile = info[0]
-    half, layers = held.shape[:2]
-    count = half // 2
-    theirs = half * (1 - tile)
-    face = (layers - 1) * (1 - tile)
-    copies = [
-        pltpu.make_async_copy(warm.at[pl.ds(theirs, count)], held.at[:count], sems.at[0]),
-        pltpu.make_async_copy(warm.at[pl.ds(theirs + count, count)], held.at[count:], sems.at[1]),
-        pltpu.make_async_copy(forward.at[pl.ds(theirs, half), pl.ds(face, 1)], edges, sems.at[2]),
-    ]
-    for copy in copies:
-        copy.start()
-    copies[0].wait()
-    for q in range(count):
-        first[layers * q : layers * (q + 1)] = held[q].astype(jnp.float32)
-    copies[1].wait()
-    for q in range(count):
-        second[layers * q : layers * (q + 1)] = held[count + q].astype(jnp.float32)
-    copies[2].wait()
-    for q in range(half):
-        second[count * layers + q] = edges[q, 0].astype(jnp.float32)
-
-
-def inject(info, order, residual, electrodes, out, weights):
-    tile = info[0]
+def tile_of(position):
+    return (position + 1) & 1
+
+
+def survey_of(position):
+    return ((position + 1) >> 1) & (SURVEYS - 1)
+
+
+def inject(order, residual, electrodes, out, weights):
+    position = lax.axis_index("space")
+    tile = tile_of(position)
     surveys = order.shape[0]
     ranks = []
-    for k in range(6):
+    for place in [position, position ^ 1] + [position ^ (4 * k) for k in range(4)]:
         found = 0
         for i in range(surveys):
-            found = found + jnp.where(order[i] == info[1 + k], i, 0)
+            found = found + jnp.where(order[i] == survey_of(place), i, 0)
         ranks.append(found)
     for k in range(4):
         a = ranks[2 + k]
@@ -247,7 +232,7 @@
     at_row = lax.broadcasted_iota(jnp.int32, (rows, count), 0) == row
     at_row = jnp.where(at_row, 1.0, 0.0).astype(jnp.bfloat16)
     at_lane = lax.broadcasted_iota(jnp.int32, (rows_z, count), 0) == lane
-    mine = residual[info[1]]
+    mine = residual[survey_of(position)]
     mine = jnp.where(tile == 0, mine[:half], mine[half:])
     total = None
     for _ in range(3):
@@ -264,9 +249,16 @@
         out[q] = total[:, q * rows_z : (q + 1) * rows_z].reshape(out.shape[1:])
 
 
-def find_coefs(info, model, other, coefs, sigma):
-    tile = info[0]
-    layers = model.shape[0]
+def prepare(model, other, warm, forward, coefs, second, sigma):
+    tile = tile_of(lax.axis_index("space"))
+    half = warm.shape[0] // 2
+    count, layers = half // 2, model.shape[0]
+    theirs = half * (1 - tile)
+    face = (layers - 1) * (1 - tile)
+    for q in range(count):
+        second[layers * q : layers * (q + 1)] = warm[theirs + count + q].astype(jnp.float32)
+    for q in range(half):
+        second[count * layers + q] = forward[theirs + q, face].astype(jnp.float32)
     full = 2 * layers
     shape = model.shape[1:]
     for i in range(layers):
@@ -315,7 +307,7 @@
             lam[q, i] = here + step
         return carry
 
-    lax.fori_loop(0, full, first, 0)
+    lax.fori_loop(0, full, first, 0, unroll=full)
     for index, (keep, gain) in enumerate(weights()):
         source, target = mine.at[index % 2], mine.at[1 - index % 2]
         last = index == ITERS - 2
@@ -333,7 +325,7 @@
                 lam[q, i] = lam[q, i] + step
             return carry
 
-        lax.fori_loop(0, full, later, 0)
+        lax.fori_loop(0, full, later, 0, unroll=full)
 
 
 def load_start(warm, source, got, start):
@@ -341,26 +333,29 @@
     layers = full // 2
     for q in range(count):
         start[q, :layers] = warm[source + q].astype(jnp.float32)
-        start[q, layers:] = got[layers * q : layers * (q + 1)]
-
-
-def solve_first(info, coefs, got, warm, rhs, own, sent, start, rest, lam, mine):
+        start[q, layers:] = got[q] if len(got.shape) == 4 else got[layers * q : layers * (q + 1)]
+
+
+def solve_first(coefs, got, warm, rhs, other, own, sent, relay, start, rest, lam, mine):
     count, layers = own.shape[:2]
-    load_start(warm, 2 * count * info[0], got, start)
+    relay[...] = other[...]
+    load_start(warm, 2 * count * tile_of(lax.axis_index("space")), got, start)
     sweeps(coefs, rhs, 0, start, rest, lam, mine)
     for q in range(count):
         own[q] = lam[q, :layers]
         sent[layers * q : layers * (q + 1)] = lam[q, layers:]
 
 
-def solve_second(info, coefs, got, warm, rhs, forward, own_first, sent_first, times, near_a, near_b, near_c, own, sent, time, start, rest, lam, mine):
+def solve_second(weights, model, beside, coefs, got, warm, rhs, forward, own_first, sent_first, own, sent, times, part_a, part_b, part_c, start, rest, lam, mine):
     count, layers = own.shape[:2]
-    time[...] = (times[...] + near_a[...]) + (near_b[...] + near_c[...])
-    source = 2 * count * info[0]
+    tile = tile_of(lax.axis_index("space"))
+    for k, out in enumerate((times, part_a, part_b, part_c)):
+        out[...] = weights[2 * k] * model[...] + weights[2 * k + 1] * beside[...]
+    source = 2 * count * tile
     load_start(warm, source + count, got, start)
     sweeps(coefs, rhs, count, start, rest, lam, mine)
-    near = (layers - 1) * (1 - info[0])
-    far = (layers - 1) * info[0]
+    near = (layers - 1) * (1 - tile)
+    far = (layers - 1) * tile
     total = None
     for q in range(2 * count):
         slope = forward[source + q, near].astype(jnp.float32) - got[count * layers + q]
@@ -394,9 +389,9 @@
         mass[i] = mass[i] + totals[3]
 
 
-def gather_terms(info, forward, own_first, own_second, back, sums, adjoint, rounded, sems):
+def gather_terms(forward, own_first, own_second, back, sums, adjoint, rounded, sems):
     count, layers = own_first.shape[:2]
-    tile = info[0]
+    tile = tile_of(lax.axis_index("space"))
     mine, theirs = 2 * count * tile, 2 * count * (1 - tile)
     for q in range(count):
         rounded[q] = own_first[q].astype(jnp.bfloat16)
@@ -420,8 +415,8 @@
         copy.wait()
 
 
-def finish(info, sums, back, sent, forward, model, other, times, kept, adjoint, gradient, rounded, result, sems):
-    tile = info[0]
+def finish(sums, back, sent, forward, model, other, times, near_a, near_b, near_c, kept, adjoint, gradient, rounded, result, sems):
+    tile = tile_of(lax.axis_index("space"))
     count, layers = rounded.shape[:2]
     theirs = 2 * count * (1 - tile) + count
     for q in range(count):
@@ -466,16 +461,12 @@
         fall_y = jnp.where(in_y, value - after(value, 0), 0.0)
         fall_z = jnp.where(in_z, value - after(value, 1), 0.0)
         space = falls[i + 1] - falls[i] + (fall_y - before(fall_y, 0)) + (fall_z - before(fall_z, 1))
-        result[i] = space + times[i] - jnp.exp(value) * (0.5 * terms + GROUND * mass)
+        time = (times[i] + near_a[i]) + (near_b[i] + near_c[i])
+        result[i] = space + time - jnp.exp(value) * (0.5 * terms + GROUND * mass)
         copies.append(pltpu.make_async_copy(result.at[i], gradient.at[i], sems.at[i]))
         copies[-1].start()
     for copy in copies:
         copy.wait()
-
-
-def time_parts(weights, model, beside, times, part_a, part_b, part_c):
-    for k, out in enumerate((times, part_a, part_b, part_c)):
-        out[...] = weights[2 * k] * model[...] + weights[2 * k + 1] * beside[...]
 
 
 V, S, H = pltpu.VMEM, pltpu.SMEM, pltpu.HBM
@@ -513,9 +504,6 @@
     full = 2 * layers
     devices = lax.axis_size("space")
     position = lax.axis_index("space")
-    places = [position, position ^ 1] + [position ^ (4 * k) for k in range(4)]
-    tile = (position + 1) & 1
-    info = jnp.stack([tile] + [((p + 1) >> 1) & (SURVEYS - 1) for p in places]).astype(jnp.int32)
     pairs = []
     for p in range(1, devices, 2):
         pairs += [(p, (p + 1) % devices), ((p + 1) % devices, p)]
@@ -527,60 +515,50 @@
     dma = pltpu.SemaphoreType.DMA
     slab = (layers, ny, nz)
     other = swap(model)
-    first, second = call(
-        pack,
-        (info, warm_start, forward),
-        (S, H, H),
-        [f32(count * layers, ny, nz), f32(count * layers + half, ny, nz)],
-        scratch=[V((half, *slab), jnp.bfloat16), V((half, 1, ny, nz), jnp.bfloat16), dma((3,))],
-        room=60,
-    )
-    got_first = swap(first)
-    got_second = swap(second)
+    first = lax.dynamic_slice_in_dim(warm_start, half * (1 - tile_of(position)), count, 0)
+    got_first = swap(first.astype(jnp.float32))
     rhs, weights_time = call(
         inject,
-        (info, survey_order, residual_data, electrodes.reshape(1, -1)),
-        (S, S, V, V),
+        (survey_order, residual_data, electrodes.reshape(1, -1)),
+        (S, V, V),
         [f32(half, full, ny, nz), f32(8)],
         [V, S],
     )
-    beside = swap(other, 1)
-    coefs = call(
-        find_coefs,
-        (info, model, other),
-        (S, V, V),
-        [f32(7, full, ny, nz)],
+    coefs, second = call(
+        prepare,
+        (model, other, warm_start, forward),
+        (V, V, V, V),
+        [f32(7, full, ny, nz), f32(count * layers + half, ny, nz)],
         scratch=[V((full, ny, nz), jnp.float32)],
     )
-    times, part_a, part_b, part_c = call(
-        time_parts, (weights_time, model, beside), (S, V, V), [f32(*slab)] * 4
-    )
-    near = [swap(part, 4 * (k + 1)) for k, part in enumerate((part_a, part_b, part_c))]
+    got_second = swap(second)
     field = V((count, full, ny, nz), jnp.float32)
     fields = [field, field, field, V((2, count, full, ny, nz), jnp.float32)]
     block = f32(count, *slab)
-    own_first, sent_first = call(
+    own_first, sent_first, relay = call(
         solve_first,
-        (info, coefs, got_first, warm_start, rhs),
-        (S, V, V, V, V),
-        [block, f32(count * layers, ny, nz)],
+        (coefs, got_first, warm_start, rhs, other),
+        (V, V, V, V, V),
+        [block, f32(count * layers, ny, nz), f32(*slab)],
         scratch=fields,
-        micros=4,
+        micros=3,
     )
     back_first = swap(sent_first)
-    own_second, sent_second, time = call(
+    beside = swap(relay, 1)
+    own_second, sent_second, times, *parts = call(
         solve_second,
-        (info, coefs, got_second, warm_start, rhs, forward, own_first, sent_first, times, *near),
-        (S, V, V, V, V, V, V, V, V, V, V, V),
-        [block, f32(count * layers + 1, ny, nz), f32(*slab)],
+        (weights_time, model, beside, coefs, got_second, warm_start, rhs, forward, own_first, sent_first),
+        (S, V, V, V, V, V, V, V, V, V),
+        [block, f32(count * layers + 1, ny, nz)] + [f32(*slab)] * 4,
         scratch=fields,
-        micros=4,
+        micros=3,
     )
     back_second = swap(sent_second)
+    near = [swap(part, 4 * (k + 1)) for k, part in enumerate(parts)]
     sums, kept = call(
         gather_terms,
-        (info, forward, own_first, own_second, back_first),
-        (S, V, V, V, V),
+        (forward, own_first, own_second, back_first),
+        (V, V, V, V),
         [f32(4, *slab), bf16(*forward.shape)],
         [V, H],
         scratch=[V((3 * count, *slab), jnp.bfloat16), dma((2,))],
@@ -588,12 +566,12 @@
     )
     adjoint, gradient = call(
         finish,
-        (info, sums, back_second, sent_second, forward, model, other, time, kept),
-        (S, V, V, V, V, V, V, V, H),
+        (sums, back_second, sent_second, forward, model, other, times, *near, kept),
+        (V, V, V, V, V, V, V, V, V, V, H),
         [bf16(*forward.shape), f32(*slab)],
         [H, H],
         scratch=[V((count, *slab), jnp.bfloat16), V(slab, jnp.float32), dma((layers + 1,))],
-        aliases={8: 0},
+        aliases={10: 0},
     )
     return adjoint, gradient
 

time: 48.6 us -> 46.3 us (0.953)
  the two profiles are of different devices: /device:TPU:12 before, /device:TPU:17 now
where the time goes in v3:
time: 46.3 us; the launch traced here: 46.1 us
  waiting for transfers between devices  25.7 us (56%)
  Pallas kernels  8.42 us (18%)
  starting transfers between devices  8.17 us (18%)
  local copies, waits for them, and re-layouts  2.18 us (5%)
  other arithmetic  0.93 us (2%)
  between operations  0.7 us (2%)
    ppermute x9, waiting for transfers between devices, swap(): return lax.ppermute(x, 'space', links)  25.7 us
    pallas_call x6, Pallas kernels, call(): pl.pallas_call(kernel, out_shape=out_shapes if several else out_shapes[0]...  8.42 us
    ppermute x9, starting transfers between devices, swap(): return lax.ppermute(x, 'space', links)  8.17 us
    unnamed x12, local copies, waits for them, and re-layouts  2.18 us
    convert_element_type x1, other arithmetic, paired(): got_first = swap(first.astype(jnp.float32))  0.93 us
  transfers between devices with their start and end apart: 9, of which 6 were waited for; matrix products, arithmetic and copies ran while one was open for 0% of the time, Pallas kernels for 16%

profile of v3, /device:TPU:17, one launch (start us, length us, event | category | flops | bytes accessed | tf_op | source)
XLA Modules:
  0.0 46.1 jit_solution(7279311595903948742)
XLA Ops:
  0.6 0.9 %dynamic-slice_convert_fusion = f32[2,4,64,128]{3,2,1,0:T(8,128)S(1)} fusion(bf16[8,4,64,128]{3,2,1,0:T(8,128)(2,1)} %warm.5, s32[]{:T(128)S(6)} %select_n.3), kind=kLoop, calls=%fused_computation | loop fusion | flops 65536 | bytes 393220 | tf_op jit(solution)/shard_map/convert_element_type | solution.py:519
  1.6 1.9 %collective-permute-start.1 = (f32[2,4,64,128]{3,2,1,0:T(8,128)S(1)}, f32[2,4,64,128]{3,2,1,0:T(8,128)S(1)}, u32[]{:S(2)}, u32[]{:S(2)}) collective-permute-start(f32[2,4,64,128]{3,2,1,0:T(8,128)S(1)} %dynamic-slice_convert_fusion), channel_id=1, source_target_pairs={{1,2},{2,1},{3,4},{4,3},{5,6},{6,5},{7,8},{8,7},{9,10},{10,9},{11,... | collective-permute-start | bytes 786440 | tf_op jit(solution)/shard_map/ppermute | solution.py:513
  3.4 0.1 collective-permute-start
  3.5 0.0 copy-start.3
  3.5 0.8 %copy-done.3 = f32[8,8,256]{2,1,0:T(8,128)S(1)} copy-done((f32[8,8,256]{2,1,0:T(8,128)S(1)}, f32[8,8,256]{2,1,0:T(8,128)}, u32[]{:S(2)}) %copy-start.3) | copy-done | bytes 65560
  4.3 0.0 copy-start.4
  4.4 0.7 %copy-done.4 = s32[256]{0:T(256)S(1)} copy-done((s32[256]{0:T(256)S(1)}, s32[256]{0:T(256)}, u32[]{:S(2)}) %copy-start.4) | copy-done | bytes 1048
  5.0 0.0 copy-start.5
  5.0 0.7 %copy-done.5 = s32[8]{0:T(128)S(1)} copy-done((s32[8]{0:T(128)S(1)}, s32[8]{0:T(128)}, u32[]{:S(2)}) %copy-start.5) | copy-done | bytes 56
  5.7 0.0 copy-start
  5.7 0.0 copy-start.1
  5.7 0.0 copy-start.2
  5.7 1.2 %shard_map.78 = (f32[4,8,64,128]{3,2,1,0:T(8,128)S(1)}, f32[8]{0:T(128)S(1)}) custom-call(s32[8]{0:T(128)S(1)} %copy-done.5, f32[8,8,256]{2,1,0:T(8,128)S(1)} %copy-done.3, s32[1,256]{1,0:T(1,128)S(1)} %bitcast.1), custom_call_target="tpu_custom_call" | custom-call | flops 1000000000 | bytes 3000000 | tf_op jit(solution)/shard_map/pallas_call | solution.py:479
  6.9 6.2 %collective-permute-done.other = f32[4,64,128]{2,1,0:T(8,128)S(1)} collective-permute-done((f32[4,64,128]{2,1,0:T(8,128)}, f32[4,64,128]{2,1,0:T(8,128)S(1)}, u32[]{:S(2)}, u32[]{:S(2)}) %collective-permute-start) | collective-permute-done | bytes 131104 | tf_op jit(solution)/shard_map/ppermute | solution.py:513
  13.1 0.0 copy-done
  13.1 0.0 copy-done.1
  13.1 0.0 copy-done.2
  13.1 0.3 shard_map.77
  13.5 1.8 %collective-permute-start.3 = (f32[12,64,128]{2,1,0:T(8,128)S(1)}, f32[12,64,128]{2,1,0:T(8,128)S(1)}, u32[]{:S(2)}, u32[]{:S(2)}) collective-permute-start(f32[12,64,128]{2,1,0:T(8,128)S(1)} %get-tuple-element.22), channel_id=1, source_target_pairs={{1,2},{2,1},{3,4},{4,3},{5,6},{6,5},{7,8},{8,7},{9,10},{10,9},{11,... | collective-permute-start | bytes 1179656 | tf_op jit(solution)/shard_map/ppermute | solution.py:513
  15.3 0.0 collective-permute-done.1.got
  15.3 1.8 %shard_map.79 = (f32[2,4,64,128]{3,2,1,0:T(8,128)S(1)}, f32[8,64,128]{2,1,0:T(8,128)S(1)}, f32[4,64,128]{2,1,0:T(8,128)S(1)}) custom-call(f32[7,8,64,128]{3,2,1,0:T(8,128)S(1)} %get-tuple-element.17.coefs, f32[2,4,64,128]{3,2,1,0:T(8,128)S(1)} %collective-permute-done.1.got, bf16[8,4,64,128]{3,2,1,0:T(8,128)(2,1)S(1)} %copy-done, ...), custom_call_target="tpu_custom_call" | custom-call | flops 3000000000 | bytes 9000000 | tf_op jit(solution)/shard_map/pallas_call | solution.py:479
  17.1 0.1 collective-permute-start.2
  17.2 0.1 collective-permute-start.4
  17.3 1.2 %collective-permute-done.2.beside = f32[4,64,128]{2,1,0:T(8,128)S(1)} collective-permute-done((f32[4,64,128]{2,1,0:T(8,128)S(1)}, f32[4,64,128]{2,1,0:T(8,128)S(1)}, u32[]{:S(2)}, u32[]{:S(2)}) %collective-permute-start.2) | collective-permute-done | bytes 131104 | tf_op jit(solution)/shard_map/ppermute | solution.py:513
  18.5 10.3 %collective-permute-done.3.got = f32[12,64,128]{2,1,0:T(8,128)S(1)} collective-permute-done((f32[12,64,128]{2,1,0:T(8,128)S(1)}, f32[12,64,128]{2,1,0:T(8,128)S(1)}, u32[]{:S(2)}, u32[]{:S(2)}) %collective-permute-start.3) | collective-permute-done | bytes 393248 | tf_op jit(solution)/shard_map/ppermute | solution.py:513
  28.8 2.5 %shard_map.80 = (f32[2,4,64,128]{3,2,1,0:T(8,128)S(1)}, f32[9,64,128]{2,1,0:T(8,128)S(1)}, f32[4,64,128]{2,1,0:T(8,128)S(1)}, f32[4,64,128]{2,1,0:T(8,128)S(1)},...) custom-call(f32[8]{0:T(128)S(1)} %get-tuple-element.20.weights, f32[4,64,128]{2,1,0:T(8,128)S(1)} %copy-done.2, ...), custom_call_target="tpu_custom_call" | custom-call | flops 3000000000 | bytes 9000000 | tf_op jit(solution)/shard_map/pallas_call | solution.py:479
  31.3 1.6 %collective-permute-start.5 = (f32[9,64,128]{2,1,0:T(8,128)S(1)}, f32[9,64,128]{2,1,0:T(8,128)S(1)}, u32[]{:S(2)}, u32[]{:S(2)}) collective-permute-start(f32[9,64,128]{2,1,0:T(8,128)S(1)} %get-tuple-element.26.sent), channel_id=1, source_target_pairs={{1,2},{2,1},{3,4},{4,3},{5,6},{6,5},{7,8},{8,7},{9,10},{10,9},{11,... | collective-permute-start | bytes 884744 | tf_op jit(solution)/shard_map/ppermute | solution.py:513
  32.9 0.4 collective-permute-start.6
  33.4 0.9 %collective-permute-start.7 = (f32[4,64,128]{2,1,0:T(8,128)S(1)}, f32[4,64,128]{2,1,0:T(8,128)S(1)}, u32[]{:S(2)}, u32[]{:S(2)}) collective-permute-start(f32[4,64,128]{2,1,0:T(8,128)S(1)} %get-tuple-element.29), channel_id=1, source_target_pairs={{0,8},{1,9},{2,10},{3,11},{4,12},{5,13},{6,14},{7,15},{8,0},{9,1},... | collective-permute-start | bytes 393224 | tf_op jit(solution)/shard_map/ppermute | solution.py:513
  34.3 1.3 %collective-permute-start.8 = (f32[4,64,128]{2,1,0:T(8,128)S(1)}, f32[4,64,128]{2,1,0:T(8,128)S(1)}, u32[]{:S(2)}, u32[]{:S(2)}) collective-permute-start(f32[4,64,128]{2,1,0:T(8,128)S(1)} %get-tuple-element.30), channel_id=1, source_target_pairs={{0,12},{1,13},{2,14},{3,15},{4,8},{5,9},{6,10},{7,11},{8,4},{9,5},... | collective-permute-start | bytes 393224 | tf_op jit(solution)/shard_map/ppermute | solution.py:513
  35.6 0.0 collective-permute-done.4.back
  35.6 1.3 %shard_map.81 = (f32[4,4,64,128]{3,2,1,0:T(8,128)S(1)}, bf16[8,4,64,128]{3,2,1,0:T(8,128)(2,1)}) custom-call(bf16[8,4,64,128]{3,2,1,0:T(8,128)(2,1)S(1)} %copy-done.1, f32[2,4,64,128]{3,2,1,0:T(8,128)S(1)} %get-tuple-element.19.own_first, f32[2,4,64,128]{3,2,1,0:T(8,128)S(1)} %get-tuple-element.24.own_second, f32[8,64,128]{2,1,0:T(8,128)S(1)} %collective-permute-done.4.back), custom_call_target="tpu_custom_call" | custom-call | flops 2000000000 | bytes 6000000 | tf_op jit(solution)/shard_map/pallas_call | solution.py:479
  36.9 0.1 collective-permute-done.6.near_a
  37.1 3.6 %collective-permute-done.7.near_b = f32[4,64,128]{2,1,0:T(8,128)S(1)} collective-permute-done((f32[4,64,128]{2,1,0:T(8,128)S(1)}, f32[4,64,128]{2,1,0:T(8,128)S(1)}, u32[]{:S(2)}, u32[]{:S(2)}) %collective-permute-start.7) | collective-permute-done | bytes 131104 | tf_op jit(solution)/shard_map/ppermute | solution.py:513
  40.7 4.2 %collective-permute-done.8.near_c = f32[4,64,128]{2,1,0:T(8,128)S(1)} collective-permute-done((f32[4,64,128]{2,1,0:T(8,128)S(1)}, f32[4,64,128]{2,1,0:T(8,128)S(1)}, u32[]{:S(2)}, u32[]{:S(2)}) %collective-permute-start.8) | collective-permute-done | bytes 131104 | tf_op jit(solution)/shard_map/ppermute | solution.py:513
  44.9 0.0 collective-permute-done.5.back
  44.9 1.2 %shard_map.82 = (bf16[8,4,64,128]{3,2,1,0:T(8,128)(2,1)}, f32[4,64,128]{2,1,0:T(8,128)}) custom-call(f32[4,4,64,128]{3,2,1,0:T(8,128)S(1)} %get-tuple-element.25.sums, f32[9,64,128]{2,1,0:T(8,128)S(1)} %collective-permute-done.5.back, f32[9,64,128]{2,1,0:T(8,128)S(1)} %get-tuple-element.26.sent, ...), custom_call_target="tpu_custom_call", output_to_operand_aliasing={{0}: (10, {})} | custom-call | flops 1000000000 | bytes 3000000 | tf_op jit(solution)/shard_map/pallas_call | solution.py:479
Async XLA Ops:
  1.6 13.7 %collective-permute-start.1 = (f32[2,4,64,128]{3,2,1,0:T(8,128)S(1)}, f32[2,4,64,128]{3,2,1,0:T(8,128)S(1)}, u32[]{:S(2)}, u32[]{:S(2)}) collective-permute-start(f32[2,4,64,128]{3,2,1,0:T(8,128)S(1)} %dynamic-slice_convert_fusion), channel_id=1, source_target_pairs={{1,2},{2,1},{3,4},{4,3},{5,6},{6,5},{7,8},{8,7},{9,10},{10,9},{11,... | collective-permute-start | bytes 786440 | tf_op jit(solution)/shard_map/ppermute | solution.py:513
  3.4 9.7 %collective-permute-start = (f32[4,64,128]{2,1,0:T(8,128)}, f32[4,64,128]{2,1,0:T(8,128)S(1)}, u32[]{:S(2)}, u32[]{:S(2)}) collective-permute-start(f32[4,64,128]{2,1,0:T(8,128)} %model.5), channel_id=1, source_target_pairs={{1,2},{2,1},{3,4},{4,3},{5,6},{6,5},{7,8},{8,7},{9,10},{10,9},{11,... | collective-permute-start | bytes 393224 | tf_op jit(solution)/shard_map/ppermute | solution.py:513
  3.5 0.8 %copy-start.3 = (f32[8,8,256]{2,1,0:T(8,128)S(1)}, f32[8,8,256]{2,1,0:T(8,128)}, u32[]{:S(2)}) copy-start(f32[8,8,256]{2,1,0:T(8,128)} %residual.1) | copy-start | bytes 196612
  4.3 0.7 %copy-start.4 = (s32[256]{0:T(256)S(1)}, s32[256]{0:T(256)}, u32[]{:S(2)}) copy-start(s32[256]{0:T(256)} %param.10) | copy-start | bytes 3076
  5.0 0.7 %copy-start.5 = (s32[8]{0:T(128)S(1)}, s32[8]{0:T(128)}, u32[]{:S(2)}) copy-start(s32[8]{0:T(128)} %order.1) | copy-start | bytes 100
  5.7 7.4 %copy-start = (bf16[8,4,64,128]{3,2,1,0:T(8,128)(2,1)S(1)}, bf16[8,4,64,128]{3,2,1,0:T(8,128)(2,1)}, u32[]{:S(2)}) copy-start(bf16[8,4,64,128]{3,2,1,0:T(8,128)(2,1)} %warm.5) | copy-start | bytes 1572868
  5.7 7.4 %copy-start.1 = (bf16[8,4,64,128]{3,2,1,0:T(8,128)(2,1)S(1)}, bf16[8,4,64,128]{3,2,1,0:T(8,128)(2,1)}, u32[]{:S(2)}) copy-start(bf16[8,4,64,128]{3,2,1,0:T(8,128)(2,1)} %forward.7) | copy-start | bytes 1572868
  5.7 7.4 %copy-start.2 = (f32[4,64,128]{2,1,0:T(8,128)S(1)}, f32[4,64,128]{2,1,0:T(8,128)}, u32[]{:S(2)}) copy-start(f32[4,64,128]{2,1,0:T(8,128)} %model.5) | copy-start | bytes 393220
  13.5 15.4 %collective-permute-start.3 = (f32[12,64,128]{2,1,0:T(8,128)S(1)}, f32[12,64,128]{2,1,0:T(8,128)S(1)}, u32[]{:S(2)}, u32[]{:S(2)}) collective-permute-start(f32[12,64,128]{2,1,0:T(8,128)S(1)} %get-tuple-element.22), channel_id=1, source_target_pairs={{1,2},{2,1},{3,4},{4,3},{5,6},{6,5},{7,8},{8,7},{9,10},{10,9},{11,... | collective-permute-start | bytes 1179656 | tf_op jit(solution)/shard_map/ppermute | solution.py:513
  17.1 1.4 %collective-permute-start.2 = (f32[4,64,128]{2,1,0:T(8,128)S(1)}, f32[4,64,128]{2,1,0:T(8,128)S(1)}, u32[]{:S(2)}, u32[]{:S(2)}) collective-permute-start(f32[4,64,128]{2,1,0:T(8,128)S(1)} %get-tuple-element.21), channel_id=1, source_target_pairs={{0,1},{1,0},{2,3},{3,2},{4,5},{5,4},{6,7},{7,6},{8,9},{9,8},{10,11... | collective-permute-start | bytes 393224 | tf_op jit(solution)/shard_map/ppermute | solution.py:513
  17.2 18.4 %collective-permute-start.4 = (f32[8,64,128]{2,1,0:T(8,128)S(1)}, f32[8,64,128]{2,1,0:T(8,128)S(1)}, u32[]{:S(2)}, u32[]{:S(2)}) collective-permute-start(f32[8,64,128]{2,1,0:T(8,128)S(1)} %get-tuple-element.23.sent_first), channel_id=1, source_target_pairs={{1,2},{2,1},{3,4},{4,3},{5,6},{6,5},{7,8},{8,7},{9,10},{10,9},{11,... | collective-permute-start | bytes 786440 | tf_op jit(solution)/shard_map/ppermute | solution.py:513
  31.3 13.6 %collective-permute-start.5 = (f32[9,64,128]{2,1,0:T(8,128)S(1)}, f32[9,64,128]{2,1,0:T(8,128)S(1)}, u32[]{:S(2)}, u32[]{:S(2)}) collective-permute-start(f32[9,64,128]{2,1,0:T(8,128)S(1)} %get-tuple-element.26.sent), channel_id=1, source_target_pairs={{1,2},{2,1},{3,4},{4,3},{5,6},{6,5},{7,8},{8,7},{9,10},{10,9},{11,... | collective-permute-start | bytes 884744 | tf_op jit(solution)/shard_map/ppermute | solution.py:513
  32.9 4.1 %collective-permute-start.6 = (f32[4,64,128]{2,1,0:T(8,128)S(1)}, f32[4,64,128]{2,1,0:T(8,128)S(1)}, u32[]{:S(2)}, u32[]{:S(2)}) collective-permute-start(f32[4,64,128]{2,1,0:T(8,128)S(1)} %get-tuple-element.28), channel_id=1, source_target_pairs={{0,4},{1,5},{2,6},{3,7},{4,0},{5,1},{6,2},{7,3},{8,12},{9,13},{10,... | collective-permute-start | bytes 393224 | tf_op jit(solution)/shard_map/ppermute | solution.py:513
  33.4 7.3 %collective-permute-start.7 = (f32[4,64,128]{2,1,0:T(8,128)S(1)}, f32[4,64,128]{2,1,0:T(8,128)S(1)}, u32[]{:S(2)}, u32[]{:S(2)}) collective-permute-start(f32[4,64,128]{2,1,0:T(8,128)S(1)} %get-tuple-element.29), channel_id=1, source_target_pairs={{0,8},{1,9},{2,10},{3,11},{4,12},{5,13},{6,14},{7,15},{8,0},{9,1},... | collective-permute-start | bytes 393224 | tf_op jit(solution)/shard_map/ppermute | solution.py:513
  34.3 10.6 %collective-permute-start.8 = (f32[4,64,128]{2,1,0:T(8,128)S(1)}, f32[4,64,128]{2,1,0:T(8,128)S(1)}, u32[]{:S(2)}, u32[]{:S(2)}) collective-permute-start(f32[4,64,128]{2,1,0:T(8,128)S(1)} %get-tuple-element.30), channel_id=1, source_target_pairs={{0,12},{1,13},{2,14},{3,15},{4,8},{5,9},{6,10},{7,11},{8,4},{9,5},... | collective-permute-start | bytes 393224 | tf_op jit(solution)/shard_map/ppermute | solution.py:513

commit v4 on v3

--- a/solution.py
+++ b/solution.py
@@ -202,6 +202,13 @@
 
 def survey_of(position):
     return ((position + 1) >> 1) & (SURVEYS - 1)
+
+
+def pack(warm, first):
+    tile = tile_of(lax.axis_index("space"))
+    count = first.shape[0]
+    for q in range(count):
+        first[q] = warm[2 * count * (1 - tile) + q].astype(jnp.float32)
 
 
 def inject(order, residual, electrodes, out, weights):
@@ -336,9 +343,13 @@
         start[q, layers:] = got[q] if len(got.shape) == 4 else got[layers * q : layers * (q + 1)]
 
 
-def solve_first(coefs, got, warm, rhs, other, own, sent, relay, start, rest, lam, mine):
+def solve_first(weights, model, beside, coefs, got, warm, rhs, own, sent, time, opposite, parts, start, rest, lam, mine):
     count, layers = own.shape[:2]
-    relay[...] = other[...]
+    here, there = model[...], beside[...]
+    time[...] = weights[0] * here + weights[1] * there
+    parts[:layers] = weights[2] * here + weights[3] * there
+    opposite[...] = weights[4] * here + weights[5] * there
+    parts[layers:] = weights[6] * here + weights[7] * there
     load_start(warm, 2 * count * tile_of(lax.axis_index("space")), got, start)
     sweeps(coefs, rhs, 0, start, rest, lam, mine)
     for q in range(count):
@@ -346,11 +357,11 @@
         sent[layers * q : layers * (q + 1)] = lam[q, layers:]
 
 
-def solve_second(weights, model, beside, coefs, got, warm, rhs, forward, own_first, sent_first, own, sent, times, part_a, part_b, part_c, start, rest, lam, mine):
+def solve_second(time, opposite, near, coefs, got, warm, rhs, forward, own_first, sent_first, own, sent, times, joined, start, rest, lam, mine):
     count, layers = own.shape[:2]
     tile = tile_of(lax.axis_index("space"))
-    for k, out in enumerate((times, part_a, part_b, part_c)):
-        out[...] = weights[2 * k] * model[...] + weights[2 * k + 1] * beside[...]
+    times[...] = time[...] + near[:layers]
+    joined[...] = opposite[...] + near[layers:]
     source = 2 * count * tile
     load_start(warm, source + count, got, start)
     sweeps(coefs, rhs, count, start, rest, lam, mine)
@@ -415,7 +426,7 @@
         copy.wait()
 
 
-def finish(sums, back, sent, forward, model, other, times, near_a, near_b, near_c, kept, adjoint, gradient, rounded, result, sems):
+def finish(sums, back, sent, forward, model, other, times, far, kept, adjoint, gradient, rounded, result, sems):
     tile = tile_of(lax.axis_index("space"))
     count, layers = rounded.shape[:2]
     theirs = 2 * count * (1 - tile) + count
@@ -461,8 +472,7 @@
         fall_y = jnp.where(in_y, value - after(value, 0), 0.0)
         fall_z = jnp.where(in_z, value - after(value, 1), 0.0)
         space = falls[i + 1] - falls[i] + (fall_y - before(fall_y, 0)) + (fall_z - before(fall_z, 1))
-        time = (times[i] + near_a[i]) + (near_b[i] + near_c[i])
-        result[i] = space + time - jnp.exp(value) * (0.5 * terms + GROUND * mass)
+        result[i] = space + (times[i] + far[i]) - jnp.exp(value) * (0.5 * terms + GROUND * mass)
         copies.append(pltpu.make_async_copy(result.at[i], gradient.at[i], sems.at[i]))
         copies[-1].start()
     for copy in copies:
@@ -503,7 +513,6 @@
     half, count = sources // 2, sources // 4
     full = 2 * layers
     devices = lax.axis_size("space")
-    position = lax.axis_index("space")
     pairs = []
     for p in range(1, devices, 2):
         pairs += [(p, (p + 1) % devices), ((p + 1) % devices, p)]
@@ -515,8 +524,9 @@
     dma = pltpu.SemaphoreType.DMA
     slab = (layers, ny, nz)
     other = swap(model)
-    first = lax.dynamic_slice_in_dim(warm_start, half * (1 - tile_of(position)), count, 0)
-    got_first = swap(first.astype(jnp.float32))
+    first = call(pack, (warm_start,), (V,), [f32(count, *slab)], micros=2)
+    got_first = swap(first)
+    beside = swap(other, 1)
     rhs, weights_time = call(
         inject,
         (survey_order, residual_data, electrodes.reshape(1, -1)),
@@ -535,26 +545,26 @@
     field = V((count, full, ny, nz), jnp.float32)
     fields = [field, field, field, V((2, count, full, ny, nz), jnp.float32)]
     block = f32(count, *slab)
-    own_first, sent_first, relay = call(
+    own_first, sent_first, time, opposite, parts = call(
         solve_first,
-        (coefs, got_first, warm_start, rhs, other),
-        (V, V, V, V, V),
-        [block, f32(count * layers, ny, nz), f32(*slab)],
+        (weights_time, model, beside, coefs, got_first, warm_start, rhs),
+        (S, V, V, V, V, V, V),
+        [block, f32(count * layers, ny, nz), f32(*slab), f32(*slab), f32(2 * layers, ny, nz)],
         scratch=fields,
         micros=3,
     )
     back_first = swap(sent_first)
-    beside = swap(relay, 1)
-    own_second, sent_second, times, *parts = call(
+    near = swap(parts, 4)
+    own_second, sent_second, times, joined = call(
         solve_second,
-        (weights_time, model, beside, coefs, got_second, warm_start, rhs, forward, own_first, sent_first),
-        (S, V, V, V, V, V, V, V, V, V),
-        [block, f32(count * layers + 1, ny, nz)] + [f32(*slab)] * 4,
+        (time, opposite, near, coefs, got_second, warm_start, rhs, forward, own_first, sent_first),
+        (V, V, V, V, V, V, V, V, V, V),
+        [block, f32(count * layers + 1, ny, nz), f32(*slab), f32(*slab)],
         scratch=fields,
         micros=3,
     )
     back_second = swap(sent_second)
-    near = [swap(part, 4 * (k + 1)) for k, part in enumerate(parts)]
+    far = swap(joined, 8)
     sums, kept = call(
         gather_terms,
         (forward, own_first, own_second, back_first),
@@ -566,12 +576,12 @@
     )
     adjoint, gradient = call(
         finish,
-        (sums, back_second, sent_second, forward, model, other, times, *near, kept),
-        (V, V, V, V, V, V, V, V, V, V, H),
+        (sums, back_second, sent_second, forward, model, other, times, far, kept),
+        (V, V, V, V, V, V, V, V, H),
         [bf16(*forward.shape), f32(*slab)],
         [H, H],
         scratch=[V((count, *slab), jnp.bfloat16), V(slab, jnp.float32), dma((layers + 1,))],
-        aliases={10: 0},
+        aliases={8: 0},
     )
     return adjoint, gradient
 

time: 46.3 us -> 42.5 us (0.918)
  the two profiles are of different devices: /device:TPU:17 before, /device:TPU:0 now
where the time goes in v4:
time: 42.5 us; the launch traced here: 42.3 us
  starting transfers between devices  16.4 us (39%)
  waiting for transfers between devices  16.1 us (38%)
  Pallas kernels  8.03 us (19%)
  local copies, waits for them, and re-layouts  1.07 us (3%)
  between operations  0.75 us (2%)
    ppermute x8, starting transfers between devices, swap(): return lax.ppermute(x, 'space', links)  16.4 us
    ppermute x8, waiting for transfers between devices, swap(): return lax.ppermute(x, 'space', links)  16.1 us
    pallas_call x7, Pallas kernels, call(): pl.pallas_call(kernel, out_shape=out_shapes if several else out_shapes[0]...  8.03 us
    unnamed x14, local copies, waits for them, and re-layouts  1.07 us
  transfers between devices with their start and end apart: 8, of which 5 were waited for; matrix products, arithmetic and copies ran while one was open for 0% of the time, Pallas kernels for 16%

profile of v4, /device:TPU:0, one launch (start us, length us, event | category | flops | bytes accessed | tf_op | source)
XLA Modules:
  0.0 42.3 jit_solution(8942128408391741044)
XLA Ops:
  0.6 5.5 %collective-permute-start = (f32[4,64,128]{2,1,0:T(8,128)}, f32[4,64,128]{2,1,0:T(8,128)S(1)}, u32[]{:S(2)}, u32[]{:S(2)}) collective-permute-start(f32[4,64,128]{2,1,0:T(8,128)} %model.5), channel_id=1, source_target_pairs={{1,2},{2,1},{3,4},{4,3},{5,6},{6,5},{7,8},{8,7},{9,10},{10,9},{11,... | collective-permute-start | bytes 393224 | tf_op jit(solution)/shard_map/ppermute | solution.py:522
  6.1 0.0 copy-start
  6.1 1.0 %copy-done = bf16[8,4,64,128]{3,2,1,0:T(8,128)(2,1)S(1)} copy-done((bf16[8,4,64,128]{3,2,1,0:T(8,128)(2,1)S(1)}, bf16[8,4,64,128]{3,2,1,0:T(8,128)(2,1)}, u32[]{:S(2)}) %copy-start) | copy-done | bytes 524312
  7.2 0.0 copy-start.4
  7.2 0.0 copy-start.5
  7.2 0.0 copy-start.6
  7.2 0.1 collective-permute-start.2
  7.3 1.8 %collective-permute-done.other = f32[4,64,128]{2,1,0:T(8,128)S(1)} collective-permute-done((f32[4,64,128]{2,1,0:T(8,128)}, f32[4,64,128]{2,1,0:T(8,128)S(1)}, u32[]{:S(2)}, u32[]{:S(2)}) %collective-permute-start) | collective-permute-done | bytes 131104 | tf_op jit(solution)/shard_map/ppermute | solution.py:522
  9.1 0.0 collective-permute-start.1
  9.1 0.0 copy-done.4
  9.1 0.0 copy-done.5
  9.1 0.0 copy-done.6
  9.1 0.0 copy-start.1
  9.1 0.0 copy-start.2
  9.2 0.0 copy-start.3
  9.2 1.2 %shard_map.77 = (f32[4,8,64,128]{3,2,1,0:T(8,128)S(1)}, f32[8]{0:T(128)S(1)}) custom-call(s32[8]{0:T(128)S(1)} %copy-done.6, f32[8,8,256]{2,1,0:T(8,128)S(1)} %copy-done.4, s32[1,256]{1,0:T(1,128)S(1)} %bitcast.1), custom_call_target="tpu_custom_call" | custom-call | flops 1000000000 | bytes 3000000 | tf_op jit(solution)/shard_map/pallas_call | solution.py:489
  10.4 0.0 copy-done.1
  10.4 0.0 copy-done.2
  10.4 0.0 copy-done.3
  10.4 0.3 shard_map.78
  10.8 4.5 %collective-permute-start.4 = (f32[12,64,128]{2,1,0:T(8,128)S(1)}, f32[12,64,128]{2,1,0:T(8,128)S(1)}, u32[]{:S(2)}, u32[]{:S(2)}) collective-permute-start(f32[12,64,128]{2,1,0:T(8,128)S(1)} %get-tuple-element.24), channel_id=1, source_target_pairs={{1,2},{2,1},{3,4},{4,3},{5,6},{6,5},{7,8},{8,7},{9,10},{10,9},{11,... | collective-permute-start | bytes 1179656 | tf_op jit(solution)/shard_map/ppermute | solution.py:522
  15.3 0.0 collective-permute-done.1.beside
  15.3 0.6 %collective-permute-done.2.got = f32[2,4,64,128]{3,2,1,0:T(8,128)S(1)} collective-permute-done((f32[2,4,64,128]{3,2,1,0:T(8,128)S(1)}, f32[2,4,64,128]{3,2,1,0:T(8,128)S(1)}, u32[]{:S(2)}, u32[]{:S(2)}) %collective-permute-start.2) | collective-permute-done | bytes 262176 | tf_op jit(solution)/shard_map/ppermute | solution.py:522
  15.9 2.3 %shard_map.80 = (f32[2,4,64,128]{3,2,1,0:T(8,128)S(1)}, f32[8,64,128]{2,1,0:T(8,128)S(1)}, f32[4,64,128]{2,1,0:T(8,128)S(1)}, f32[4,64,128]{2,1,0:T(8,128)S(1)}, f32[8,64,128]{2,1,0:T(8,128)S(1)}) custom-call(f32[8]{0:T(128)S(1)} %get-tuple-element.17.weights, f32[4,64,128]{2,1,0:T(8,128)S(1)} %copy-done.3, f32[4,64,128]{2,1,0:T(8,128)S(1)} %collective-permute-done.1.beside, ...), custom_call_target="tpu_custom_call" | custom-call | flops 3000000000 | bytes 9000000 | tf_op jit(solution)/shard_map/pallas_call | solution.py:489
  18.1 0.1 collective-permute-start.3
  18.2 2.7 %collective-permute-start.5 = (f32[8,64,128]{2,1,0:T(8,128)S(1)}, f32[8,64,128]{2,1,0:T(8,128)S(1)}, u32[]{:S(2)}, u32[]{:S(2)}) collective-permute-start(f32[8,64,128]{2,1,0:T(8,128)S(1)} %get-tuple-element.25.sent_first), channel_id=1, source_target_pairs={{1,2},{2,1},{3,4},{4,3},{5,6},{6,5},{7,8},{8,7},{9,10},{10,9},{11,... | collective-permute-start | bytes 786440 | tf_op jit(solution)/shard_map/ppermute | solution.py:522
  20.9 2.5 %collective-permute-done.4.got = f32[12,64,128]{2,1,0:T(8,128)S(1)} collective-permute-done((f32[12,64,128]{2,1,0:T(8,128)S(1)}, f32[12,64,128]{2,1,0:T(8,128)S(1)}, u32[]{:S(2)}, u32[]{:S(2)}) %collective-permute-start.4) | collective-permute-done | bytes 393248 | tf_op jit(solution)/shard_map/ppermute | solution.py:522
  23.4 2.8 %collective-permute-done.3.near = f32[8,64,128]{2,1,0:T(8,128)S(1)} collective-permute-done((f32[8,64,128]{2,1,0:T(8,128)S(1)}, f32[8,64,128]{2,1,0:T(8,128)S(1)}, u32[]{:S(2)}, u32[]{:S(2)}) %collective-permute-start.3) | collective-permute-done | bytes 262176 | tf_op jit(solution)/shard_map/ppermute | solution.py:522
  26.2 1.7 %shard_map.81 = (f32[2,4,64,128]{3,2,1,0:T(8,128)S(1)}, f32[9,64,128]{2,1,0:T(8,128)S(1)}, f32[4,64,128]{2,1,0:T(8,128)S(1)}, f32[4,64,128]{2,1,0:T(8,128)S(1)}) custom-call(f32[4,64,128]{2,1,0:T(8,128)S(1)} %get-tuple-element.21.time, f32[4,64,128]{2,1,0:T(8,128)S(1)} %get-tuple-element.22.opposite, f32[8,64,128]{2,1,0:T(8,128)S(1)} %collective-permute-done.3.near, ...), custom_call_target="tpu_custom_call" | custom-call | flops 3000000000 | bytes 9000000 | tf_op jit(solution)/shard_map/pallas_call | solution.py:489
  27.9 3.5 %collective-permute-start.6 = (f32[9,64,128]{2,1,0:T(8,128)S(1)}, f32[9,64,128]{2,1,0:T(8,128)S(1)}, u32[]{:S(2)}, u32[]{:S(2)}) collective-permute-start(f32[9,64,128]{2,1,0:T(8,128)S(1)} %get-tuple-element.28.sent), channel_id=1, source_target_pairs={{1,2},{2,1},{3,4},{4,3},{5,6},{6,5},{7,8},{8,7},{9,10},{10,9},{11,... | collective-permute-start | bytes 884744 | tf_op jit(solution)/shard_map/ppermute | solution.py:522
  31.4 0.0 collective-permute-start.7
  31.4 0.0 collective-permute-done.5.back
  31.4 1.3 %shard_map.82 = (f32[4,4,64,128]{3,2,1,0:T(8,128)S(1)}, bf16[8,4,64,128]{3,2,1,0:T(8,128)(2,1)}) custom-call(bf16[8,4,64,128]{3,2,1,0:T(8,128)(2,1)S(1)} %copy-done.2, f32[2,4,64,128]{3,2,1,0:T(8,128)S(1)} %get-tuple-element.20.own_first, f32[2,4,64,128]{3,2,1,0:T(8,128)S(1)} %get-tuple-element.26.own_second, f32[8,64,128]{2,1,0:T(8,128)S(1)} %collective-permute-done.5.back), custom_call_target="tpu_custom_call" | custom-call | flops 2000000000 | bytes 6000000 | tf_op jit(solution)/shard_map/pallas_call | solution.py:489
  32.7 8.4 %collective-permute-done.7.far = f32[4,64,128]{2,1,0:T(8,128)S(1)} collective-permute-done((f32[4,64,128]{2,1,0:T(8,128)S(1)}, f32[4,64,128]{2,1,0:T(8,128)S(1)}, u32[]{:S(2)}, u32[]{:S(2)}) %collective-permute-start.7) | collective-permute-done | bytes 131104 | tf_op jit(solution)/shard_map/ppermute | solution.py:522
  41.1 0.0 collective-permute-done.6.back
  41.1 1.2 %shard_map.83 = (bf16[8,4,64,128]{3,2,1,0:T(8,128)(2,1)}, f32[4,64,128]{2,1,0:T(8,128)}) custom-call(f32[4,4,64,128]{3,2,1,0:T(8,128)S(1)} %get-tuple-element.27.sums, f32[9,64,128]{2,1,0:T(8,128)S(1)} %collective-permute-done.6.back, f32[9,64,128]{2,1,0:T(8,128)S(1)} %get-tuple-element.28.sent, ...), custom_call_target="tpu_custom_call", output_to_operand_aliasing={{0}: (8, {})} | custom-call | flops 1000000000 | bytes 3000000 | tf_op jit(solution)/shard_map/pallas_call | solution.py:489
  (1 shorter events, 0.0 us)
Async XLA Ops:
  0.6 8.5 %collective-permute-start = (f32[4,64,128]{2,1,0:T(8,128)}, f32[4,64,128]{2,1,0:T(8,128)S(1)}, u32[]{:S(2)}, u32[]{:S(2)}) collective-permute-start(f32[4,64,128]{2,1,0:T(8,128)} %model.5), channel_id=1, source_target_pairs={{1,2},{2,1},{3,4},{4,3},{5,6},{6,5},{7,8},{8,7},{9,10},{10,9},{11,... | collective-permute-start | bytes 393224 | tf_op jit(solution)/shard_map/ppermute | solution.py:522
  6.1 1.0 %copy-start = (bf16[8,4,64,128]{3,2,1,0:T(8,128)(2,1)S(1)}, bf16[8,4,64,128]{3,2,1,0:T(8,128)(2,1)}, u32[]{:S(2)}) copy-start(bf16[8,4,64,128]{3,2,1,0:T(8,128)(2,1)} %warm.7) | copy-start | bytes 1572868
  7.2 1.9 %copy-start.4 = (f32[8,8,256]{2,1,0:T(8,128)S(1)}, f32[8,8,256]{2,1,0:T(8,128)}, u32[]{:S(2)}) copy-start(f32[8,8,256]{2,1,0:T(8,128)} %residual.1) | copy-start | bytes 196612
  7.2 1.9 %copy-start.5 = (s32[256]{0:T(256)S(1)}, s32[256]{0:T(256)}, u32[]{:S(2)}) copy-start(s32[256]{0:T(256)} %param.10) | copy-start | bytes 3076
  7.2 1.9 %copy-start.6 = (s32[8]{0:T(128)S(1)}, s32[8]{0:T(128)}, u32[]{:S(2)}) copy-start(s32[8]{0:T(128)} %order.1) | copy-start | bytes 100
  7.2 8.7 %collective-permute-start.2 = (f32[2,4,64,128]{3,2,1,0:T(8,128)S(1)}, f32[2,4,64,128]{3,2,1,0:T(8,128)S(1)}, u32[]{:S(2)}, u32[]{:S(2)}) collective-permute-start(f32[2,4,64,128]{3,2,1,0:T(8,128)S(1)} %shard_map.79), channel_id=1, source_target_pairs={{1,2},{2,1},{3,4},{4,3},{5,6},{6,5},{7,8},{8,7},{9,10},{10,9},{11,... | collective-permute-start | bytes 786440 | tf_op jit(solution)/shard_map/ppermute | solution.py:522
  9.1 6.2 %collective-permute-start.1 = (f32[4,64,128]{2,1,0:T(8,128)S(1)}, f32[4,64,128]{2,1,0:T(8,128)S(1)}, u32[]{:S(2)}, u32[]{:S(2)}) collective-permute-start(f32[4,64,128]{2,1,0:T(8,128)S(1)} %collective-permute-done.other), channel_id=1, source_target_pairs={{0,1},{1,0},{2,3},{3,2},{4,5},{5,4},{6,7},{7,6},{8,9},{9,8},{10,11... | collective-permute-start | bytes 393224 | tf_op jit(solution)/shard_map/ppermute | solution.py:522
  9.1 1.3 %copy-start.1 = (bf16[8,4,64,128]{3,2,1,0:T(8,128)(2,1)S(1)}, bf16[8,4,64,128]{3,2,1,0:T(8,128)(2,1)}, u32[]{:S(2)}) copy-start(bf16[8,4,64,128]{3,2,1,0:T(8,128)(2,1)} %warm.7) | copy-start | bytes 1572868
  9.1 1.3 %copy-start.2 = (bf16[8,4,64,128]{3,2,1,0:T(8,128)(2,1)S(1)}, bf16[8,4,64,128]{3,2,1,0:T(8,128)(2,1)}, u32[]{:S(2)}) copy-start(bf16[8,4,64,128]{3,2,1,0:T(8,128)(2,1)} %forward.7) | copy-start | bytes 1572868
  9.2 1.3 %copy-start.3 = (f32[4,64,128]{2,1,0:T(8,128)S(1)}, f32[4,64,128]{2,1,0:T(8,128)}, u32[]{:S(2)}) copy-start(f32[4,64,128]{2,1,0:T(8,128)} %model.5) | copy-start | bytes 393220
  10.8 12.6 %collective-permute-start.4 = (f32[12,64,128]{2,1,0:T(8,128)S(1)}, f32[12,64,128]{2,1,0:T(8,128)S(1)}, u32[]{:S(2)}, u32[]{:S(2)}) collective-permute-start(f32[12,64,128]{2,1,0:T(8,128)S(1)} %get-tuple-element.24), channel_id=1, source_target_pairs={{1,2},{2,1},{3,4},{4,3},{5,6},{6,5},{7,8},{8,7},{9,10},{10,9},{11,... | collective-permute-start | bytes 1179656 | tf_op jit(solution)/shard_map/ppermute | solution.py:522
  18.1 8.0 %collective-permute-start.3 = (f32[8,64,128]{2,1,0:T(8,128)S(1)}, f32[8,64,128]{2,1,0:T(8,128)S(1)}, u32[]{:S(2)}, u32[]{:S(2)}) collective-permute-start(f32[8,64,128]{2,1,0:T(8,128)S(1)} %get-tuple-element.23), channel_id=1, source_target_pairs={{0,4},{1,5},{2,6},{3,7},{4,0},{5,1},{6,2},{7,3},{8,12},{9,13},{10,... | collective-permute-start | bytes 786440 | tf_op jit(solution)/shard_map/ppermute | solution.py:522
  18.2 13.2 %collective-permute-start.5 = (f32[8,64,128]{2,1,0:T(8,128)S(1)}, f32[8,64,128]{2,1,0:T(8,128)S(1)}, u32[]{:S(2)}, u32[]{:S(2)}) collective-permute-start(f32[8,64,128]{2,1,0:T(8,128)S(1)} %get-tuple-element.25.sent_first), channel_id=1, source_target_pairs={{1,2},{2,1},{3,4},{4,3},{5,6},{6,5},{7,8},{8,7},{9,10},{10,9},{11,... | collective-permute-start | bytes 786440 | tf_op jit(solution)/shard_map/ppermute | solution.py:522
  27.9 13.2 %collective-permute-start.6 = (f32[9,64,128]{2,1,0:T(8,128)S(1)}, f32[9,64,128]{2,1,0:T(8,128)S(1)}, u32[]{:S(2)}, u32[]{:S(2)}) collective-permute-start(f32[9,64,128]{2,1,0:T(8,128)S(1)} %get-tuple-element.28.sent), channel_id=1, source_target_pairs={{1,2},{2,1},{3,4},{4,3},{5,6},{6,5},{7,8},{8,7},{9,10},{10,9},{11,... | collective-permute-start | bytes 884744 | tf_op jit(solution)/shard_map/ppermute | solution.py:522
  31.4 9.7 %collective-permute-start.7 = (f32[4,64,128]{2,1,0:T(8,128)S(1)}, f32[4,64,128]{2,1,0:T(8,128)S(1)}, u32[]{:S(2)}, u32[]{:S(2)}) collective-permute-start(f32[4,64,128]{2,1,0:T(8,128)S(1)} %get-tuple-element.30), channel_id=1, source_target_pairs={{0,8},{1,9},{2,10},{3,11},{4,12},{5,13},{6,14},{7,15},{8,0},{9,1},... | collective-permute-start | bytes 393224 | tf_op jit(solution)/shard_map/ppermute | solution.py:522

commit v5 on v4

--- a/solution.py
+++ b/solution.py
@@ -343,13 +343,23 @@
         start[q, layers:] = got[q] if len(got.shape) == 4 else got[layers * q : layers * (q + 1)]
 
 
-def solve_first(weights, model, beside, coefs, got, warm, rhs, own, sent, time, opposite, parts, start, rest, lam, mine):
-    count, layers = own.shape[:2]
+def split_time(weights, model, beside, time, opposite, parts):
+    layers = model.shape[0]
     here, there = model[...], beside[...]
     time[...] = weights[0] * here + weights[1] * there
     parts[:layers] = weights[2] * here + weights[3] * there
     opposite[...] = weights[4] * here + weights[5] * there
     parts[layers:] = weights[6] * here + weights[7] * there
+
+
+def join_time(time, opposite, near, times, joined):
+    layers = time.shape[0]
+    times[...] = time[...] + near[:layers]
+    joined[...] = opposite[...] + near[layers:]
+
+
+def solve_first(coefs, got, warm, rhs, own, sent, start, rest, lam, mine):
+    count, layers = own.shape[:2]
     load_start(warm, 2 * count * tile_of(lax.axis_index("space")), got, start)
     sweeps(coefs, rhs, 0, start, rest, lam, mine)
     for q in range(count):
@@ -357,11 +367,9 @@
         sent[layers * q : layers * (q + 1)] = lam[q, layers:]
 
 
-def solve_second(time, opposite, near, coefs, got, warm, rhs, forward, own_first, sent_first, own, sent, times, joined, start, rest, lam, mine):
+def solve_second(times, coefs, got, warm, rhs, forward, own_first, sent_first, own, sent, start, rest, lam, mine):
     count, layers = own.shape[:2]
     tile = tile_of(lax.axis_index("space"))
-    times[...] = time[...] + near[:layers]
-    joined[...] = opposite[...] + near[layers:]
     source = 2 * count * tile
     load_start(warm, source + count, got, start)
     sweeps(coefs, rhs, count, start, rest, lam, mine)
@@ -400,8 +408,9 @@
         mass[i] = mass[i] + totals[3]
 
 
-def gather_terms(forward, own_first, own_second, back, sums, adjoint, rounded, sems):
+def gather_terms(forward, own_first, own_second, back, times, far, sums, adjoint, time, rounded, sems):
     count, layers = own_first.shape[:2]
+    time[...] = times[...] + far[...]
     tile = tile_of(lax.axis_index("space"))
     mine, theirs = 2 * count * tile, 2 * count * (1 - tile)
     for q in range(count):
@@ -426,7 +435,7 @@
         copy.wait()
 
 
-def finish(sums, back, sent, forward, model, other, times, far, kept, adjoint, gradient, rounded, result, sems):
+def finish(sums, back, sent, forward, model, other, times, kept, adjoint, gradient, rounded, result, sems):
     tile = tile_of(lax.axis_index("space"))
     count, layers = rounded.shape[:2]
     theirs = 2 * count * (1 - tile) + count
@@ -472,7 +481,7 @@
         fall_y = jnp.where(in_y, value - after(value, 0), 0.0)
         fall_z = jnp.where(in_z, value - after(value, 1), 0.0)
         space = falls[i + 1] - falls[i] + (fall_y - before(fall_y, 0)) + (fall_z - before(fall_z, 1))
-        result[i] = space + (times[i] + far[i]) - jnp.exp(value) * (0.5 * terms + GROUND * mass)
+        result[i] = space + times[i] - jnp.exp(value) * (0.5 * terms + GROUND * mass)
         copies.append(pltpu.make_async_copy(result.at[i], gradient.at[i], sems.at[i]))
         copies[-1].start()
     for copy in copies:
@@ -524,7 +533,7 @@
     dma = pltpu.SemaphoreType.DMA
     slab = (layers, ny, nz)
     other = swap(model)
-    first = call(pack, (warm_start,), (V,), [f32(count, *slab)], micros=2)
+    first = call(pack, (warm_start,), (V,), [f32(count, *slab)])
     got_first = swap(first)
     beside = swap(other, 1)
     rhs, weights_time = call(
@@ -545,43 +554,50 @@
     field = V((count, full, ny, nz), jnp.float32)
     fields = [field, field, field, V((2, count, full, ny, nz), jnp.float32)]
     block = f32(count, *slab)
-    own_first, sent_first, time, opposite, parts = call(
+    time, opposite, parts = call(
+        split_time,
+        (weights_time, model, beside),
+        (S, V, V),
+        [f32(*slab), f32(*slab), f32(2 * layers, ny, nz)],
+    )
+    near = swap(parts, 4)
+    own_first, sent_first = call(
         solve_first,
-        (weights_time, model, beside, coefs, got_first, warm_start, rhs),
-        (S, V, V, V, V, V, V),
-        [block, f32(count * layers, ny, nz), f32(*slab), f32(*slab), f32(2 * layers, ny, nz)],
+        (coefs, got_first, warm_start, rhs),
+        (V, V, V, V),
+        [block, f32(count * layers, ny, nz)],
         scratch=fields,
         micros=3,
     )
     back_first = swap(sent_first)
-    near = swap(parts, 4)
-    own_second, sent_second, times, joined = call(
+    times, joined = call(join_time, (time, opposite, near), (V, V, V), [f32(*slab), f32(*slab)])
+    far = swap(joined, 8)
+    own_second, sent_second = call(
         solve_second,
-        (time, opposite, near, coefs, got_second, warm_start, rhs, forward, own_first, sent_first),
-        (V, V, V, V, V, V, V, V, V, V),
-        [block, f32(count * layers + 1, ny, nz), f32(*slab), f32(*slab)],
+        (times, coefs, got_second, warm_start, rhs, forward, own_first, sent_first),
+        (V, V, V, V, V, V, V, V),
+        [block, f32(count * layers + 1, ny, nz)],
         scratch=fields,
         micros=3,
     )
     back_second = swap(sent_second)
-    far = swap(joined, 8)
-    sums, kept = call(
+    sums, kept, time = call(
         gather_terms,
-        (forward, own_first, own_second, back_first),
-        (V, V, V, V),
-        [f32(4, *slab), bf16(*forward.shape)],
-        [V, H],
+        (forward, own_first, own_second, back_first, times, far),
+        (V, V, V, V, V, V),
+        [f32(4, *slab), bf16(*forward.shape), f32(*slab)],
+        [V, H, V],
         scratch=[V((3 * count, *slab), jnp.bfloat16), dma((2,))],
         micros=2,
     )
     adjoint, gradient = call(
         finish,
-        (sums, back_second, sent_second, forward, model, other, times, far, kept),
-        (V, V, V, V, V, V, V, V, H),
+        (sums, back_second, sent_second, forward, model, other, time, kept),
+        (V, V, V, V, V, V, V, H),
         [bf16(*forward.shape), f32(*slab)],
         [H, H],
         scratch=[V((count, *slab), jnp.bfloat16), V(slab, jnp.float32), dma((layers + 1,))],
-        aliases={8: 0},
+        aliases={7: 0},
     )
     return adjoint, gradient
 

time: 42.5 us -> 40.2 us (0.946)
  waiting for transfers between devices: 16.1 us -> 12.3 us
  starting transfers between devices: 16.4 us -> 17.9 us
    ppermute x8, waiting for transfers between devices: 16.1 us -> 12.3 us  [swap(): return lax.ppermute(x, 'space', links)]
    ppermute x8, starting transfers between devices: 16.4 us -> 17.9 us  [swap(): return lax.ppermute(x, 'space', links)]
    pallas_call x7 -> x9, Pallas kernels: 8.03 us -> 8 us  [call(): pl.pallas_call(kernel, out_shape=out_shapes if several else out_shapes[0]...]
  transfers between devices with their start and end apart: 8 -> 8, of which waited for: 5 -> 4; matrix products, arithmetic and copies ran while one was open for 0% -> 0% of each run, Pallas kernels for 16% -> 17%
where the time goes in v5:
time: 40.2 us; the launch traced here: 40 us
  starting transfers between devices  17.9 us (45%)
  waiting for transfers between devices  12.3 us (31%)
  Pallas kernels  8 us (20%)
  local copies, waits for them, and re-layouts  1.07 us (3%)
  between operations  0.76 us (2%)
    ppermute x8, starting transfers between devices, swap(): return lax.ppermute(x, 'space', links)  17.9 us
    ppermute x8, waiting for transfers between devices, swap(): return lax.ppermute(x, 'space', links)  12.3 us
    pallas_call x9, Pallas kernels, call(): pl.pallas_call(kernel, out_shape=out_shapes if several else out_shapes[0]...  8 us
    unnamed x14, local copies, waits for them, and re-layouts  1.07 us
  transfers between devices with their start and end apart: 8, of which 4 were waited for; matrix products, arithmetic and copies ran while one was open for 0% of the time, Pallas kernels for 17%

profile of v5, /device:TPU:0, one launch (start us, length us, event | category | flops | bytes accessed | tf_op | source)
XLA Modules:
  0.0 40.0 jit_solution(11682740887716198813)
XLA Ops:
  0.6 5.5 %collective-permute-start = (f32[4,64,128]{2,1,0:T(8,128)}, f32[4,64,128]{2,1,0:T(8,128)S(1)}, u32[]{:S(2)}, u32[]{:S(2)}) collective-permute-start(f32[4,64,128]{2,1,0:T(8,128)} %model.5), channel_id=1, source_target_pairs={{1,2},{2,1},{3,4},{4,3},{5,6},{6,5},{7,8},{8,7},{9,10},{10,9},{11,... | collective-permute-start | bytes 393224 | tf_op jit(solution)/shard_map/ppermute | solution.py:531
  6.1 0.0 copy-start
  6.1 1.0 %copy-done = bf16[8,4,64,128]{3,2,1,0:T(8,128)(2,1)S(1)} copy-done((bf16[8,4,64,128]{3,2,1,0:T(8,128)(2,1)S(1)}, bf16[8,4,64,128]{3,2,1,0:T(8,128)(2,1)}, u32[]{:S(2)}) %copy-start) | copy-done | bytes 524312
  7.2 0.0 copy-start.4
  7.2 0.0 copy-start.5
  7.2 0.0 copy-start.6
  7.2 0.1 collective-permute-start.1
  7.3 1.8 %collective-permute-done.other = f32[4,64,128]{2,1,0:T(8,128)S(1)} collective-permute-done((f32[4,64,128]{2,1,0:T(8,128)}, f32[4,64,128]{2,1,0:T(8,128)S(1)}, u32[]{:S(2)}, u32[]{:S(2)}) %collective-permute-start) | collective-permute-done | bytes 131104 | tf_op jit(solution)/shard_map/ppermute | solution.py:531
  9.1 0.0 collective-permute-start.2
  9.1 0.0 copy-done.4
  9.1 0.0 copy-done.5
  9.1 0.0 copy-done.6
  9.1 0.0 copy-start.1
  9.1 0.0 copy-start.2
  9.2 0.0 copy-start.3
  9.2 1.2 %shard_map.79 = (f32[4,8,64,128]{3,2,1,0:T(8,128)S(1)}, f32[8]{0:T(128)S(1)}) custom-call(s32[8]{0:T(128)S(1)} %copy-done.6, f32[8,8,256]{2,1,0:T(8,128)S(1)} %copy-done.4, s32[1,256]{1,0:T(1,128)S(1)} %bitcast.1), custom_call_target="tpu_custom_call" | custom-call | flops 1000000000 | bytes 3000000 | tf_op jit(solution)/shard_map/pallas_call | solution.py:498
  10.4 0.0 copy-done.1
  10.4 0.0 copy-done.2
  10.4 0.0 copy-done.3
  10.4 0.3 shard_map.77
  10.8 4.5 %collective-permute-start.4 = (f32[12,64,128]{2,1,0:T(8,128)S(1)}, f32[12,64,128]{2,1,0:T(8,128)S(1)}, u32[]{:S(2)}, u32[]{:S(2)}) collective-permute-start(f32[12,64,128]{2,1,0:T(8,128)S(1)} %get-tuple-element.26), channel_id=1, source_target_pairs={{1,2},{2,1},{3,4},{4,3},{5,6},{6,5},{7,8},{8,7},{9,10},{10,9},{11,... | collective-permute-start | bytes 1179656 | tf_op jit(solution)/shard_map/ppermute | solution.py:531
  15.3 0.0 collective-permute-done.2.beside
  15.3 0.6 %shard_map.81 = (f32[4,64,128]{2,1,0:T(8,128)S(1)}, f32[4,64,128]{2,1,0:T(8,128)S(1)}, f32[8,64,128]{2,1,0:T(8,128)S(1)}) custom-call(f32[8]{0:T(128)S(1)} %get-tuple-element.21.weights, f32[4,64,128]{2,1,0:T(8,128)S(1)} %copy-done.3, f32[4,64,128]{2,1,0:T(8,128)S(1)} %collective-permute-done.2.beside), custom_call_target="tpu_custom_call" | custom-call | flops 1000000000 | bytes 3000000 | tf_op jit(solution)/shard_map/pallas_call | solution.py:498
  15.9 0.1 collective-permute-start.3
  16.0 0.0 collective-permute-done.1.got
  16.0 1.6 %shard_map.80 = (f32[2,4,64,128]{3,2,1,0:T(8,128)S(1)}, f32[8,64,128]{2,1,0:T(8,128)S(1)}) custom-call(f32[7,8,64,128]{3,2,1,0:T(8,128)S(1)} %get-tuple-element.18.coefs, f32[2,4,64,128]{3,2,1,0:T(8,128)S(1)} %collective-permute-done.1.got, bf16[8,4,64,128]{3,2,1,0:T(8,128)(2,1)S(1)} %copy-done.1, f32[4,8,64,128]{3,2,1,0:T(8,128)S(1)} %get-tuple-element.19.rhs), custom_call_target="tpu_custom_call" | custom-call | flops 3000000000 | bytes 9000000 | tf_op jit(solution)/shard_map/pallas_call | solution.py:498
  17.6 3.4 %collective-permute-start.5 = (f32[8,64,128]{2,1,0:T(8,128)S(1)}, f32[8,64,128]{2,1,0:T(8,128)S(1)}, u32[]{:S(2)}, u32[]{:S(2)}) collective-permute-start(f32[8,64,128]{2,1,0:T(8,128)S(1)} %get-tuple-element.27.sent_first), channel_id=1, source_target_pairs={{1,2},{2,1},{3,4},{4,3},{5,6},{6,5},{7,8},{8,7},{9,10},{10,9},{11,... | collective-permute-start | bytes 786440 | tf_op jit(solution)/shard_map/ppermute | solution.py:531
  21.0 4.6 %collective-permute-done.3.near = f32[8,64,128]{2,1,0:T(8,128)S(1)} collective-permute-done((f32[8,64,128]{2,1,0:T(8,128)S(1)}, f32[8,64,128]{2,1,0:T(8,128)S(1)}, u32[]{:S(2)}, u32[]{:S(2)}) %collective-permute-start.3) | collective-permute-done | bytes 262176 | tf_op jit(solution)/shard_map/ppermute | solution.py:531
  25.6 2.7 %collective-permute-start.6 = (f32[4,64,128]{2,1,0:T(8,128)S(1)}, f32[4,64,128]{2,1,0:T(8,128)S(1)}, u32[]{:S(2)}, u32[]{:S(2)}) collective-permute-start(f32[4,64,128]{2,1,0:T(8,128)S(1)} %get-tuple-element.29), channel_id=1, source_target_pairs={{0,8},{1,9},{2,10},{3,11},{4,12},{5,13},{6,14},{7,15},{8,0},{9,1},... | collective-permute-start | bytes 393224 | tf_op jit(solution)/shard_map/ppermute | solution.py:531
  28.3 0.0 collective-permute-done.4.got
  28.3 1.7 %shard_map.83 = (f32[2,4,64,128]{3,2,1,0:T(8,128)S(1)}, f32[9,64,128]{2,1,0:T(8,128)S(1)}) custom-call(f32[4,64,128]{2,1,0:T(8,128)S(1)} %get-tuple-element.25.times, f32[7,8,64,128]{3,2,1,0:T(8,128)S(1)} %get-tuple-element.18.coefs, f32[12,64,128]{2,1,0:T(8,128)S(1)} %collective-permute-done.4.got, bf16[8,4,64,128]{3,2,1,0:T(8,128)(2,1)S(1)} %copy-done.1, ...), custom_call_target="tpu_custom_call" | custom-call | flops 3000000000 | bytes 9000000 | tf_op jit(solution)/shard_map/pallas_call | solution.py:498
  30.0 1.7 %collective-permute-start.7 = (f32[9,64,128]{2,1,0:T(8,128)S(1)}, f32[9,64,128]{2,1,0:T(8,128)S(1)}, u32[]{:S(2)}, u32[]{:S(2)}) collective-permute-start(f32[9,64,128]{2,1,0:T(8,128)S(1)} %get-tuple-element.31.sent), channel_id=1, source_target_pairs={{1,2},{2,1},{3,4},{4,3},{5,6},{6,5},{7,8},{8,7},{9,10},{10,9},{11,... | collective-permute-start | bytes 884744 | tf_op jit(solution)/shard_map/ppermute | solution.py:531
  31.6 0.0 collective-permute-done.5.back
  31.6 1.1 %collective-permute-done.6.far = f32[4,64,128]{2,1,0:T(8,128)S(1)} collective-permute-done((f32[4,64,128]{2,1,0:T(8,128)S(1)}, f32[4,64,128]{2,1,0:T(8,128)S(1)}, u32[]{:S(2)}, u32[]{:S(2)}) %collective-permute-start.6) | collective-permute-done | bytes 131104 | tf_op jit(solution)/shard_map/ppermute | solution.py:531
  32.7 1.3 %shard_map.84 = (f32[4,4,64,128]{3,2,1,0:T(8,128)S(1)}, bf16[8,4,64,128]{3,2,1,0:T(8,128)(2,1)}, f32[4,64,128]{2,1,0:T(8,128)S(1)}) custom-call(bf16[8,4,64,128]{3,2,1,0:T(8,128)(2,1)S(1)} %copy-done.2, f32[2,4,64,128]{3,2,1,0:T(8,128)S(1)} %get-tuple-element.20.own_first, f32[2,4,64,128]{3,2,1,0:T(8,128)S(1)} %get-tuple-element.28.own_second, ...), custom_call_target="tpu_custom_call" | custom-call | flops 2000000000 | bytes 6000000 | tf_op jit(solution)/shard_map/pallas_call | solution.py:498
  34.1 4.8 %collective-permute-done.7.back = f32[9,64,128]{2,1,0:T(8,128)S(1)} collective-permute-done((f32[9,64,128]{2,1,0:T(8,128)S(1)}, f32[9,64,128]{2,1,0:T(8,128)S(1)}, u32[]{:S(2)}, u32[]{:S(2)}) %collective-permute-start.7) | collective-permute-done | bytes 294944 | tf_op jit(solution)/shard_map/ppermute | solution.py:531
  38.9 1.2 %shard_map.85 = (bf16[8,4,64,128]{3,2,1,0:T(8,128)(2,1)}, f32[4,64,128]{2,1,0:T(8,128)}) custom-call(f32[4,4,64,128]{3,2,1,0:T(8,128)S(1)} %get-tuple-element.30.sums, f32[9,64,128]{2,1,0:T(8,128)S(1)} %collective-permute-done.7.back, f32[9,64,128]{2,1,0:T(8,128)S(1)} %get-tuple-element.31.sent, ...), custom_call_target="tpu_custom_call", output_to_operand_aliasing={{0}: (7, {})} | custom-call | flops 1000000000 | bytes 3000000 | tf_op jit(solution)/shard_map/pallas_call | solution.py:498
  (2 shorter events, 0.0 us)
Async XLA Ops:
  0.6 8.5 %collective-permute-start = (f32[4,64,128]{2,1,0:T(8,128)}, f32[4,64,128]{2,1,0:T(8,128)S(1)}, u32[]{:S(2)}, u32[]{:S(2)}) collective-permute-start(f32[4,64,128]{2,1,0:T(8,128)} %model.5), channel_id=1, source_target_pairs={{1,2},{2,1},{3,4},{4,3},{5,6},{6,5},{7,8},{8,7},{9,10},{10,9},{11,... | collective-permute-start | bytes 393224 | tf_op jit(solution)/shard_map/ppermute | solution.py:531
  6.1 1.0 %copy-start = (bf16[8,4,64,128]{3,2,1,0:T(8,128)(2,1)S(1)}, bf16[8,4,64,128]{3,2,1,0:T(8,128)(2,1)}, u32[]{:S(2)}) copy-start(bf16[8,4,64,128]{3,2,1,0:T(8,128)(2,1)} %warm.7) | copy-start | bytes 1572868
  7.2 1.9 %copy-start.4 = (f32[8,8,256]{2,1,0:T(8,128)S(1)}, f32[8,8,256]{2,1,0:T(8,128)}, u32[]{:S(2)}) copy-start(f32[8,8,256]{2,1,0:T(8,128)} %residual.1) | copy-start | bytes 196612
  7.2 1.9 %copy-start.5 = (s32[256]{0:T(256)S(1)}, s32[256]{0:T(256)}, u32[]{:S(2)}) copy-start(s32[256]{0:T(256)} %param.10) | copy-start | bytes 3076
  7.2 1.9 %copy-start.6 = (s32[8]{0:T(128)S(1)}, s32[8]{0:T(128)}, u32[]{:S(2)}) copy-start(s32[8]{0:T(128)} %order.1) | copy-start | bytes 100
  7.2 8.8 %collective-permute-start.1 = (f32[2,4,64,128]{3,2,1,0:T(8,128)S(1)}, f32[2,4,64,128]{3,2,1,0:T(8,128)S(1)}, u32[]{:S(2)}, u32[]{:S(2)}) collective-permute-start(f32[2,4,64,128]{3,2,1,0:T(8,128)S(1)} %shard_map.78), channel_id=1, source_target_pairs={{1,2},{2,1},{3,4},{4,3},{5,6},{6,5},{7,8},{8,7},{9,10},{10,9},{11,... | collective-permute-start | bytes 786440 | tf_op jit(solution)/shard_map/ppermute | solution.py:531
  9.1 6.2 %collective-permute-start.2 = (f32[4,64,128]{2,1,0:T(8,128)S(1)}, f32[4,64,128]{2,1,0:T(8,128)S(1)}, u32[]{:S(2)}, u32[]{:S(2)}) collective-permute-start(f32[4,64,128]{2,1,0:T(8,128)S(1)} %collective-permute-done.other), channel_id=1, source_target_pairs={{0,1},{1,0},{2,3},{3,2},{4,5},{5,4},{6,7},{7,6},{8,9},{9,8},{10,11... | collective-permute-start | bytes 393224 | tf_op jit(solution)/shard_map/ppermute | solution.py:531
  9.1 1.3 %copy-start.1 = (bf16[8,4,64,128]{3,2,1,0:T(8,128)(2,1)S(1)}, bf16[8,4,64,128]{3,2,1,0:T(8,128)(2,1)}, u32[]{:S(2)}) copy-start(bf16[8,4,64,128]{3,2,1,0:T(8,128)(2,1)} %warm.7) | copy-start | bytes 1572868
  9.1 1.3 %copy-start.2 = (bf16[8,4,64,128]{3,2,1,0:T(8,128)(2,1)S(1)}, bf16[8,4,64,128]{3,2,1,0:T(8,128)(2,1)}, u32[]{:S(2)}) copy-start(bf16[8,4,64,128]{3,2,1,0:T(8,128)(2,1)} %forward.7) | copy-start | bytes 1572868
  9.2 1.3 %copy-start.3 = (f32[4,64,128]{2,1,0:T(8,128)S(1)}, f32[4,64,128]{2,1,0:T(8,128)}, u32[]{:S(2)}) copy-start(f32[4,64,128]{2,1,0:T(8,128)} %model.5) | copy-start | bytes 393220
  10.8 17.5 %collective-permute-start.4 = (f32[12,64,128]{2,1,0:T(8,128)S(1)}, f32[12,64,128]{2,1,0:T(8,128)S(1)}, u32[]{:S(2)}, u32[]{:S(2)}) collective-permute-start(f32[12,64,128]{2,1,0:T(8,128)S(1)} %get-tuple-element.26), channel_id=1, source_target_pairs={{1,2},{2,1},{3,4},{4,3},{5,6},{6,5},{7,8},{8,7},{9,10},{10,9},{11,... | collective-permute-start | bytes 1179656 | tf_op jit(solution)/shard_map/ppermute | solution.py:531
  15.9 9.7 %collective-permute-start.3 = (f32[8,64,128]{2,1,0:T(8,128)S(1)}, f32[8,64,128]{2,1,0:T(8,128)S(1)}, u32[]{:S(2)}, u32[]{:S(2)}) collective-permute-start(f32[8,64,128]{2,1,0:T(8,128)S(1)} %get-tuple-element.24), channel_id=1, source_target_pairs={{0,4},{1,5},{2,6},{3,7},{4,0},{5,1},{6,2},{7,3},{8,12},{9,13},{10,... | collective-permute-start | bytes 786440 | tf_op jit(solution)/shard_map/ppermute | solution.py:531
  17.6 14.0 %collective-permute-start.5 = (f32[8,64,128]{2,1,0:T(8,128)S(1)}, f32[8,64,128]{2,1,0:T(8,128)S(1)}, u32[]{:S(2)}, u32[]{:S(2)}) collective-permute-start(f32[8,64,128]{2,1,0:T(8,128)S(1)} %get-tuple-element.27.sent_first), channel_id=1, source_target_pairs={{1,2},{2,1},{3,4},{4,3},{5,6},{6,5},{7,8},{8,7},{9,10},{10,9},{11,... | collective-permute-start | bytes 786440 | tf_op jit(solution)/shard_map/ppermute | solution.py:531
  25.6 7.1 %collective-permute-start.6 = (f32[4,64,128]{2,1,0:T(8,128)S(1)}, f32[4,64,128]{2,1,0:T(8,128)S(1)}, u32[]{:S(2)}, u32[]{:S(2)}) collective-permute-start(f32[4,64,128]{2,1,0:T(8,128)S(1)} %get-tuple-element.29), channel_id=1, source_target_pairs={{0,8},{1,9},{2,10},{3,11},{4,12},{5,13},{6,14},{7,15},{8,0},{9,1},... | collective-permute-start | bytes 393224 | tf_op jit(solution)/shard_map/ppermute | solution.py:531
  30.0 8.9 %collective-permute-start.7 = (f32[9,64,128]{2,1,0:T(8,128)S(1)}, f32[9,64,128]{2,1,0:T(8,128)S(1)}, u32[]{:S(2)}, u32[]{:S(2)}) collective-permute-start(f32[9,64,128]{2,1,0:T(8,128)S(1)} %get-tuple-element.31.sent), channel_id=1, source_target_pairs={{1,2},{2,1},{3,4},{4,3},{5,6},{6,5},{7,8},{8,7},{9,10},{10,9},{11,... | collective-permute-start | bytes 884744 | tf_op jit(solution)/shard_map/ppermute | solution.py:531

commit v6 on v5

--- a/solution.py
+++ b/solution.py
@@ -211,7 +211,7 @@
         first[q] = warm[2 * count * (1 - tile) + q].astype(jnp.float32)
 
 
-def inject(order, residual, electrodes, out, weights):
+def inject(order, residual, electrodes, coefs, out, weights):
     position = lax.axis_index("space")
     tile = tile_of(position)
     surveys = order.shape[0]
@@ -253,7 +253,7 @@
         )
         total = term if total is None else total + term
     for q in range(sources):
-        out[q] = total[:, q * rows_z : (q + 1) * rows_z].reshape(out.shape[1:])
+        out[q] = coefs[6] * total[:, q * rows_z : (q + 1) * rows_z].reshape(out.shape[1:])
 
 
 def prepare(model, other, warm, forward, coefs, second, sigma):
@@ -306,10 +306,10 @@
         return here, total
 
     def first(i, carry):
-        weight = [coefs[k, i] for k in range(7)]
+        weight = [coefs[k, i] for k in range(6)]
         for q in range(count):
             here, total = around(start, q, i, weight)
-            step = rhs[base + q, i] * weight[6] - here + total
+            step = rhs[base + q, i] - here + total
             mine[0, q, i] = step
             lam[q, i] = here + step
         return carry
@@ -352,7 +352,7 @@
     parts[layers:] = weights[6] * here + weights[7] * there
 
 
-def join_time(time, opposite, near, times, joined):
+def join_time(time, opposite, near, solved, times, joined):
     layers = time.shape[0]
     times[...] = time[...] + near[:layers]
     joined[...] = opposite[...] + near[layers:]
@@ -367,7 +367,7 @@
         sent[layers * q : layers * (q + 1)] = lam[q, layers:]
 
 
-def solve_second(times, coefs, got, warm, rhs, forward, own_first, sent_first, own, sent, start, rest, lam, mine):
+def solve_second(coefs, got, warm, rhs, forward, own_first, sent_first, own, sent, start, rest, lam, mine):
     count, layers = own.shape[:2]
     tile = tile_of(lax.axis_index("space"))
     source = 2 * count * tile
@@ -408,9 +408,8 @@
         mass[i] = mass[i] + totals[3]
 
 
-def gather_terms(forward, own_first, own_second, back, times, far, sums, adjoint, time, rounded, sems):
+def gather_terms(forward, own_first, own_second, back, sums, adjoint, rounded, sems):
     count, layers = own_first.shape[:2]
-    time[...] = times[...] + far[...]
     tile = tile_of(lax.axis_index("space"))
     mine, theirs = 2 * count * tile, 2 * count * (1 - tile)
     for q in range(count):
@@ -435,7 +434,7 @@
         copy.wait()
 
 
-def finish(sums, back, sent, forward, model, other, times, kept, adjoint, gradient, rounded, result, sems):
+def finish(sums, back, sent, forward, model, other, times, far, kept, adjoint, gradient, rounded, result, sems):
     tile = tile_of(lax.axis_index("space"))
     count, layers = rounded.shape[:2]
     theirs = 2 * count * (1 - tile) + count
@@ -481,7 +480,7 @@
         fall_y = jnp.where(in_y, value - after(value, 0), 0.0)
         fall_z = jnp.where(in_z, value - after(value, 1), 0.0)
         space = falls[i + 1] - falls[i] + (fall_y - before(fall_y, 0)) + (fall_z - before(fall_z, 1))
-        result[i] = space + times[i] - jnp.exp(value) * (0.5 * terms + GROUND * mass)
+        result[i] = space + (times[i] + far[i]) - jnp.exp(value) * (0.5 * terms + GROUND * mass)
         copies.append(pltpu.make_async_copy(result.at[i], gradient.at[i], sems.at[i]))
         copies[-1].start()
     for copy in copies:
@@ -536,19 +535,19 @@
     first = call(pack, (warm_start,), (V,), [f32(count, *slab)])
     got_first = swap(first)
     beside = swap(other, 1)
-    rhs, weights_time = call(
-        inject,
-        (survey_order, residual_data, electrodes.reshape(1, -1)),
-        (S, V, V),
-        [f32(half, full, ny, nz), f32(8)],
-        [V, S],
-    )
     coefs, second = call(
         prepare,
         (model, other, warm_start, forward),
         (V, V, V, V),
         [f32(7, full, ny, nz), f32(count * layers + half, ny, nz)],
         scratch=[V((full, ny, nz), jnp.float32)],
+    )
+    rhs, weights_time = call(
+        inject,
+        (survey_order, residual_data, electrodes.reshape(1, -1), coefs),
+        (S, V, V, V),
+        [f32(half, full, ny, nz), f32(8)],
+        [V, S],
     )
     got_second = swap(second)
     field = V((count, full, ny, nz), jnp.float32)
@@ -570,34 +569,34 @@
         micros=3,
     )
     back_first = swap(sent_first)
-    times, joined = call(join_time, (time, opposite, near), (V, V, V), [f32(*slab), f32(*slab)])
-    far = swap(joined, 8)
     own_second, sent_second = call(
         solve_second,
-        (times, coefs, got_second, warm_start, rhs, forward, own_first, sent_first),
-        (V, V, V, V, V, V, V, V),
+        (coefs, got_second, warm_start, rhs, forward, own_first, sent_first),
+        (V, V, V, V, V, V, V),
         [block, f32(count * layers + 1, ny, nz)],
         scratch=fields,
         micros=3,
     )
     back_second = swap(sent_second)
-    sums, kept, time = call(
+    times, joined = call(join_time, (time, opposite, near, own_second), (V, V, V, V), [f32(*slab), f32(*slab)])
+    far = swap(joined, 8)
+    sums, kept = call(
         gather_terms,
-        (forward, own_first, own_second, back_first, times, far),
-        (V, V, V, V, V, V),
-        [f32(4, *slab), bf16(*forward.shape), f32(*slab)],
-        [V, H, V],
+        (forward, own_first, own_second, back_first),
+        (V, V, V, V),
+        [f32(4, *slab), bf16(*forward.shape)],
+        [V, H],
         scratch=[V((3 * count, *slab), jnp.bfloat16), dma((2,))],
         micros=2,
     )
     adjoint, gradient = call(
         finish,
-        (sums, back_second, sent_second, forward, model, other, time, kept),
-        (V, V, V, V, V, V, V, H),
+        (sums, back_second, sent_second, forward, model, other, times, far, kept),
+        (V, V, V, V, V, V, V, V, H),
         [bf16(*forward.shape), f32(*slab)],
         [H, H],
         scratch=[V((count, *slab), jnp.bfloat16), V(slab, jnp.float32), dma((layers + 1,))],
-        aliases={7: 0},
+        aliases={8: 0},
     )
     return adjoint, gradient
 

time: 40.2 us -> 39.9 us (level)
  waiting for transfers between devices: 12.3 us -> 11.6 us
  starting transfers between devices: 17.9 us -> 18.5 us
    ppermute x8, waiting for transfers between devices: 12.3 us -> 11.6 us  [swap(): return lax.ppermute(x, 'space', links)]
    ppermute x8, starting transfers between devices: 17.9 us -> 18.5 us  [swap(): return lax.ppermute(x, 'space', links)]
  transfers between devices with their start and end apart: 8 -> 8, of which waited for: 4 -> 3; matrix products, arithmetic and copies ran while one was open for 0% -> 0% of each run, Pallas kernels for 17% -> 17%
where the time goes in v6:
time: 39.9 us; the launch traced here: 39.8 us
  starting transfers between devices  18.5 us (46%)
  waiting for transfers between devices  11.6 us (29%)
  Pallas kernels  7.88 us (20%)
  local copies, waits for them, and re-layouts  1.07 us (3%)
  between operations  0.76 us (2%)
    ppermute x8, starting transfers between devices, swap(): return lax.ppermute(x, 'space', links)  18.5 us
    ppermute x8, waiting for transfers between devices, swap(): return lax.ppermute(x, 'space', links)  11.6 us
    pallas_call x9, Pallas kernels, call(): pl.pallas_call(kernel, out_shape=out_shapes if several else out_shapes[0]...  7.88 us
    unnamed x14, local copies, waits for them, and re-layouts  1.07 us
  transfers between devices with their start and end apart: 8, of which 3 were waited for; matrix products, arithmetic and copies ran while one was open for 0% of the time, Pallas kernels for 17%

profile of v6, /device:TPU:0, one launch (start us, length us, event | category | flops | bytes accessed | tf_op | source)
XLA Modules:
  0.0 39.8 jit_solution(16674725845634913645)
XLA Ops:
  0.6 5.5 %collective-permute-start = (f32[4,64,128]{2,1,0:T(8,128)}, f32[4,64,128]{2,1,0:T(8,128)S(1)}, u32[]{:S(2)}, u32[]{:S(2)}) collective-permute-start(f32[4,64,128]{2,1,0:T(8,128)} %model.5), channel_id=1, source_target_pairs={{1,2},{2,1},{3,4},{4,3},{5,6},{6,5},{7,8},{8,7},{9,10},{10,9},{11,... | collective-permute-start | bytes 393224 | tf_op jit(solution)/shard_map/ppermute | solution.py:530
  6.1 0.0 copy-start
  6.1 1.0 %copy-done = bf16[8,4,64,128]{3,2,1,0:T(8,128)(2,1)S(1)} copy-done((bf16[8,4,64,128]{3,2,1,0:T(8,128)(2,1)S(1)}, bf16[8,4,64,128]{3,2,1,0:T(8,128)(2,1)}, u32[]{:S(2)}) %copy-start) | copy-done | bytes 524312
  7.2 0.0 copy-start.1
  7.2 0.0 copy-start.2
  7.2 0.0 copy-start.3
  7.2 0.0 copy-start.4
  7.2 0.0 copy-start.5
  7.2 0.0 copy-start.6
  7.2 0.1 collective-permute-start.1
  7.3 1.8 %collective-permute-done.other = f32[4,64,128]{2,1,0:T(8,128)S(1)} collective-permute-done((f32[4,64,128]{2,1,0:T(8,128)}, f32[4,64,128]{2,1,0:T(8,128)S(1)}, u32[]{:S(2)}, u32[]{:S(2)}) %collective-permute-start) | collective-permute-done | bytes 131104 | tf_op jit(solution)/shard_map/ppermute | solution.py:530
  9.1 0.0 collective-permute-start.5
  9.1 0.0 copy-done.1
  9.1 0.0 copy-done.2
  9.1 0.0 copy-done.3
  9.1 0.3 shard_map.77
  9.5 4.5 %collective-permute-start.2 = (f32[12,64,128]{2,1,0:T(8,128)S(1)}, f32[12,64,128]{2,1,0:T(8,128)S(1)}, u32[]{:S(2)}, u32[]{:S(2)}) collective-permute-start(f32[12,64,128]{2,1,0:T(8,128)S(1)} %get-tuple-element.20), channel_id=1, source_target_pairs={{1,2},{2,1},{3,4},{4,3},{5,6},{6,5},{7,8},{8,7},{9,10},{10,9},{11,... | collective-permute-start | bytes 1179656 | tf_op jit(solution)/shard_map/ppermute | solution.py:530
  14.0 0.0 copy-done.4
  14.0 0.0 copy-done.5
  14.0 0.0 copy-done.6
  14.0 1.2 %shard_map.79 = (f32[4,8,64,128]{3,2,1,0:T(8,128)S(1)}, f32[8]{0:T(128)S(1)}) custom-call(s32[8]{0:T(128)S(1)} %copy-done.6, f32[8,8,256]{2,1,0:T(8,128)S(1)} %copy-done.4, s32[1,256]{1,0:T(1,128)S(1)} %bitcast.1, f32[7,8,64,128]{3,2,1,0:T(8,128)S(1)} %get-tuple-element.17.coefs), custom_call_target="tpu_custom_call" | custom-call | flops 1000000000 | bytes 3000000 | tf_op jit(solution)/shard_map/pallas_call | solution.py:497
  15.2 0.0 collective-permute-done.5.beside
  15.2 0.6 %shard_map.83 = (f32[4,64,128]{2,1,0:T(8,128)S(1)}, f32[4,64,128]{2,1,0:T(8,128)S(1)}, f32[8,64,128]{2,1,0:T(8,128)S(1)}) custom-call(f32[8]{0:T(128)S(1)} %get-tuple-element.25.weights, f32[4,64,128]{2,1,0:T(8,128)S(1)} %copy-done.3, f32[4,64,128]{2,1,0:T(8,128)S(1)} %collective-permute-done.5.beside), custom_call_target="tpu_custom_call" | custom-call | flops 1000000000 | bytes 3000000 | tf_op jit(solution)/shard_map/pallas_call | solution.py:497
  15.8 0.1 collective-permute-start.6
  15.9 0.0 collective-permute-done.1.got
  15.9 1.6 %shard_map.80 = (f32[2,4,64,128]{3,2,1,0:T(8,128)S(1)}, f32[8,64,128]{2,1,0:T(8,128)S(1)}) custom-call(f32[7,8,64,128]{3,2,1,0:T(8,128)S(1)} %get-tuple-element.17.coefs, f32[2,4,64,128]{3,2,1,0:T(8,128)S(1)} %collective-permute-done.1.got, bf16[8,4,64,128]{3,2,1,0:T(8,128)(2,1)S(1)} %copy-done.1, f32[4,8,64,128]{3,2,1,0:T(8,128)S(1)} %get-tuple-element.18.rhs), custom_call_target="tpu_custom_call" | custom-call | flops 3000000000 | bytes 9000000 | tf_op jit(solution)/shard_map/pallas_call | solution.py:497
  17.5 3.4 %collective-permute-start.3 = (f32[8,64,128]{2,1,0:T(8,128)S(1)}, f32[8,64,128]{2,1,0:T(8,128)S(1)}, u32[]{:S(2)}, u32[]{:S(2)}) collective-permute-start(f32[8,64,128]{2,1,0:T(8,128)S(1)} %get-tuple-element.21.sent_first), channel_id=1, source_target_pairs={{1,2},{2,1},{3,4},{4,3},{5,6},{6,5},{7,8},{8,7},{9,10},{10,9},{11,... | collective-permute-start | bytes 786440 | tf_op jit(solution)/shard_map/ppermute | solution.py:530
  20.9 1.2 %collective-permute-done.2.got = f32[12,64,128]{2,1,0:T(8,128)S(1)} collective-permute-done((f32[12,64,128]{2,1,0:T(8,128)S(1)}, f32[12,64,128]{2,1,0:T(8,128)S(1)}, u32[]{:S(2)}, u32[]{:S(2)}) %collective-permute-start.2) | collective-permute-done | bytes 393248 | tf_op jit(solution)/shard_map/ppermute | solution.py:530
  22.1 1.6 %shard_map.81 = (f32[2,4,64,128]{3,2,1,0:T(8,128)S(1)}, f32[9,64,128]{2,1,0:T(8,128)S(1)}) custom-call(f32[7,8,64,128]{3,2,1,0:T(8,128)S(1)} %get-tuple-element.17.coefs, f32[12,64,128]{2,1,0:T(8,128)S(1)} %collective-permute-done.2.got, bf16[8,4,64,128]{3,2,1,0:T(8,128)(2,1)S(1)} %copy-done.1, f32[4,8,64,128]{3,2,1,0:T(8,128)S(1)} %get-tuple-element.18.rhs, ...), custom_call_target="tpu_custom_call" | custom-call | flops 3000000000 | bytes 9000000 | tf_op jit(solution)/shard_map/pallas_call | solution.py:497
  23.7 4.8 %collective-permute-start.4 = (f32[9,64,128]{2,1,0:T(8,128)S(1)}, f32[9,64,128]{2,1,0:T(8,128)S(1)}, u32[]{:S(2)}, u32[]{:S(2)}) collective-permute-start(f32[9,64,128]{2,1,0:T(8,128)S(1)} %get-tuple-element.24.sent), channel_id=1, source_target_pairs={{1,2},{2,1},{3,4},{4,3},{5,6},{6,5},{7,8},{8,7},{9,10},{10,9},{11,... | collective-permute-start | bytes 884744 | tf_op jit(solution)/shard_map/ppermute | solution.py:530
  28.5 0.0 collective-permute-done.6.near
  28.5 0.1 collective-permute-start.7
  28.6 0.0 collective-permute-done.3.back
  28.6 1.3 %shard_map.82 = (f32[4,4,64,128]{3,2,1,0:T(8,128)S(1)}, bf16[8,4,64,128]{3,2,1,0:T(8,128)(2,1)}) custom-call(bf16[8,4,64,128]{3,2,1,0:T(8,128)(2,1)S(1)} %copy-done.2, f32[2,4,64,128]{3,2,1,0:T(8,128)S(1)} %get-tuple-element.19.own_first, f32[2,4,64,128]{3,2,1,0:T(8,128)S(1)} %get-tuple-element.22.own_second.solved, ...), custom_call_target="tpu_custom_call" | custom-call | flops 2000000000 | bytes 6000000 | tf_op jit(solution)/shard_map/pallas_call | solution.py:497
  29.9 8.6 %collective-permute-done.7.far = f32[4,64,128]{2,1,0:T(8,128)S(1)} collective-permute-done((f32[4,64,128]{2,1,0:T(8,128)S(1)}, f32[4,64,128]{2,1,0:T(8,128)S(1)}, u32[]{:S(2)}, u32[]{:S(2)}) %collective-permute-start.7) | collective-permute-done | bytes 131104 | tf_op jit(solution)/shard_map/ppermute | solution.py:530
  38.6 0.0 collective-permute-done.4.back
  38.6 1.2 %shard_map.85 = (bf16[8,4,64,128]{3,2,1,0:T(8,128)(2,1)}, f32[4,64,128]{2,1,0:T(8,128)}) custom-call(f32[4,4,64,128]{3,2,1,0:T(8,128)S(1)} %get-tuple-element.23.sums, f32[9,64,128]{2,1,0:T(8,128)S(1)} %collective-permute-done.4.back, f32[9,64,128]{2,1,0:T(8,128)S(1)} %get-tuple-element.24.sent, ...), custom_call_target="tpu_custom_call", output_to_operand_aliasing={{0}: (8, {})} | custom-call | flops 1000000000 | bytes 3000000 | tf_op jit(solution)/shard_map/pallas_call | solution.py:497
  (2 shorter events, 0.0 us)
Async XLA Ops:
  0.6 8.5 %collective-permute-start = (f32[4,64,128]{2,1,0:T(8,128)}, f32[4,64,128]{2,1,0:T(8,128)S(1)}, u32[]{:S(2)}, u32[]{:S(2)}) collective-permute-start(f32[4,64,128]{2,1,0:T(8,128)} %model.5), channel_id=1, source_target_pairs={{1,2},{2,1},{3,4},{4,3},{5,6},{6,5},{7,8},{8,7},{9,10},{10,9},{11,... | collective-permute-start | bytes 393224 | tf_op jit(solution)/shard_map/ppermute | solution.py:530
  6.1 1.0 %copy-start = (bf16[8,4,64,128]{3,2,1,0:T(8,128)(2,1)S(1)}, bf16[8,4,64,128]{3,2,1,0:T(8,128)(2,1)}, u32[]{:S(2)}) copy-start(bf16[8,4,64,128]{3,2,1,0:T(8,128)(2,1)} %warm.7) | copy-start | bytes 1572868
  7.2 1.9 %copy-start.1 = (bf16[8,4,64,128]{3,2,1,0:T(8,128)(2,1)S(1)}, bf16[8,4,64,128]{3,2,1,0:T(8,128)(2,1)}, u32[]{:S(2)}) copy-start(bf16[8,4,64,128]{3,2,1,0:T(8,128)(2,1)} %warm.7) | copy-start | bytes 1572868
  7.2 1.9 %copy-start.2 = (bf16[8,4,64,128]{3,2,1,0:T(8,128)(2,1)S(1)}, bf16[8,4,64,128]{3,2,1,0:T(8,128)(2,1)}, u32[]{:S(2)}) copy-start(bf16[8,4,64,128]{3,2,1,0:T(8,128)(2,1)} %forward.7) | copy-start | bytes 1572868
  7.2 1.9 %copy-start.3 = (f32[4,64,128]{2,1,0:T(8,128)S(1)}, f32[4,64,128]{2,1,0:T(8,128)}, u32[]{:S(2)}) copy-start(f32[4,64,128]{2,1,0:T(8,128)} %model.5) | copy-start | bytes 393220
  7.2 6.8 %copy-start.4 = (f32[8,8,256]{2,1,0:T(8,128)S(1)}, f32[8,8,256]{2,1,0:T(8,128)}, u32[]{:S(2)}) copy-start(f32[8,8,256]{2,1,0:T(8,128)} %residual.1) | copy-start | bytes 196612
  7.2 6.8 %copy-start.5 = (s32[256]{0:T(256)S(1)}, s32[256]{0:T(256)}, u32[]{:S(2)}) copy-start(s32[256]{0:T(256)} %param.10) | copy-start | bytes 3076
  7.2 6.8 %copy-start.6 = (s32[8]{0:T(128)S(1)}, s32[8]{0:T(128)}, u32[]{:S(2)}) copy-start(s32[8]{0:T(128)} %order.1) | copy-start | bytes 100
  7.2 8.7 %collective-permute-start.1 = (f32[2,4,64,128]{3,2,1,0:T(8,128)S(1)}, f32[2,4,64,128]{3,2,1,0:T(8,128)S(1)}, u32[]{:S(2)}, u32[]{:S(2)}) collective-permute-start(f32[2,4,64,128]{3,2,1,0:T(8,128)S(1)} %shard_map.78), channel_id=1, source_target_pairs={{1,2},{2,1},{3,4},{4,3},{5,6},{6,5},{7,8},{8,7},{9,10},{10,9},{11,... | collective-permute-start | bytes 786440 | tf_op jit(solution)/shard_map/ppermute | solution.py:530
  9.1 6.1 %collective-permute-start.5 = (f32[4,64,128]{2,1,0:T(8,128)S(1)}, f32[4,64,128]{2,1,0:T(8,128)S(1)}, u32[]{:S(2)}, u32[]{:S(2)}) collective-permute-start(f32[4,64,128]{2,1,0:T(8,128)S(1)} %collective-permute-done.other), channel_id=1, source_target_pairs={{0,1},{1,0},{2,3},{3,2},{4,5},{5,4},{6,7},{7,6},{8,9},{9,8},{10,11... | collective-permute-start | bytes 393224 | tf_op jit(solution)/shard_map/ppermute | solution.py:530
  9.5 12.6 %collective-permute-start.2 = (f32[12,64,128]{2,1,0:T(8,128)S(1)}, f32[12,64,128]{2,1,0:T(8,128)S(1)}, u32[]{:S(2)}, u32[]{:S(2)}) collective-permute-start(f32[12,64,128]{2,1,0:T(8,128)S(1)} %get-tuple-element.20), channel_id=1, source_target_pairs={{1,2},{2,1},{3,4},{4,3},{5,6},{6,5},{7,8},{8,7},{9,10},{10,9},{11,... | collective-permute-start | bytes 1179656 | tf_op jit(solution)/shard_map/ppermute | solution.py:530
  15.8 12.7 %collective-permute-start.6 = (f32[8,64,128]{2,1,0:T(8,128)S(1)}, f32[8,64,128]{2,1,0:T(8,128)S(1)}, u32[]{:S(2)}, u32[]{:S(2)}) collective-permute-start(f32[8,64,128]{2,1,0:T(8,128)S(1)} %get-tuple-element.28), channel_id=1, source_target_pairs={{0,4},{1,5},{2,6},{3,7},{4,0},{5,1},{6,2},{7,3},{8,12},{9,13},{10,... | collective-permute-start | bytes 786440 | tf_op jit(solution)/shard_map/ppermute | solution.py:530
  17.5 11.1 %collective-permute-start.3 = (f32[8,64,128]{2,1,0:T(8,128)S(1)}, f32[8,64,128]{2,1,0:T(8,128)S(1)}, u32[]{:S(2)}, u32[]{:S(2)}) collective-permute-start(f32[8,64,128]{2,1,0:T(8,128)S(1)} %get-tuple-element.21.sent_first), channel_id=1, source_target_pairs={{1,2},{2,1},{3,4},{4,3},{5,6},{6,5},{7,8},{8,7},{9,10},{10,9},{11,... | collective-permute-start | bytes 786440 | tf_op jit(solution)/shard_map/ppermute | solution.py:530
  23.7 14.9 %collective-permute-start.4 = (f32[9,64,128]{2,1,0:T(8,128)S(1)}, f32[9,64,128]{2,1,0:T(8,128)S(1)}, u32[]{:S(2)}, u32[]{:S(2)}) collective-permute-start(f32[9,64,128]{2,1,0:T(8,128)S(1)} %get-tuple-element.24.sent), channel_id=1, source_target_pairs={{1,2},{2,1},{3,4},{4,3},{5,6},{6,5},{7,8},{8,7},{9,10},{10,9},{11,... | collective-permute-start | bytes 884744 | tf_op jit(solution)/shard_map/ppermute | solution.py:530
  28.5 10.1 %collective-permute-start.7 = (f32[4,64,128]{2,1,0:T(8,128)S(1)}, f32[4,64,128]{2,1,0:T(8,128)S(1)}, u32[]{:S(2)}, u32[]{:S(2)}) collective-permute-start(f32[4,64,128]{2,1,0:T(8,128)S(1)} %get-tuple-element.30), channel_id=1, source_target_pairs={{0,8},{1,9},{2,10},{3,11},{4,12},{5,13},{6,14},{7,15},{8,0},{9,1},... | collective-permute-start | bytes 393224 | tf_op jit(solution)/shard_map/ppermute | solution.py:530

commit v7 on v6

--- a/solution.py
+++ b/solution.py
@@ -206,9 +206,22 @@
 
 def pack(warm, first):
     tile = tile_of(lax.axis_index("space"))
-    count = first.shape[0]
+    half = warm.shape[0] // 2
+    for q in range(first.shape[0]):
+        first[q] = warm[half * (1 - tile) + q].astype(jnp.float32)
+
+
+def pack_second(warm, forward, parts, second):
+    tile = tile_of(lax.axis_index("space"))
+    half, layers = warm.shape[0] // 2, warm.shape[1]
+    count = (second.shape[0] - half) // layers
+    theirs = half * (1 - tile)
+    face = (layers - 1) * (1 - tile)
     for q in range(count):
-        first[q] = warm[2 * count * (1 - tile) + q].astype(jnp.float32)
+        source = theirs + half - count + q
+        second[layers * q : layers * (q + 1)] = warm[source].astype(jnp.float32)
+    for q in range(half):
+        second[count * layers + q] = forward[theirs + q, face].astype(jnp.float32)
 
 
 def inject(order, residual, electrodes, coefs, out, weights):
@@ -256,16 +269,9 @@
         out[q] = coefs[6] * total[:, q * rows_z : (q + 1) * rows_z].reshape(out.shape[1:])
 
 
-def prepare(model, other, warm, forward, coefs, second, sigma):
+def prepare(model, other, coefs, sigma):
     tile = tile_of(lax.axis_index("space"))
-    half = warm.shape[0] // 2
-    count, layers = half // 2, model.shape[0]
-    theirs = half * (1 - tile)
-    face = (layers - 1) * (1 - tile)
-    for q in range(count):
-        second[layers * q : layers * (q + 1)] = warm[theirs + count + q].astype(jnp.float32)
-    for q in range(half):
-        second[count * layers + q] = forward[theirs + q, face].astype(jnp.float32)
+    layers = model.shape[0]
     full = 2 * layers
     shape = model.shape[1:]
     for i in range(layers):
@@ -360,7 +366,8 @@
 
 def solve_first(coefs, got, warm, rhs, own, sent, start, rest, lam, mine):
     count, layers = own.shape[:2]
-    load_start(warm, 2 * count * tile_of(lax.axis_index("space")), got, start)
+    half = warm.shape[0] // 2
+    load_start(warm, half * tile_of(lax.axis_index("space")), got, start)
     sweeps(coefs, rhs, 0, start, rest, lam, mine)
     for q in range(count):
         own[q] = lam[q, :layers]
@@ -370,18 +377,19 @@
 def solve_second(coefs, got, warm, rhs, forward, own_first, sent_first, own, sent, start, rest, lam, mine):
     count, layers = own.shape[:2]
     tile = tile_of(lax.axis_index("space"))
-    source = 2 * count * tile
-    load_start(warm, source + count, got, start)
-    sweeps(coefs, rhs, count, start, rest, lam, mine)
+    half = warm.shape[0] // 2
+    early, source = half - count, half * tile
+    load_start(warm, source + early, got, start)
+    sweeps(coefs, rhs, early, start, rest, lam, mine)
     near = (layers - 1) * (1 - tile)
     far = (layers - 1) * tile
     total = None
-    for q in range(2 * count):
+    for q in range(half):
         slope = forward[source + q, near].astype(jnp.float32) - got[count * layers + q]
-        if q < count:
+        if q < early:
             drop = own_first[q, near] - sent_first[layers * q + far]
         else:
-            drop = lam[q - count, near] - lam[q - count, layers + far]
+            drop = lam[q - early, near] - lam[q - early, layers + far]
         total = slope * drop if total is None else total + slope * drop
     for q in range(count):
         own[q] = lam[q, :layers]
@@ -409,25 +417,28 @@
 
 
 def gather_terms(forward, own_first, own_second, back, sums, adjoint, rounded, sems):
-    count, layers = own_first.shape[:2]
+    early, layers = own_first.shape[:2]
+    half = early + own_second.shape[0]
     tile = tile_of(lax.axis_index("space"))
-    mine, theirs = 2 * count * tile, 2 * count * (1 - tile)
-    for q in range(count):
-        rounded[q] = own_first[q].astype(jnp.bfloat16)
-        rounded[count + q] = own_second[q].astype(jnp.bfloat16)
-        rounded[2 * count + q] = back[layers * q : layers * (q + 1)].astype(jnp.bfloat16)
+    mine, theirs = half * tile, half * (1 - tile)
+    rounded[:early] = own_first[...].astype(jnp.bfloat16)
+    rounded[early:half] = own_second[...].astype(jnp.bfloat16)
+    for q in range(early):
+        rounded[half + q] = back[layers * q : layers * (q + 1)].astype(jnp.bfloat16)
     copies = [
-        pltpu.make_async_copy(rounded.at[: 2 * count], adjoint.at[pl.ds(mine, 2 * count)], sems.at[0]),
-        pltpu.make_async_copy(rounded.at[2 * count :], adjoint.at[pl.ds(theirs, count)], sems.at[1]),
+        pltpu.make_async_copy(rounded.at[:half], adjoint.at[pl.ds(mine, half)], sems.at[0]),
+        pltpu.make_async_copy(rounded.at[half:], adjoint.at[pl.ds(theirs, early)], sems.at[1]),
     ]
     for copy in copies:
         copy.start()
     sums[...] = jnp.zeros(sums.shape, jnp.float32)
     pairs = []
-    for q in range(count):
-        pairs.append((mine + q, lambda i, q=q: own_first[q, i]))
-        pairs.append((mine + count + q, lambda i, q=q: own_second[q, i]))
-        pairs.append((theirs + q, lambda i, q=q: back[layers * q + i]))
+    for q in range(half):
+        if q < early:
+            pairs.append((mine + q, lambda i, q=q: own_first[q, i]))
+            pairs.append((theirs + q, lambda i, q=q: back[layers * q + i]))
+        else:
+            pairs.append((mine + q, lambda i, q=q: own_second[q - early, i]))
     pairs = [(lambda i, s=s: forward[s, i].astype(jnp.float32), lam) for s, lam in pairs]
     data_sums(pairs, layers, sums.at[0], sums.at[1], sums.at[2], sums.at[3])
     for copy in copies:
@@ -437,7 +448,8 @@
 def finish(sums, back, sent, forward, model, other, times, far, kept, adjoint, gradient, rounded, result, sems):
     tile = tile_of(lax.axis_index("space"))
     count, layers = rounded.shape[:2]
-    theirs = 2 * count * (1 - tile) + count
+    half = forward.shape[0] // 2
+    theirs = half * (1 - tile) + half - count
     for q in range(count):
         rounded[q] = back[layers * q : layers * (q + 1)].astype(jnp.bfloat16)
     copies = [pltpu.make_async_copy(rounded, adjoint.at[pl.ds(theirs, count)], sems.at[layers])]
@@ -518,7 +530,9 @@
 
 def paired(model, forward, warm_start, residual_data, electrodes, survey_order):
     sources, layers, ny, nz = forward.shape
-    half, count = sources // 2, sources // 4
+    half = sources // 2
+    late = (half + 3) // 4
+    early = half - late
     full = 2 * layers
     devices = lax.axis_size("space")
     pairs = []
@@ -532,14 +546,14 @@
     dma = pltpu.SemaphoreType.DMA
     slab = (layers, ny, nz)
     other = swap(model)
-    first = call(pack, (warm_start,), (V,), [f32(count, *slab)])
+    first = call(pack, (warm_start,), (V,), [f32(early, *slab)])
     got_first = swap(first)
     beside = swap(other, 1)
-    coefs, second = call(
+    coefs = call(
         prepare,
-        (model, other, warm_start, forward),
-        (V, V, V, V),
-        [f32(7, full, ny, nz), f32(count * layers + half, ny, nz)],
+        (model, other),
+        (V, V),
+        [f32(7, full, ny, nz)],
         scratch=[V((full, ny, nz), jnp.float32)],
     )
     rhs, weights_time = call(
@@ -549,10 +563,11 @@
         [f32(half, full, ny, nz), f32(8)],
         [V, S],
     )
-    got_second = swap(second)
-    field = V((count, full, ny, nz), jnp.float32)
-    fields = [field, field, field, V((2, count, full, ny, nz), jnp.float32)]
-    block = f32(count, *slab)
+
+    def fields(count):
+        field = V((count, full, ny, nz), jnp.float32)
+        return [field, field, field, V((2, count, full, ny, nz), jnp.float32)]
+
     time, opposite, parts = call(
         split_time,
         (weights_time, model, beside),
@@ -560,12 +575,16 @@
         [f32(*slab), f32(*slab), f32(2 * layers, ny, nz)],
     )
     near = swap(parts, 4)
+    second = call(
+        pack_second, (warm_start, forward, parts), (V, V, V), [f32(late * layers + half, ny, nz)]
+    )
+    got_second = swap(second)
     own_first, sent_first = call(
         solve_first,
         (coefs, got_first, warm_start, rhs),
         (V, V, V, V),
-        [block, f32(count * layers, ny, nz)],
-        scratch=fields,
+        [f32(early, *slab), f32(early * layers, ny, nz)],
+        scratch=fields(early),
         micros=3,
     )
     back_first = swap(sent_first)
@@ -573,8 +592,8 @@
         solve_second,
         (coefs, got_second, warm_start, rhs, forward, own_first, sent_first),
         (V, V, V, V, V, V, V),
-        [block, f32(count * layers + 1, ny, nz)],
-        scratch=fields,
+        [f32(late, *slab), f32(late * layers + 1, ny, nz)],
+        scratch=fields(late),
         micros=3,
     )
     back_second = swap(sent_second)
@@ -586,8 +605,8 @@
         (V, V, V, V),
         [f32(4, *slab), bf16(*forward.shape)],
         [V, H],
-        scratch=[V((3 * count, *slab), jnp.bfloat16), dma((2,))],
-        micros=2,
+        scratch=[V((half + early, *slab), jnp.bfloat16), dma((2,))],
+        micros=1,
     )
     adjoint, gradient = call(
         finish,
@@ -595,7 +614,7 @@
         (V, V, V, V, V, V, V, V, H),
         [bf16(*forward.shape), f32(*slab)],
         [H, H],
-        scratch=[V((count, *slab), jnp.bfloat16), V(slab, jnp.float32), dma((layers + 1,))],
+        scratch=[V((late, *slab), jnp.bfloat16), V(slab, jnp.float32), dma((layers + 1,))],
         aliases={8: 0},
     )
     return adjoint, gradient

time: 39.9 us -> 41.1 us (1.030)
  waiting for transfers between devices: 11.6 us -> 13.3 us
  starting transfers between devices: 18.5 us -> 18 us
    ppermute x8, waiting for transfers between devices: 11.6 us -> 13.3 us  [swap(): return lax.ppermute(x, 'space', links)]
    ppermute x8, starting transfers between devices: 18.5 us -> 18 us  [swap(): return lax.ppermute(x, 'space', links)]
    pallas_call x9 -> x10, Pallas kernels: 7.88 us -> 7.77 us  [call(): pl.pallas_call(kernel, out_shape=out_shapes if several else out_shapes[0]...]
  transfers between devices with their start and end apart: 8 -> 8, of which waited for: 3 -> 4; matrix products, arithmetic and copies ran while one was open for 0% -> 0% of each run, Pallas kernels for 17% -> 17%
where the time goes in v7:
time: 41.1 us; the launch traced here: 41 us
  starting transfers between devices  18 us (44%)
  waiting for transfers between devices  13.3 us (32%)
  Pallas kernels  7.77 us (19%)
  local copies, waits for them, and re-layouts  1.08 us (3%)
  between operations  0.78 us (2%)
    ppermute x8, starting transfers between devices, swap(): return lax.ppermute(x, 'space', links)  18 us
    ppermute x8, waiting for transfers between devices, swap(): return lax.ppermute(x, 'space', links)  13.3 us
    pallas_call x10, Pallas kernels, call(): pl.pallas_call(kernel, out_shape=out_shapes if several else out_shapes[0]...  7.77 us
    unnamed x14, local copies, waits for them, and re-layouts  1.08 us
  transfers between devices with their start and end apart: 8, of which 4 were waited for; matrix products, arithmetic and copies ran while one was open for 0% of the time, Pallas kernels for 17%

profile of v7, /device:TPU:0, one launch (start us, length us, event | category | flops | bytes accessed | tf_op | source)
XLA Modules:
  0.0 41.0 jit_solution(11051765237921889343)
XLA Ops:
  0.6 5.5 %collective-permute-start = (f32[4,64,128]{2,1,0:T(8,128)}, f32[4,64,128]{2,1,0:T(8,128)S(1)}, u32[]{:S(2)}, u32[]{:S(2)}) collective-permute-start(f32[4,64,128]{2,1,0:T(8,128)} %model.5), channel_id=1, source_target_pairs={{1,2},{2,1},{3,4},{4,3},{5,6},{6,5},{7,8},{8,7},{9,10},{10,9},{11,... | collective-permute-start | bytes 393224 | tf_op jit(solution)/shard_map/ppermute | solution.py:544
  6.1 0.0 copy-start
  6.1 1.0 %copy-done = bf16[8,4,64,128]{3,2,1,0:T(8,128)(2,1)S(1)} copy-done((bf16[8,4,64,128]{3,2,1,0:T(8,128)(2,1)S(1)}, bf16[8,4,64,128]{3,2,1,0:T(8,128)(2,1)}, u32[]{:S(2)}) %copy-start) | copy-done | bytes 524312
  7.2 0.0 copy-start.3
  7.2 0.0 copy-start.4
  7.2 0.0 copy-start.5
  7.2 0.0 copy-start.6
  7.2 0.1 collective-permute-start.1
  7.3 1.8 %collective-permute-done.other = f32[4,64,128]{2,1,0:T(8,128)S(1)} collective-permute-done((f32[4,64,128]{2,1,0:T(8,128)}, f32[4,64,128]{2,1,0:T(8,128)S(1)}, u32[]{:S(2)}, u32[]{:S(2)}) %collective-permute-start) | collective-permute-done | bytes 131104 | tf_op jit(solution)/shard_map/ppermute | solution.py:544
  9.1 0.0 collective-permute-start.2
  9.1 0.0 copy-done.3
  9.1 0.3 shard_map.77.coefs
  9.4 0.0 copy-done.4
  9.4 0.0 copy-done.5
  9.4 0.0 copy-done.6
  9.5 1.2 %shard_map.79 = (f32[4,8,64,128]{3,2,1,0:T(8,128)S(1)}, f32[8]{0:T(128)S(1)}) custom-call(s32[8]{0:T(128)S(1)} %copy-done.6, f32[8,8,256]{2,1,0:T(8,128)S(1)} %copy-done.4, s32[1,256]{1,0:T(1,128)S(1)} %bitcast.1, f32[7,8,64,128]{3,2,1,0:T(8,128)S(1)} %shard_map.77.coefs), custom_call_target="tpu_custom_call" | custom-call | flops 1000000000 | bytes 3000000 | tf_op jit(solution)/shard_map/pallas_call | solution.py:509
  10.7 0.0 collective-permute-done.2.beside
  10.7 0.0 copy-start.1
  10.7 0.0 copy-start.2
  10.7 0.6 %shard_map.81 = (f32[4,64,128]{2,1,0:T(8,128)S(1)}, f32[4,64,128]{2,1,0:T(8,128)S(1)}, f32[8,64,128]{2,1,0:T(8,128)S(1)}) custom-call(f32[8]{0:T(128)S(1)} %get-tuple-element.17.weights, f32[4,64,128]{2,1,0:T(8,128)S(1)} %copy-done.3, f32[4,64,128]{2,1,0:T(8,128)S(1)} %collective-permute-done.2.beside), custom_call_target="tpu_custom_call" | custom-call | flops 1000000000 | bytes 3000000 | tf_op jit(solution)/shard_map/pallas_call | solution.py:509
  11.3 4.9 %collective-permute-start.6 = (f32[8,64,128]{2,1,0:T(8,128)S(1)}, f32[8,64,128]{2,1,0:T(8,128)S(1)}, u32[]{:S(2)}, u32[]{:S(2)}) collective-permute-start(f32[8,64,128]{2,1,0:T(8,128)S(1)} %get-tuple-element.18.parts), channel_id=1, source_target_pairs={{0,4},{1,5},{2,6},{3,7},{4,0},{5,1},{6,2},{7,3},{8,12},{9,13},{10,... | collective-permute-start | bytes 786440 | tf_op jit(solution)/shard_map/ppermute | solution.py:544
  16.3 0.0 copy-done.1
  16.3 0.0 copy-done.2
  16.3 0.1 collective-permute-start.3
  16.4 1.0 %collective-permute-done.1.got = f32[3,4,64,128]{3,2,1,0:T(8,128)S(1)} collective-permute-done((f32[3,4,64,128]{3,2,1,0:T(8,128)S(1)}, f32[3,4,64,128]{3,2,1,0:T(8,128)S(1)}, u32[]{:S(2)}, u32[]{:S(2)}) %collective-permute-start.1) | collective-permute-done | bytes 393248 | tf_op jit(solution)/shard_map/ppermute | solution.py:544
  17.4 2.3 %shard_map.80 = (f32[3,4,64,128]{3,2,1,0:T(8,128)S(1)}, f32[12,64,128]{2,1,0:T(8,128)S(1)}) custom-call(f32[7,8,64,128]{3,2,1,0:T(8,128)S(1)} %shard_map.77.coefs, f32[3,4,64,128]{3,2,1,0:T(8,128)S(1)} %collective-permute-done.1.got, bf16[8,4,64,128]{3,2,1,0:T(8,128)(2,1)S(1)} %copy-done.1, f32[4,8,64,128]{3,2,1,0:T(8,128)S(1)} %get-tuple-element.15.rhs), custom_call_target="tpu_custom_call" | custom-call | flops 3000000000 | bytes 9000000 | tf_op jit(solution)/shard_map/pallas_call | solution.py:509
  19.8 3.4 %collective-permute-start.4 = (f32[12,64,128]{2,1,0:T(8,128)S(1)}, f32[12,64,128]{2,1,0:T(8,128)S(1)}, u32[]{:S(2)}, u32[]{:S(2)}) collective-permute-start(f32[12,64,128]{2,1,0:T(8,128)S(1)} %get-tuple-element.19.sent_first), channel_id=1, source_target_pairs={{1,2},{2,1},{3,4},{4,3},{5,6},{6,5},{7,8},{8,7},{9,10},{10,9},{11,... | collective-permute-start | bytes 1179656 | tf_op jit(solution)/shard_map/ppermute | solution.py:544
  23.2 2.6 %collective-permute-done.3.got = f32[8,64,128]{2,1,0:T(8,128)S(1)} collective-permute-done((f32[8,64,128]{2,1,0:T(8,128)S(1)}, f32[8,64,128]{2,1,0:T(8,128)S(1)}, u32[]{:S(2)}, u32[]{:S(2)}) %collective-permute-start.3) | collective-permute-done | bytes 262176 | tf_op jit(solution)/shard_map/ppermute | solution.py:544
  25.8 0.8 %shard_map.83 = (f32[1,4,64,128]{3,2,1,0:T(8,128)S(1)}, f32[5,64,128]{2,1,0:T(8,128)S(1)}) custom-call(f32[7,8,64,128]{3,2,1,0:T(8,128)S(1)} %shard_map.77.coefs, f32[8,64,128]{2,1,0:T(8,128)S(1)} %collective-permute-done.3.got, bf16[8,4,64,128]{3,2,1,0:T(8,128)(2,1)S(1)} %copy-done.1, f32[4,8,64,128]{3,2,1,0:T(8,128)S(1)} %get-tuple-element.15.rhs, ...), custom_call_target="tpu_custom_call" | custom-call | flops 3000000000 | bytes 9000000 | tf_op jit(solution)/shard_map/pallas_call | solution.py:509
  26.6 3.8 %collective-permute-start.5 = (f32[5,64,128]{2,1,0:T(8,128)S(1)}, f32[5,64,128]{2,1,0:T(8,128)S(1)}, u32[]{:S(2)}, u32[]{:S(2)}) collective-permute-start(f32[5,64,128]{2,1,0:T(8,128)S(1)} %get-tuple-element.22.sent), channel_id=1, source_target_pairs={{1,2},{2,1},{3,4},{4,3},{5,6},{6,5},{7,8},{8,7},{9,10},{10,9},{11,... | collective-permute-start | bytes 491528 | tf_op jit(solution)/shard_map/ppermute | solution.py:544
  30.4 0.0 collective-permute-done.6.near
  30.4 0.1 collective-permute-start.7
  30.5 0.0 collective-permute-done.4.back
  30.5 1.4 %shard_map.84 = (f32[4,4,64,128]{3,2,1,0:T(8,128)S(1)}, bf16[8,4,64,128]{3,2,1,0:T(8,128)(2,1)}) custom-call(bf16[8,4,64,128]{3,2,1,0:T(8,128)(2,1)S(1)} %copy-done.2, f32[3,4,64,128]{3,2,1,0:T(8,128)S(1)} %get-tuple-element.16.own_first, f32[1,4,64,128]{3,2,1,0:T(8,128)S(1)} %get-tuple-element.20.own_second.solved, ...), custom_call_target="tpu_custom_call" | custom-call | flops 1000000000 | bytes 3000000 | tf_op jit(solution)/shard_map/pallas_call | solution.py:509
  32.0 8.0 %collective-permute-done.7.far = f32[4,64,128]{2,1,0:T(8,128)S(1)} collective-permute-done((f32[4,64,128]{2,1,0:T(8,128)S(1)}, f32[4,64,128]{2,1,0:T(8,128)S(1)}, u32[]{:S(2)}, u32[]{:S(2)}) %collective-permute-start.7) | collective-permute-done | bytes 131104 | tf_op jit(solution)/shard_map/ppermute | solution.py:544
  40.0 0.0 collective-permute-done.5.back
  40.0 1.0 %shard_map.86 = (bf16[8,4,64,128]{3,2,1,0:T(8,128)(2,1)}, f32[4,64,128]{2,1,0:T(8,128)}) custom-call(f32[4,4,64,128]{3,2,1,0:T(8,128)S(1)} %get-tuple-element.21.sums, f32[5,64,128]{2,1,0:T(8,128)S(1)} %collective-permute-done.5.back, f32[5,64,128]{2,1,0:T(8,128)S(1)} %get-tuple-element.22.sent, ...), custom_call_target="tpu_custom_call", output_to_operand_aliasing={{0}: (8, {})} | custom-call | flops 1000000000 | bytes 3000000 | tf_op jit(solution)/shard_map/pallas_call | solution.py:509
  (3 shorter events, 0.1 us)
Async XLA Ops:
  0.6 8.5 %collective-permute-start = (f32[4,64,128]{2,1,0:T(8,128)}, f32[4,64,128]{2,1,0:T(8,128)S(1)}, u32[]{:S(2)}, u32[]{:S(2)}) collective-permute-start(f32[4,64,128]{2,1,0:T(8,128)} %model.5), channel_id=1, source_target_pairs={{1,2},{2,1},{3,4},{4,3},{5,6},{6,5},{7,8},{8,7},{9,10},{10,9},{11,... | collective-permute-start | bytes 393224 | tf_op jit(solution)/shard_map/ppermute | solution.py:544
  6.1 1.0 %copy-start = (bf16[8,4,64,128]{3,2,1,0:T(8,128)(2,1)S(1)}, bf16[8,4,64,128]{3,2,1,0:T(8,128)(2,1)}, u32[]{:S(2)}) copy-start(bf16[8,4,64,128]{3,2,1,0:T(8,128)(2,1)} %warm.7) | copy-start | bytes 1572868
  7.2 1.9 %copy-start.3 = (f32[4,64,128]{2,1,0:T(8,128)S(1)}, f32[4,64,128]{2,1,0:T(8,128)}, u32[]{:S(2)}) copy-start(f32[4,64,128]{2,1,0:T(8,128)} %model.5) | copy-start | bytes 393220
  7.2 2.2 %copy-start.4 = (f32[8,8,256]{2,1,0:T(8,128)S(1)}, f32[8,8,256]{2,1,0:T(8,128)}, u32[]{:S(2)}) copy-start(f32[8,8,256]{2,1,0:T(8,128)} %residual.1) | copy-start | bytes 196612
  7.2 2.2 %copy-start.5 = (s32[256]{0:T(256)S(1)}, s32[256]{0:T(256)}, u32[]{:S(2)}) copy-start(s32[256]{0:T(256)} %param.10) | copy-start | bytes 3076
  7.2 2.2 %copy-start.6 = (s32[8]{0:T(128)S(1)}, s32[8]{0:T(128)}, u32[]{:S(2)}) copy-start(s32[8]{0:T(128)} %order.1) | copy-start | bytes 100
  7.2 10.2 %collective-permute-start.1 = (f32[3,4,64,128]{3,2,1,0:T(8,128)S(1)}, f32[3,4,64,128]{3,2,1,0:T(8,128)S(1)}, u32[]{:S(2)}, u32[]{:S(2)}) collective-permute-start(f32[3,4,64,128]{3,2,1,0:T(8,128)S(1)} %shard_map.78), channel_id=1, source_target_pairs={{1,2},{2,1},{3,4},{4,3},{5,6},{6,5},{7,8},{8,7},{9,10},{10,9},{11,... | collective-permute-start | bytes 1179656 | tf_op jit(solution)/shard_map/ppermute | solution.py:544
  9.1 1.6 %collective-permute-start.2 = (f32[4,64,128]{2,1,0:T(8,128)S(1)}, f32[4,64,128]{2,1,0:T(8,128)S(1)}, u32[]{:S(2)}, u32[]{:S(2)}) collective-permute-start(f32[4,64,128]{2,1,0:T(8,128)S(1)} %collective-permute-done.other), channel_id=1, source_target_pairs={{0,1},{1,0},{2,3},{3,2},{4,5},{5,4},{6,7},{7,6},{8,9},{9,8},{10,11... | collective-permute-start | bytes 393224 | tf_op jit(solution)/shard_map/ppermute | solution.py:544
  10.7 5.6 %copy-start.1 = (bf16[8,4,64,128]{3,2,1,0:T(8,128)(2,1)S(1)}, bf16[8,4,64,128]{3,2,1,0:T(8,128)(2,1)}, u32[]{:S(2)}) copy-start(bf16[8,4,64,128]{3,2,1,0:T(8,128)(2,1)} %warm.7) | copy-start | bytes 1572868
  10.7 5.6 %copy-start.2 = (bf16[8,4,64,128]{3,2,1,0:T(8,128)(2,1)S(1)}, bf16[8,4,64,128]{3,2,1,0:T(8,128)(2,1)}, u32[]{:S(2)}) copy-start(bf16[8,4,64,128]{3,2,1,0:T(8,128)(2,1)} %forward.7) | copy-start | bytes 1572868
  11.3 19.1 %collective-permute-start.6 = (f32[8,64,128]{2,1,0:T(8,128)S(1)}, f32[8,64,128]{2,1,0:T(8,128)S(1)}, u32[]{:S(2)}, u32[]{:S(2)}) collective-permute-start(f32[8,64,128]{2,1,0:T(8,128)S(1)} %get-tuple-element.18.parts), channel_id=1, source_target_pairs={{0,4},{1,5},{2,6},{3,7},{4,0},{5,1},{6,2},{7,3},{8,12},{9,13},{10,... | collective-permute-start | bytes 786440 | tf_op jit(solution)/shard_map/ppermute | solution.py:544
  16.3 9.5 %collective-permute-start.3 = (f32[8,64,128]{2,1,0:T(8,128)S(1)}, f32[8,64,128]{2,1,0:T(8,128)S(1)}, u32[]{:S(2)}, u32[]{:S(2)}) collective-permute-start(f32[8,64,128]{2,1,0:T(8,128)S(1)} %shard_map.82), channel_id=1, source_target_pairs={{1,2},{2,1},{3,4},{4,3},{5,6},{6,5},{7,8},{8,7},{9,10},{10,9},{11,... | collective-permute-start | bytes 786440 | tf_op jit(solution)/shard_map/ppermute | solution.py:544
  19.8 10.8 %collective-permute-start.4 = (f32[12,64,128]{2,1,0:T(8,128)S(1)}, f32[12,64,128]{2,1,0:T(8,128)S(1)}, u32[]{:S(2)}, u32[]{:S(2)}) collective-permute-start(f32[12,64,128]{2,1,0:T(8,128)S(1)} %get-tuple-element.19.sent_first), channel_id=1, source_target_pairs={{1,2},{2,1},{3,4},{4,3},{5,6},{6,5},{7,8},{8,7},{9,10},{10,9},{11,... | collective-permute-start | bytes 1179656 | tf_op jit(solution)/shard_map/ppermute | solution.py:544
  26.6 13.4 %collective-permute-start.5 = (f32[5,64,128]{2,1,0:T(8,128)S(1)}, f32[5,64,128]{2,1,0:T(8,128)S(1)}, u32[]{:S(2)}, u32[]{:S(2)}) collective-permute-start(f32[5,64,128]{2,1,0:T(8,128)S(1)} %get-tuple-element.22.sent), channel_id=1, source_target_pairs={{1,2},{2,1},{3,4},{4,3},{5,6},{6,5},{7,8},{8,7},{9,10},{10,9},{11,... | collective-permute-start | bytes 491528 | tf_op jit(solution)/shard_map/ppermute | solution.py:544
  30.4 9.5 %collective-permute-start.7 = (f32[4,64,128]{2,1,0:T(8,128)S(1)}, f32[4,64,128]{2,1,0:T(8,128)S(1)}, u32[]{:S(2)}, u32[]{:S(2)}) collective-permute-start(f32[4,64,128]{2,1,0:T(8,128)S(1)} %get-tuple-element.26), channel_id=1, source_target_pairs={{0,8},{1,9},{2,10},{3,11},{4,12},{5,13},{6,14},{7,15},{8,0},{9,1},... | collective-permute-start | bytes 393224 | tf_op jit(solution)/shard_map/ppermute | solution.py:544

commit v8 on v7

--- a/solution.py
+++ b/solution.py
@@ -358,7 +358,7 @@
     parts[layers:] = weights[6] * here + weights[7] * there
 
 
-def join_time(time, opposite, near, solved, times, joined):
+def join_time(time, opposite, near, times, joined):
     layers = time.shape[0]
     times[...] = time[...] + near[:layers]
     joined[...] = opposite[...] + near[layers:]
@@ -416,7 +416,8 @@
         mass[i] = mass[i] + totals[3]
 
 
-def gather_terms(forward, own_first, own_second, back, sums, adjoint, rounded, sems):
+def gather_terms(forward, own_first, own_second, back, times, far, sums, adjoint, time, rounded, sems):
+    time[...] = times[...] + far[...]
     early, layers = own_first.shape[:2]
     half = early + own_second.shape[0]
     tile = tile_of(lax.axis_index("space"))
@@ -445,7 +446,7 @@
         copy.wait()
 
 
-def finish(sums, back, sent, forward, model, other, times, far, kept, adjoint, gradient, rounded, result, sems):
+def finish(sums, back, sent, forward, model, other, times, kept, adjoint, gradient, rounded, result, sems):
     tile = tile_of(lax.axis_index("space"))
     count, layers = rounded.shape[:2]
     half = forward.shape[0] // 2
@@ -492,7 +493,7 @@
         fall_y = jnp.where(in_y, value - after(value, 0), 0.0)
         fall_z = jnp.where(in_z, value - after(value, 1), 0.0)
         space = falls[i + 1] - falls[i] + (fall_y - before(fall_y, 0)) + (fall_z - before(fall_z, 1))
-        result[i] = space + (times[i] + far[i]) - jnp.exp(value) * (0.5 * terms + GROUND * mass)
+        result[i] = space + times[i] - jnp.exp(value) * (0.5 * terms + GROUND * mass)
         copies.append(pltpu.make_async_copy(result.at[i], gradient.at[i], sems.at[i]))
         copies[-1].start()
     for copy in copies:
@@ -588,6 +589,8 @@
         micros=3,
     )
     back_first = swap(sent_first)
+    times, joined = call(join_time, (time, opposite, near), (V, V, V), [f32(*slab), f32(*slab)], micros=1)
+    far = swap(joined, 8)
     own_second, sent_second = call(
         solve_second,
         (coefs, got_second, warm_start, rhs, forward, own_first, sent_first),
@@ -597,25 +600,23 @@
         micros=3,
     )
     back_second = swap(sent_second)
-    times, joined = call(join_time, (time, opposite, near, own_second), (V, V, V, V), [f32(*slab), f32(*slab)])
-    far = swap(joined, 8)
-    sums, kept = call(
+    sums, kept, time = call(
         gather_terms,
-        (forward, own_first, own_second, back_first),
-        (V, V, V, V),
-        [f32(4, *slab), bf16(*forward.shape)],
-        [V, H],
+        (forward, own_first, own_second, back_first, times, far),
+        (V, V, V, V, V, V),
+        [f32(4, *slab), bf16(*forward.shape), f32(*slab)],
+        [V, H, V],
         scratch=[V((half + early, *slab), jnp.bfloat16), dma((2,))],
         micros=1,
     )
     adjoint, gradient = call(
         finish,
-        (sums, back_second, sent_second, forward, model, other, times, far, kept),
-        (V, V, V, V, V, V, V, V, H),
+        (sums, back_second, sent_second, forward, model, other, time, kept),
+        (V, V, V, V, V, V, V, H),
         [bf16(*forward.shape), f32(*slab)],
         [H, H],
         scratch=[V((late, *slab), jnp.bfloat16), V(slab, jnp.float32), dma((layers + 1,))],
-        aliases={8: 0},
+        aliases={7: 0},
     )
     return adjoint, gradient
 

time: 41.1 us -> 38.5 us (0.937); the launches traced: 41 us -> 37.9 us
  waiting for transfers between devices: 13.3 us -> 7.97 us
  starting transfers between devices: 18 us -> 20.3 us
    ppermute x8, waiting for transfers between devices: 13.3 us -> 7.97 us  [swap(): return lax.ppermute(x, 'space', links)]
    ppermute x8, starting transfers between devices: 18 us -> 20.3 us  [swap(): return lax.ppermute(x, 'space', links)]
  transfers between devices with their start and end apart: 8 -> 8, of which waited for: 4 -> 4; matrix products, arithmetic and copies ran while one was open for 0% -> 0% of each run, Pallas kernels for 17% -> 18%
where the time goes in v8:
time: 38.5 us; the launch traced here: 37.9 us
  starting transfers between devices  20.3 us (53%)
  waiting for transfers between devices  7.97 us (21%)
  Pallas kernels  7.74 us (20%)
  local copies, waits for them, and re-layouts  1.08 us (3%)
  between operations  0.77 us (2%)
    ppermute x8, starting transfers between devices, swap(): return lax.ppermute(x, 'space', links)  20.3 us
    ppermute x8, waiting for transfers between devices, swap(): return lax.ppermute(x, 'space', links)  7.97 us
    pallas_call x10, Pallas kernels, call(): pl.pallas_call(kernel, out_shape=out_shapes if several else out_shapes[0]...  7.74 us
    unnamed x14, local copies, waits for them, and re-layouts  1.08 us
  transfers between devices with their start and end apart: 8, of which 4 were waited for; matrix products, arithmetic and copies ran while one was open for 0% of the time, Pallas kernels for 18%

profile of v8, /device:TPU:0, one launch (start us, length us, event | category | flops | bytes accessed | tf_op | source)
XLA Modules:
  0.0 37.9 jit_solution(10309484159057214416)
XLA Ops:
  0.6 5.5 %collective-permute-start = (f32[4,64,128]{2,1,0:T(8,128)}, f32[4,64,128]{2,1,0:T(8,128)S(1)}, u32[]{:S(2)}, u32[]{:S(2)}) collective-permute-start(f32[4,64,128]{2,1,0:T(8,128)} %model.5), channel_id=1, source_target_pairs={{1,2},{2,1},{3,4},{4,3},{5,6},{6,5},{7,8},{8,7},{9,10},{10,9},{11,... | collective-permute-start | bytes 393224 | tf_op jit(solution)/shard_map/ppermute | solution.py:545
  6.1 0.0 copy-start
  6.1 1.0 %copy-done = bf16[8,4,64,128]{3,2,1,0:T(8,128)(2,1)S(1)} copy-done((bf16[8,4,64,128]{3,2,1,0:T(8,128)(2,1)S(1)}, bf16[8,4,64,128]{3,2,1,0:T(8,128)(2,1)}, u32[]{:S(2)}) %copy-start) | copy-done | bytes 524312
  7.2 0.0 copy-start.3
  7.2 0.0 copy-start.4
  7.2 0.0 copy-start.5
  7.2 0.0 copy-start.6
  7.2 0.1 collective-permute-start.1
  7.3 1.8 %collective-permute-done.other = f32[4,64,128]{2,1,0:T(8,128)S(1)} collective-permute-done((f32[4,64,128]{2,1,0:T(8,128)}, f32[4,64,128]{2,1,0:T(8,128)S(1)}, u32[]{:S(2)}, u32[]{:S(2)}) %collective-permute-start) | collective-permute-done | bytes 131104 | tf_op jit(solution)/shard_map/ppermute | solution.py:545
  9.1 0.0 collective-permute-start.2
  9.1 0.0 copy-done.3
  9.1 0.3 shard_map.77.coefs
  9.4 0.0 copy-done.4
  9.4 0.0 copy-done.5
  9.4 0.0 copy-done.6
  9.5 1.2 %shard_map.79 = (f32[4,8,64,128]{3,2,1,0:T(8,128)S(1)}, f32[8]{0:T(128)S(1)}) custom-call(s32[8]{0:T(128)S(1)} %copy-done.6, f32[8,8,256]{2,1,0:T(8,128)S(1)} %copy-done.4, s32[1,256]{1,0:T(1,128)S(1)} %bitcast.1, f32[7,8,64,128]{3,2,1,0:T(8,128)S(1)} %shard_map.77.coefs), custom_call_target="tpu_custom_call" | custom-call | flops 1000000000 | bytes 3000000 | tf_op jit(solution)/shard_map/pallas_call | solution.py:510
  10.7 0.0 collective-permute-done.2.beside
  10.7 0.0 copy-start.1
  10.7 0.0 copy-start.2
  10.7 0.6 %shard_map.81 = (f32[4,64,128]{2,1,0:T(8,128)S(1)}, f32[4,64,128]{2,1,0:T(8,128)S(1)}, f32[8,64,128]{2,1,0:T(8,128)S(1)}) custom-call(f32[8]{0:T(128)S(1)} %get-tuple-element.18.weights, f32[4,64,128]{2,1,0:T(8,128)S(1)} %copy-done.3, f32[4,64,128]{2,1,0:T(8,128)S(1)} %collective-permute-done.2.beside), custom_call_target="tpu_custom_call" | custom-call | flops 1000000000 | bytes 3000000 | tf_op jit(solution)/shard_map/pallas_call | solution.py:510
  11.3 4.9 %collective-permute-start.5 = (f32[8,64,128]{2,1,0:T(8,128)S(1)}, f32[8,64,128]{2,1,0:T(8,128)S(1)}, u32[]{:S(2)}, u32[]{:S(2)}) collective-permute-start(f32[8,64,128]{2,1,0:T(8,128)S(1)} %get-tuple-element.19.parts), channel_id=1, source_target_pairs={{0,4},{1,5},{2,6},{3,7},{4,0},{5,1},{6,2},{7,3},{8,12},{9,13},{10,... | collective-permute-start | bytes 786440 | tf_op jit(solution)/shard_map/ppermute | solution.py:545
  16.3 0.0 copy-done.1
  16.3 0.0 copy-done.2
  16.3 0.1 collective-permute-start.3
  16.4 1.0 %collective-permute-done.1.got = f32[3,4,64,128]{3,2,1,0:T(8,128)S(1)} collective-permute-done((f32[3,4,64,128]{3,2,1,0:T(8,128)S(1)}, f32[3,4,64,128]{3,2,1,0:T(8,128)S(1)}, u32[]{:S(2)}, u32[]{:S(2)}) %collective-permute-start.1) | collective-permute-done | bytes 393248 | tf_op jit(solution)/shard_map/ppermute | solution.py:545
  17.4 2.3 %shard_map.80 = (f32[3,4,64,128]{3,2,1,0:T(8,128)S(1)}, f32[12,64,128]{2,1,0:T(8,128)S(1)}) custom-call(f32[7,8,64,128]{3,2,1,0:T(8,128)S(1)} %shard_map.77.coefs, f32[3,4,64,128]{3,2,1,0:T(8,128)S(1)} %collective-permute-done.1.got, bf16[8,4,64,128]{3,2,1,0:T(8,128)(2,1)S(1)} %copy-done.1, f32[4,8,64,128]{3,2,1,0:T(8,128)S(1)} %get-tuple-element.16.rhs), custom_call_target="tpu_custom_call" | custom-call | flops 3000000000 | bytes 9000000 | tf_op jit(solution)/shard_map/pallas_call | solution.py:510
  19.7 3.4 %collective-permute-start.4 = (f32[12,64,128]{2,1,0:T(8,128)S(1)}, f32[12,64,128]{2,1,0:T(8,128)S(1)}, u32[]{:S(2)}, u32[]{:S(2)}) collective-permute-start(f32[12,64,128]{2,1,0:T(8,128)S(1)} %get-tuple-element.20.sent_first), channel_id=1, source_target_pairs={{1,2},{2,1},{3,4},{4,3},{5,6},{6,5},{7,8},{8,7},{9,10},{10,9},{11,... | collective-permute-start | bytes 1179656 | tf_op jit(solution)/shard_map/ppermute | solution.py:545
  23.2 0.0 collective-permute-done.5.near
  23.2 2.4 %collective-permute-start.6 = (f32[4,64,128]{2,1,0:T(8,128)S(1)}, f32[4,64,128]{2,1,0:T(8,128)S(1)}, u32[]{:S(2)}, u32[]{:S(2)}) collective-permute-start(f32[4,64,128]{2,1,0:T(8,128)S(1)} %get-tuple-element.25), channel_id=1, source_target_pairs={{0,8},{1,9},{2,10},{3,11},{4,12},{5,13},{6,14},{7,15},{8,0},{9,1},... | collective-permute-start | bytes 393224 | tf_op jit(solution)/shard_map/ppermute | solution.py:545
  25.6 0.2 collective-permute-done.3.got
  25.8 0.8 %shard_map.83 = (f32[1,4,64,128]{3,2,1,0:T(8,128)S(1)}, f32[5,64,128]{2,1,0:T(8,128)S(1)}) custom-call(f32[7,8,64,128]{3,2,1,0:T(8,128)S(1)} %shard_map.77.coefs, f32[8,64,128]{2,1,0:T(8,128)S(1)} %collective-permute-done.3.got, bf16[8,4,64,128]{3,2,1,0:T(8,128)(2,1)S(1)} %copy-done.1, f32[4,8,64,128]{3,2,1,0:T(8,128)S(1)} %get-tuple-element.16.rhs, ...), custom_call_target="tpu_custom_call" | custom-call | flops 3000000000 | bytes 9000000 | tf_op jit(solution)/shard_map/pallas_call | solution.py:510
  26.6 3.8 %collective-permute-start.7 = (f32[5,64,128]{2,1,0:T(8,128)S(1)}, f32[5,64,128]{2,1,0:T(8,128)S(1)}, u32[]{:S(2)}, u32[]{:S(2)}) collective-permute-start(f32[5,64,128]{2,1,0:T(8,128)S(1)} %get-tuple-element.27.sent), channel_id=1, source_target_pairs={{1,2},{2,1},{3,4},{4,3},{5,6},{6,5},{7,8},{8,7},{9,10},{10,9},{11,... | collective-permute-start | bytes 491528 | tf_op jit(solution)/shard_map/ppermute | solution.py:545
  30.4 5.0 %collective-permute-done.6.far = f32[4,64,128]{2,1,0:T(8,128)S(1)} collective-permute-done((f32[4,64,128]{2,1,0:T(8,128)S(1)}, f32[4,64,128]{2,1,0:T(8,128)S(1)}, u32[]{:S(2)}, u32[]{:S(2)}) %collective-permute-start.6) | collective-permute-done | bytes 131104 | tf_op jit(solution)/shard_map/ppermute | solution.py:545
  35.4 0.0 collective-permute-done.4.back
  35.4 1.4 %shard_map.85 = (f32[4,4,64,128]{3,2,1,0:T(8,128)S(1)}, bf16[8,4,64,128]{3,2,1,0:T(8,128)(2,1)}, f32[4,64,128]{2,1,0:T(8,128)S(1)}) custom-call(bf16[8,4,64,128]{3,2,1,0:T(8,128)(2,1)S(1)} %copy-done.2, f32[3,4,64,128]{3,2,1,0:T(8,128)S(1)} %get-tuple-element.17.own_first, f32[1,4,64,128]{3,2,1,0:T(8,128)S(1)} %get-tuple-element.21.own_second, ...), custom_call_target="tpu_custom_call" | custom-call | flops 1000000000 | bytes 3000000 | tf_op jit(solution)/shard_map/pallas_call | solution.py:510
  36.9 0.0 collective-permute-done.7.back
  36.9 1.0 %shard_map.86 = (bf16[8,4,64,128]{3,2,1,0:T(8,128)(2,1)}, f32[4,64,128]{2,1,0:T(8,128)}) custom-call(f32[4,4,64,128]{3,2,1,0:T(8,128)S(1)} %get-tuple-element.26.sums, f32[5,64,128]{2,1,0:T(8,128)S(1)} %collective-permute-done.7.back, f32[5,64,128]{2,1,0:T(8,128)S(1)} %get-tuple-element.27.sent, ...), custom_call_target="tpu_custom_call", output_to_operand_aliasing={{0}: (7, {})} | custom-call | flops 1000000000 | bytes 3000000 | tf_op jit(solution)/shard_map/pallas_call | solution.py:510
  (3 shorter events, 0.1 us)
Async XLA Ops:
  0.6 8.5 %collective-permute-start = (f32[4,64,128]{2,1,0:T(8,128)}, f32[4,64,128]{2,1,0:T(8,128)S(1)}, u32[]{:S(2)}, u32[]{:S(2)}) collective-permute-start(f32[4,64,128]{2,1,0:T(8,128)} %model.5), channel_id=1, source_target_pairs={{1,2},{2,1},{3,4},{4,3},{5,6},{6,5},{7,8},{8,7},{9,10},{10,9},{11,... | collective-permute-start | bytes 393224 | tf_op jit(solution)/shard_map/ppermute | solution.py:545
  6.1 1.0 %copy-start = (bf16[8,4,64,128]{3,2,1,0:T(8,128)(2,1)S(1)}, bf16[8,4,64,128]{3,2,1,0:T(8,128)(2,1)}, u32[]{:S(2)}) copy-start(bf16[8,4,64,128]{3,2,1,0:T(8,128)(2,1)} %warm.7) | copy-start | bytes 1572868
  7.2 1.9 %copy-start.3 = (f32[4,64,128]{2,1,0:T(8,128)S(1)}, f32[4,64,128]{2,1,0:T(8,128)}, u32[]{:S(2)}) copy-start(f32[4,64,128]{2,1,0:T(8,128)} %model.5) | copy-start | bytes 393220
  7.2 2.2 %copy-start.4 = (f32[8,8,256]{2,1,0:T(8,128)S(1)}, f32[8,8,256]{2,1,0:T(8,128)}, u32[]{:S(2)}) copy-start(f32[8,8,256]{2,1,0:T(8,128)} %residual.1) | copy-start | bytes 196612
  7.2 2.2 %copy-start.5 = (s32[256]{0:T(256)S(1)}, s32[256]{0:T(256)}, u32[]{:S(2)}) copy-start(s32[256]{0:T(256)} %param.10) | copy-start | bytes 3076
  7.2 2.2 %copy-start.6 = (s32[8]{0:T(128)S(1)}, s32[8]{0:T(128)}, u32[]{:S(2)}) copy-start(s32[8]{0:T(128)} %order.1) | copy-start | bytes 100
  7.2 10.2 %collective-permute-start.1 = (f32[3,4,64,128]{3,2,1,0:T(8,128)S(1)}, f32[3,4,64,128]{3,2,1,0:T(8,128)S(1)}, u32[]{:S(2)}, u32[]{:S(2)}) collective-permute-start(f32[3,4,64,128]{3,2,1,0:T(8,128)S(1)} %shard_map.78), channel_id=1, source_target_pairs={{1,2},{2,1},{3,4},{4,3},{5,6},{6,5},{7,8},{8,7},{9,10},{10,9},{11,... | collective-permute-start | bytes 1179656 | tf_op jit(solution)/shard_map/ppermute | solution.py:545
  9.1 1.6 %collective-permute-start.2 = (f32[4,64,128]{2,1,0:T(8,128)S(1)}, f32[4,64,128]{2,1,0:T(8,128)S(1)}, u32[]{:S(2)}, u32[]{:S(2)}) collective-permute-start(f32[4,64,128]{2,1,0:T(8,128)S(1)} %collective-permute-done.other), channel_id=1, source_target_pairs={{0,1},{1,0},{2,3},{3,2},{4,5},{5,4},{6,7},{7,6},{8,9},{9,8},{10,11... | collective-permute-start | bytes 393224 | tf_op jit(solution)/shard_map/ppermute | solution.py:545
  10.7 5.6 %copy-start.1 = (bf16[8,4,64,128]{3,2,1,0:T(8,128)(2,1)S(1)}, bf16[8,4,64,128]{3,2,1,0:T(8,128)(2,1)}, u32[]{:S(2)}) copy-start(bf16[8,4,64,128]{3,2,1,0:T(8,128)(2,1)} %warm.7) | copy-start | bytes 1572868
  10.7 5.6 %copy-start.2 = (bf16[8,4,64,128]{3,2,1,0:T(8,128)(2,1)S(1)}, bf16[8,4,64,128]{3,2,1,0:T(8,128)(2,1)}, u32[]{:S(2)}) copy-start(bf16[8,4,64,128]{3,2,1,0:T(8,128)(2,1)} %forward.7) | copy-start | bytes 1572868
  11.3 11.8 %collective-permute-start.5 = (f32[8,64,128]{2,1,0:T(8,128)S(1)}, f32[8,64,128]{2,1,0:T(8,128)S(1)}, u32[]{:S(2)}, u32[]{:S(2)}) collective-permute-start(f32[8,64,128]{2,1,0:T(8,128)S(1)} %get-tuple-element.19.parts), channel_id=1, source_target_pairs={{0,4},{1,5},{2,6},{3,7},{4,0},{5,1},{6,2},{7,3},{8,12},{9,13},{10,... | collective-permute-start | bytes 786440 | tf_op jit(solution)/shard_map/ppermute | solution.py:545
  16.3 9.5 %collective-permute-start.3 = (f32[8,64,128]{2,1,0:T(8,128)S(1)}, f32[8,64,128]{2,1,0:T(8,128)S(1)}, u32[]{:S(2)}, u32[]{:S(2)}) collective-permute-start(f32[8,64,128]{2,1,0:T(8,128)S(1)} %shard_map.82), channel_id=1, source_target_pairs={{1,2},{2,1},{3,4},{4,3},{5,6},{6,5},{7,8},{8,7},{9,10},{10,9},{11,... | collective-permute-start | bytes 786440 | tf_op jit(solution)/shard_map/ppermute | solution.py:545
  19.7 15.7 %collective-permute-start.4 = (f32[12,64,128]{2,1,0:T(8,128)S(1)}, f32[12,64,128]{2,1,0:T(8,128)S(1)}, u32[]{:S(2)}, u32[]{:S(2)}) collective-permute-start(f32[12,64,128]{2,1,0:T(8,128)S(1)} %get-tuple-element.20.sent_first), channel_id=1, source_target_pairs={{1,2},{2,1},{3,4},{4,3},{5,6},{6,5},{7,8},{8,7},{9,10},{10,9},{11,... | collective-permute-start | bytes 1179656 | tf_op jit(solution)/shard_map/ppermute | solution.py:545
  23.2 12.2 %collective-permute-start.6 = (f32[4,64,128]{2,1,0:T(8,128)S(1)}, f32[4,64,128]{2,1,0:T(8,128)S(1)}, u32[]{:S(2)}, u32[]{:S(2)}) collective-permute-start(f32[4,64,128]{2,1,0:T(8,128)S(1)} %get-tuple-element.25), channel_id=1, source_target_pairs={{0,8},{1,9},{2,10},{3,11},{4,12},{5,13},{6,14},{7,15},{8,0},{9,1},... | collective-permute-start | bytes 393224 | tf_op jit(solution)/shard_map/ppermute | solution.py:545
  26.6 10.3 %collective-permute-start.7 = (f32[5,64,128]{2,1,0:T(8,128)S(1)}, f32[5,64,128]{2,1,0:T(8,128)S(1)}, u32[]{:S(2)}, u32[]{:S(2)}) collective-permute-start(f32[5,64,128]{2,1,0:T(8,128)S(1)} %get-tuple-element.27.sent), channel_id=1, source_target_pairs={{1,2},{2,1},{3,4},{4,3},{5,6},{6,5},{7,8},{8,7},{9,10},{10,9},{11,... | collective-permute-start | bytes 491528 | tf_op jit(solution)/shard_map/ppermute | solution.py:545

commit v9 on v7

--- a/solution.py
+++ b/solution.py
@@ -358,7 +358,7 @@
     parts[layers:] = weights[6] * here + weights[7] * there
 
 
-def join_time(time, opposite, near, solved, times, joined):
+def join_time(time, opposite, near, times, joined):
     layers = time.shape[0]
     times[...] = time[...] + near[:layers]
     joined[...] = opposite[...] + near[layers:]
@@ -416,50 +416,44 @@
         mass[i] = mass[i] + totals[3]
 
 
-def gather_terms(forward, own_first, own_second, back, sums, adjoint, rounded, sems):
+def gather_terms(forward, own_first, own_second, sums, adjoint, rounded, sem):
     early, layers = own_first.shape[:2]
-    half = early + own_second.shape[0]
-    tile = tile_of(lax.axis_index("space"))
-    mine, theirs = half * tile, half * (1 - tile)
+    half = rounded.shape[0]
+    mine = half * tile_of(lax.axis_index("space"))
     rounded[:early] = own_first[...].astype(jnp.bfloat16)
-    rounded[early:half] = own_second[...].astype(jnp.bfloat16)
-    for q in range(early):
-        rounded[half + q] = back[layers * q : layers * (q + 1)].astype(jnp.bfloat16)
-    copies = [
-        pltpu.make_async_copy(rounded.at[:half], adjoint.at[pl.ds(mine, half)], sems.at[0]),
-        pltpu.make_async_copy(rounded.at[half:], adjoint.at[pl.ds(theirs, early)], sems.at[1]),
-    ]
-    for copy in copies:
-        copy.start()
+    rounded[early:] = own_second[...].astype(jnp.bfloat16)
+    copy = pltpu.make_async_copy(rounded, adjoint.at[pl.ds(mine, half)], sem)
+    copy.start()
     sums[...] = jnp.zeros(sums.shape, jnp.float32)
     pairs = []
     for q in range(half):
-        if q < early:
-            pairs.append((mine + q, lambda i, q=q: own_first[q, i]))
-            pairs.append((theirs + q, lambda i, q=q: back[layers * q + i]))
-        else:
-            pairs.append((mine + q, lambda i, q=q: own_second[q - early, i]))
-    pairs = [(lambda i, s=s: forward[s, i].astype(jnp.float32), lam) for s, lam in pairs]
+        own, at = (own_first, q) if q < early else (own_second, q - early)
+        pairs.append((
+            lambda i, q=q: forward[mine + q, i].astype(jnp.float32),
+            lambda i, own=own, at=at: own[at, i],
+        ))
     data_sums(pairs, layers, sums.at[0], sums.at[1], sums.at[2], sums.at[3])
-    for copy in copies:
-        copy.wait()
-
-
-def finish(sums, back, sent, forward, model, other, times, far, kept, adjoint, gradient, rounded, result, sems):
+    copy.wait()
+
+
+def finish(sums, back_first, back, sent, forward, model, other, times, far, kept, adjoint, gradient, rounded, result, sems):
     tile = tile_of(lax.axis_index("space"))
-    count, layers = rounded.shape[:2]
-    half = forward.shape[0] // 2
-    theirs = half * (1 - tile) + half - count
-    for q in range(count):
-        rounded[q] = back[layers * q : layers * (q + 1)].astype(jnp.bfloat16)
-    copies = [pltpu.make_async_copy(rounded, adjoint.at[pl.ds(theirs, count)], sems.at[layers])]
+    half = rounded.shape[0]
+    shape = model.shape[1:]
+    layers = model.shape[0]
+    early = back_first.shape[0] // layers
+    count = half - early
+    theirs = half * (1 - tile)
+    rows = [(back_first, q) for q in range(early)] + [(back, q) for q in range(count)]
+    for q, (source, at) in enumerate(rows):
+        rounded[q] = source[layers * at : layers * (at + 1)].astype(jnp.bfloat16)
+    copies = [pltpu.make_async_copy(rounded, adjoint.at[pl.ds(theirs, half)], sems.at[layers])]
     copies[0].start()
-    shape = model.shape[1:]
     pairs = []
-    for q in range(count):
+    for q, (source, at) in enumerate(rows):
         pairs.append((
             lambda i, q=q: forward[theirs + q, i].astype(jnp.float32),
-            lambda i, q=q: back[layers * q + i],
+            lambda i, source=source, at=at: source[layers * at + i],
         ))
     in_y, in_z = inner(shape, 0), inner(shape, 1)
     low = jnp.where(tile == 0, 0.0, 1.0)
@@ -588,6 +582,8 @@
         micros=3,
     )
     back_first = swap(sent_first)
+    times, joined = call(join_time, (time, opposite, near), (V, V, V), [f32(*slab), f32(*slab)], micros=1)
+    far = swap(joined, 8)
     own_second, sent_second = call(
         solve_second,
         (coefs, got_second, warm_start, rhs, forward, own_first, sent_first),
@@ -597,25 +593,24 @@
         micros=3,
     )
     back_second = swap(sent_second)
-    times, joined = call(join_time, (time, opposite, near, own_second), (V, V, V, V), [f32(*slab), f32(*slab)])
-    far = swap(joined, 8)
     sums, kept = call(
         gather_terms,
-        (forward, own_first, own_second, back_first),
-        (V, V, V, V),
+        (forward, own_first, own_second),
+        (V, V, V),
         [f32(4, *slab), bf16(*forward.shape)],
         [V, H],
-        scratch=[V((half + early, *slab), jnp.bfloat16), dma((2,))],
-        micros=1,
+        scratch=[V((half, *slab), jnp.bfloat16), dma],
+        micros=3,
     )
     adjoint, gradient = call(
         finish,
-        (sums, back_second, sent_second, forward, model, other, times, far, kept),
-        (V, V, V, V, V, V, V, V, H),
+        (sums, back_first, back_second, sent_second, forward, model, other, times, far, kept),
+        (V, V, V, V, V, V, V, V, V, H),
         [bf16(*forward.shape), f32(*slab)],
         [H, H],
-        scratch=[V((late, *slab), jnp.bfloat16), V(slab, jnp.float32), dma((layers + 1,))],
-        aliases={8: 0},
+        scratch=[V((half, *slab), jnp.bfloat16), V(slab, jnp.float32), dma((layers + 1,))],
+        aliases={9: 0},
+        micros=1,
     )
     return adjoint, gradient
 

time: 41.1 us -> 38.3 us (0.932)
  the two profiles are of different devices: /device:TPU:0 before, /device:TPU:1 now
where the time goes in v9:
time: 38.3 us; the launch traced here: 38.1 us
  waiting for transfers between devices  15.7 us (41%)
  starting transfers between devices  12.7 us (33%)
  Pallas kernels  7.8 us (20%)
  local copies, waits for them, and re-layouts  1.08 us (3%)
  between operations  0.76 us (2%)
    ppermute x8, waiting for transfers between devices, swap(): return lax.ppermute(x, 'space', links)  15.7 us
    ppermute x8, starting transfers between devices, swap(): return lax.ppermute(x, 'space', links)  12.7 us
    pallas_call x10, Pallas kernels, call(): pl.pallas_call(kernel, out_shape=out_shapes if several else out_shapes[0]...  7.8 us
    unnamed x14, local copies, waits for them, and re-layouts  1.08 us
  transfers between devices with their start and end apart: 8, of which 5 were waited for; matrix products, arithmetic and copies ran while one was open for 0% of the time, Pallas kernels for 17%

profile of v9, /device:TPU:1, one launch (start us, length us, event | category | flops | bytes accessed | tf_op | source)
XLA Modules:
  0.0 38.1 jit_solution(10626311217308245724)
XLA Ops:
  0.6 2.7 %collective-permute-start = (f32[4,64,128]{2,1,0:T(8,128)}, f32[4,64,128]{2,1,0:T(8,128)S(1)}, u32[]{:S(2)}, u32[]{:S(2)}) collective-permute-start(f32[4,64,128]{2,1,0:T(8,128)} %model.5), channel_id=1, source_target_pairs={{1,2},{2,1},{3,4},{4,3},{5,6},{6,5},{7,8},{8,7},{9,10},{10,9},{11,... | collective-permute-start | bytes 393224 | tf_op jit(solution)/shard_map/ppermute | solution.py:538
  3.3 0.0 copy-start
  3.3 1.0 %copy-done = bf16[8,4,64,128]{3,2,1,0:T(8,128)(2,1)S(1)} copy-done((bf16[8,4,64,128]{3,2,1,0:T(8,128)(2,1)S(1)}, bf16[8,4,64,128]{3,2,1,0:T(8,128)(2,1)}, u32[]{:S(2)}) %copy-start) | copy-done | bytes 524312
  4.4 0.0 copy-start.3
  4.4 0.0 copy-start.4
  4.4 0.0 copy-start.5
  4.4 0.0 copy-start.6
  4.4 0.1 collective-permute-start.1
  4.5 2.5 %collective-permute-done.other = f32[4,64,128]{2,1,0:T(8,128)S(1)} collective-permute-done((f32[4,64,128]{2,1,0:T(8,128)}, f32[4,64,128]{2,1,0:T(8,128)S(1)}, u32[]{:S(2)}, u32[]{:S(2)}) %collective-permute-start) | collective-permute-done | bytes 131104 | tf_op jit(solution)/shard_map/ppermute | solution.py:538
  7.0 2.2 %collective-permute-start.2 = (f32[4,64,128]{2,1,0:T(8,128)S(1)}, f32[4,64,128]{2,1,0:T(8,128)S(1)}, u32[]{:S(2)}, u32[]{:S(2)}) collective-permute-start(f32[4,64,128]{2,1,0:T(8,128)S(1)} %collective-permute-done.other), channel_id=1, source_target_pairs={{0,1},{1,0},{2,3},{3,2},{4,5},{5,4},{6,7},{7,6},{8,9},{9,8},{10,11... | collective-permute-start | bytes 393224 | tf_op jit(solution)/shard_map/ppermute | solution.py:538
  9.2 0.0 copy-done.3
  9.2 0.3 shard_map.77.coefs
  9.5 0.0 copy-done.4
  9.5 0.0 copy-done.5
  9.5 0.0 copy-done.6
  9.5 1.2 %shard_map.79 = (f32[4,8,64,128]{3,2,1,0:T(8,128)S(1)}, f32[8]{0:T(128)S(1)}) custom-call(s32[8]{0:T(128)S(1)} %copy-done.6, f32[8,8,256]{2,1,0:T(8,128)S(1)} %copy-done.4, s32[1,256]{1,0:T(1,128)S(1)} %bitcast.1, f32[7,8,64,128]{3,2,1,0:T(8,128)S(1)} %shard_map.77.coefs), custom_call_target="tpu_custom_call" | custom-call | flops 1000000000 | bytes 3000000 | tf_op jit(solution)/shard_map/pallas_call | solution.py:503
  10.7 0.0 collective-permute-done.2.beside
  10.7 0.0 copy-start.1
  10.8 0.0 copy-start.2
  10.8 0.6 %shard_map.81 = (f32[4,64,128]{2,1,0:T(8,128)S(1)}, f32[4,64,128]{2,1,0:T(8,128)S(1)}, f32[8,64,128]{2,1,0:T(8,128)S(1)}) custom-call(f32[8]{0:T(128)S(1)} %get-tuple-element.17.weights, f32[4,64,128]{2,1,0:T(8,128)S(1)} %copy-done.3, f32[4,64,128]{2,1,0:T(8,128)S(1)} %collective-permute-done.2.beside), custom_call_target="tpu_custom_call" | custom-call | flops 1000000000 | bytes 3000000 | tf_op jit(solution)/shard_map/pallas_call | solution.py:503
  11.4 4.1 %collective-permute-start.6 = (f32[8,64,128]{2,1,0:T(8,128)S(1)}, f32[8,64,128]{2,1,0:T(8,128)S(1)}, u32[]{:S(2)}, u32[]{:S(2)}) collective-permute-start(f32[8,64,128]{2,1,0:T(8,128)S(1)} %get-tuple-element.18.parts), channel_id=1, source_target_pairs={{0,4},{1,5},{2,6},{3,7},{4,0},{5,1},{6,2},{7,3},{8,12},{9,13},{10,... | collective-permute-start | bytes 786440 | tf_op jit(solution)/shard_map/ppermute | solution.py:538
  15.5 0.0 copy-done.1
  15.5 0.0 copy-done.2
  15.6 0.1 collective-permute-start.3
  15.6 1.3 %collective-permute-done.1.got = f32[3,4,64,128]{3,2,1,0:T(8,128)S(1)} collective-permute-done((f32[3,4,64,128]{3,2,1,0:T(8,128)S(1)}, f32[3,4,64,128]{3,2,1,0:T(8,128)S(1)}, u32[]{:S(2)}, u32[]{:S(2)}) %collective-permute-start.1) | collective-permute-done | bytes 393248 | tf_op jit(solution)/shard_map/ppermute | solution.py:538
  16.9 2.3 %shard_map.80 = (f32[3,4,64,128]{3,2,1,0:T(8,128)S(1)}, f32[12,64,128]{2,1,0:T(8,128)S(1)}) custom-call(f32[7,8,64,128]{3,2,1,0:T(8,128)S(1)} %shard_map.77.coefs, f32[3,4,64,128]{3,2,1,0:T(8,128)S(1)} %collective-permute-done.1.got, bf16[8,4,64,128]{3,2,1,0:T(8,128)(2,1)S(1)} %copy-done.1, f32[4,8,64,128]{3,2,1,0:T(8,128)S(1)} %get-tuple-element.15.rhs), custom_call_target="tpu_custom_call" | custom-call | flops 3000000000 | bytes 9000000 | tf_op jit(solution)/shard_map/pallas_call | solution.py:503
  19.2 0.9 %collective-permute-start.4 = (f32[12,64,128]{2,1,0:T(8,128)S(1)}, f32[12,64,128]{2,1,0:T(8,128)S(1)}, u32[]{:S(2)}, u32[]{:S(2)}) collective-permute-start(f32[12,64,128]{2,1,0:T(8,128)S(1)} %get-tuple-element.19.sent_first), channel_id=1, source_target_pairs={{1,2},{2,1},{3,4},{4,3},{5,6},{6,5},{7,8},{8,7},{9,10},{10,9},{11,... | collective-permute-start | bytes 1179656 | tf_op jit(solution)/shard_map/ppermute | solution.py:538
  20.1 1.6 %collective-permute-done.6.near = f32[8,64,128]{2,1,0:T(8,128)S(1)} collective-permute-done((f32[8,64,128]{2,1,0:T(8,128)S(1)}, f32[8,64,128]{2,1,0:T(8,128)S(1)}, u32[]{:S(2)}, u32[]{:S(2)}) %collective-permute-start.6) | collective-permute-done | bytes 262176 | tf_op jit(solution)/shard_map/ppermute | solution.py:538
  21.8 2.2 %collective-permute-start.7 = (f32[4,64,128]{2,1,0:T(8,128)S(1)}, f32[4,64,128]{2,1,0:T(8,128)S(1)}, u32[]{:S(2)}, u32[]{:S(2)}) collective-permute-start(f32[4,64,128]{2,1,0:T(8,128)S(1)} %get-tuple-element.26), channel_id=1, source_target_pairs={{0,8},{1,9},{2,10},{3,11},{4,12},{5,13},{6,14},{7,15},{8,0},{9,1},... | collective-permute-start | bytes 393224 | tf_op jit(solution)/shard_map/ppermute | solution.py:538
  24.0 0.0 collective-permute-done.3.got
  24.0 0.8 %shard_map.83 = (f32[1,4,64,128]{3,2,1,0:T(8,128)S(1)}, f32[5,64,128]{2,1,0:T(8,128)S(1)}) custom-call(f32[7,8,64,128]{3,2,1,0:T(8,128)S(1)} %shard_map.77.coefs, f32[8,64,128]{2,1,0:T(8,128)S(1)} %collective-permute-done.3.got, bf16[8,4,64,128]{3,2,1,0:T(8,128)(2,1)S(1)} %copy-done.1, f32[4,8,64,128]{3,2,1,0:T(8,128)S(1)} %get-tuple-element.15.rhs, ...), custom_call_target="tpu_custom_call" | custom-call | flops 3000000000 | bytes 9000000 | tf_op jit(solution)/shard_map/pallas_call | solution.py:503
  24.8 0.4 %collective-permute-start.5 = (f32[5,64,128]{2,1,0:T(8,128)S(1)}, f32[5,64,128]{2,1,0:T(8,128)S(1)}, u32[]{:S(2)}, u32[]{:S(2)}) collective-permute-start(f32[5,64,128]{2,1,0:T(8,128)S(1)} %get-tuple-element.22.sent), channel_id=1, source_target_pairs={{1,2},{2,1},{3,4},{4,3},{5,6},{6,5},{7,8},{8,7},{9,10},{10,9},{11,... | collective-permute-start | bytes 491528 | tf_op jit(solution)/shard_map/ppermute | solution.py:538
  25.2 1.1 %shard_map.84 = (f32[4,4,64,128]{3,2,1,0:T(8,128)S(1)}, bf16[8,4,64,128]{3,2,1,0:T(8,128)(2,1)}) custom-call(bf16[8,4,64,128]{3,2,1,0:T(8,128)(2,1)S(1)} %copy-done.2, f32[3,4,64,128]{3,2,1,0:T(8,128)S(1)} %get-tuple-element.16.own_first, f32[1,4,64,128]{3,2,1,0:T(8,128)S(1)} %get-tuple-element.20.own_second), custom_call_target="tpu_custom_call" | custom-call | flops 3000000000 | bytes 9000000 | tf_op jit(solution)/shard_map/pallas_call | solution.py:503
  26.3 3.4 %collective-permute-done.7.far = f32[4,64,128]{2,1,0:T(8,128)S(1)} collective-permute-done((f32[4,64,128]{2,1,0:T(8,128)S(1)}, f32[4,64,128]{2,1,0:T(8,128)S(1)}, u32[]{:S(2)}, u32[]{:S(2)}) %collective-permute-start.7) | collective-permute-done | bytes 131104 | tf_op jit(solution)/shard_map/ppermute | solution.py:538
  29.7 7.0 %collective-permute-done.5.back = f32[5,64,128]{2,1,0:T(8,128)S(1)} collective-permute-done((f32[5,64,128]{2,1,0:T(8,128)S(1)}, f32[5,64,128]{2,1,0:T(8,128)S(1)}, u32[]{:S(2)}, u32[]{:S(2)}) %collective-permute-start.5) | collective-permute-done | bytes 163872 | tf_op jit(solution)/shard_map/ppermute | solution.py:538
  36.7 0.0 collective-permute-done.4.back_first
  36.7 1.4 %shard_map.86 = (bf16[8,4,64,128]{3,2,1,0:T(8,128)(2,1)}, f32[4,64,128]{2,1,0:T(8,128)}) custom-call(f32[4,4,64,128]{3,2,1,0:T(8,128)S(1)} %get-tuple-element.21.sums, f32[12,64,128]{2,1,0:T(8,128)S(1)} %collective-permute-done.4.back_first, f32[5,64,128]{2,1,0:T(8,128)S(1)} %collective-permute-done.5.back, ...), custom_call_target="tpu_custom_call", output_to_operand_aliasing={{0}: (9, {})} | custom-call | flops 1000000000 | bytes 3000000 | tf_op jit(solution)/shard_map/pallas_call | solution.py:503
  (3 shorter events, 0.1 us)
Async XLA Ops:
  0.6 6.4 %collective-permute-start = (f32[4,64,128]{2,1,0:T(8,128)}, f32[4,64,128]{2,1,0:T(8,128)S(1)}, u32[]{:S(2)}, u32[]{:S(2)}) collective-permute-start(f32[4,64,128]{2,1,0:T(8,128)} %model.5), channel_id=1, source_target_pairs={{1,2},{2,1},{3,4},{4,3},{5,6},{6,5},{7,8},{8,7},{9,10},{10,9},{11,... | collective-permute-start | bytes 393224 | tf_op jit(solution)/shard_map/ppermute | solution.py:538
  3.3 1.0 %copy-start = (bf16[8,4,64,128]{3,2,1,0:T(8,128)(2,1)S(1)}, bf16[8,4,64,128]{3,2,1,0:T(8,128)(2,1)}, u32[]{:S(2)}) copy-start(bf16[8,4,64,128]{3,2,1,0:T(8,128)(2,1)} %warm.7) | copy-start | bytes 1572868
  4.4 4.8 %copy-start.3 = (f32[4,64,128]{2,1,0:T(8,128)S(1)}, f32[4,64,128]{2,1,0:T(8,128)}, u32[]{:S(2)}) copy-start(f32[4,64,128]{2,1,0:T(8,128)} %model.5) | copy-start | bytes 393220
  4.4 5.1 %copy-start.4 = (f32[8,8,256]{2,1,0:T(8,128)S(1)}, f32[8,8,256]{2,1,0:T(8,128)}, u32[]{:S(2)}) copy-start(f32[8,8,256]{2,1,0:T(8,128)} %residual.1) | copy-start | bytes 196612
  4.4 5.1 %copy-start.5 = (s32[256]{0:T(256)S(1)}, s32[256]{0:T(256)}, u32[]{:S(2)}) copy-start(s32[256]{0:T(256)} %param.10) | copy-start | bytes 3076
  4.4 5.1 %copy-start.6 = (s32[8]{0:T(128)S(1)}, s32[8]{0:T(128)}, u32[]{:S(2)}) copy-start(s32[8]{0:T(128)} %order.1) | copy-start | bytes 100
  4.4 12.5 %collective-permute-start.1 = (f32[3,4,64,128]{3,2,1,0:T(8,128)S(1)}, f32[3,4,64,128]{3,2,1,0:T(8,128)S(1)}, u32[]{:S(2)}, u32[]{:S(2)}) collective-permute-start(f32[3,4,64,128]{3,2,1,0:T(8,128)S(1)} %shard_map.78), channel_id=1, source_target_pairs={{1,2},{2,1},{3,4},{4,3},{5,6},{6,5},{7,8},{8,7},{9,10},{10,9},{11,... | collective-permute-start | bytes 1179656 | tf_op jit(solution)/shard_map/ppermute | solution.py:538
  7.0 3.7 %collective-permute-start.2 = (f32[4,64,128]{2,1,0:T(8,128)S(1)}, f32[4,64,128]{2,1,0:T(8,128)S(1)}, u32[]{:S(2)}, u32[]{:S(2)}) collective-permute-start(f32[4,64,128]{2,1,0:T(8,128)S(1)} %collective-permute-done.other), channel_id=1, source_target_pairs={{0,1},{1,0},{2,3},{3,2},{4,5},{5,4},{6,7},{7,6},{8,9},{9,8},{10,11... | collective-permute-start | bytes 393224 | tf_op jit(solution)/shard_map/ppermute | solution.py:538
  10.7 4.8 %copy-start.1 = (bf16[8,4,64,128]{3,2,1,0:T(8,128)(2,1)S(1)}, bf16[8,4,64,128]{3,2,1,0:T(8,128)(2,1)}, u32[]{:S(2)}) copy-start(bf16[8,4,64,128]{3,2,1,0:T(8,128)(2,1)} %warm.7) | copy-start | bytes 1572868
  10.8 4.8 %copy-start.2 = (bf16[8,4,64,128]{3,2,1,0:T(8,128)(2,1)S(1)}, bf16[8,4,64,128]{3,2,1,0:T(8,128)(2,1)}, u32[]{:S(2)}) copy-start(bf16[8,4,64,128]{3,2,1,0:T(8,128)(2,1)} %forward.7) | copy-start | bytes 1572868
  11.4 10.4 %collective-permute-start.6 = (f32[8,64,128]{2,1,0:T(8,128)S(1)}, f32[8,64,128]{2,1,0:T(8,128)S(1)}, u32[]{:S(2)}, u32[]{:S(2)}) collective-permute-start(f32[8,64,128]{2,1,0:T(8,128)S(1)} %get-tuple-element.18.parts), channel_id=1, source_target_pairs={{0,4},{1,5},{2,6},{3,7},{4,0},{5,1},{6,2},{7,3},{8,12},{9,13},{10,... | collective-permute-start | bytes 786440 | tf_op jit(solution)/shard_map/ppermute | solution.py:538
  15.6 8.4 %collective-permute-start.3 = (f32[8,64,128]{2,1,0:T(8,128)S(1)}, f32[8,64,128]{2,1,0:T(8,128)S(1)}, u32[]{:S(2)}, u32[]{:S(2)}) collective-permute-start(f32[8,64,128]{2,1,0:T(8,128)S(1)} %shard_map.82), channel_id=1, source_target_pairs={{1,2},{2,1},{3,4},{4,3},{5,6},{6,5},{7,8},{8,7},{9,10},{10,9},{11,... | collective-permute-start | bytes 786440 | tf_op jit(solution)/shard_map/ppermute | solution.py:538
  19.2 17.5 %collective-permute-start.4 = (f32[12,64,128]{2,1,0:T(8,128)S(1)}, f32[12,64,128]{2,1,0:T(8,128)S(1)}, u32[]{:S(2)}, u32[]{:S(2)}) collective-permute-start(f32[12,64,128]{2,1,0:T(8,128)S(1)} %get-tuple-element.19.sent_first), channel_id=1, source_target_pairs={{1,2},{2,1},{3,4},{4,3},{5,6},{6,5},{7,8},{8,7},{9,10},{10,9},{11,... | collective-permute-start | bytes 1179656 | tf_op jit(solution)/shard_map/ppermute | solution.py:538
  21.8 7.9 %collective-permute-start.7 = (f32[4,64,128]{2,1,0:T(8,128)S(1)}, f32[4,64,128]{2,1,0:T(8,128)S(1)}, u32[]{:S(2)}, u32[]{:S(2)}) collective-permute-start(f32[4,64,128]{2,1,0:T(8,128)S(1)} %get-tuple-element.26), channel_id=1, source_target_pairs={{0,8},{1,9},{2,10},{3,11},{4,12},{5,13},{6,14},{7,15},{8,0},{9,1},... | collective-permute-start | bytes 393224 | tf_op jit(solution)/shard_map/ppermute | solution.py:538
  24.8 11.9 %collective-permute-start.5 = (f32[5,64,128]{2,1,0:T(8,128)S(1)}, f32[5,64,128]{2,1,0:T(8,128)S(1)}, u32[]{:S(2)}, u32[]{:S(2)}) collective-permute-start(f32[5,64,128]{2,1,0:T(8,128)S(1)} %get-tuple-element.22.sent), channel_id=1, source_target_pairs={{1,2},{2,1},{3,4},{4,3},{5,6},{6,5},{7,8},{8,7},{9,10},{10,9},{11,... | collective-permute-start | bytes 491528 | tf_op jit(solution)/shard_map/ppermute | solution.py:538

commit v10 on v9

--- a/solution.py
+++ b/solution.py
@@ -436,24 +436,39 @@
     copy.wait()
 
 
-def finish(sums, back_first, back, sent, forward, model, other, times, far, kept, adjoint, gradient, rounded, result, sems):
+def gather_back(sums, back, forward, kept, added, adjoint, rounded, sem):
+    early, layers = rounded.shape[:2]
+    theirs = forward.shape[0] // 2 * (1 - tile_of(lax.axis_index("space")))
+    for q in range(early):
+        rounded[q] = back[layers * q : layers * (q + 1)].astype(jnp.bfloat16)
+    copy = pltpu.make_async_copy(rounded, adjoint.at[pl.ds(theirs, early)], sem)
+    copy.start()
+    added[...] = sums[...]
+    pairs = []
+    for q in range(early):
+        pairs.append((
+            lambda i, q=q: forward[theirs + q, i].astype(jnp.float32),
+            lambda i, q=q: back[layers * q + i],
+        ))
+    data_sums(pairs, layers, added.at[0], added.at[1], added.at[2], added.at[3])
+    copy.wait()
+
+
+def finish(sums, back, sent, forward, model, other, times, far, kept, adjoint, gradient, rounded, result, sems):
     tile = tile_of(lax.axis_index("space"))
-    half = rounded.shape[0]
     shape = model.shape[1:]
-    layers = model.shape[0]
-    early = back_first.shape[0] // layers
-    count = half - early
-    theirs = half * (1 - tile)
-    rows = [(back_first, q) for q in range(early)] + [(back, q) for q in range(count)]
-    for q, (source, at) in enumerate(rows):
-        rounded[q] = source[layers * at : layers * (at + 1)].astype(jnp.bfloat16)
-    copies = [pltpu.make_async_copy(rounded, adjoint.at[pl.ds(theirs, half)], sems.at[layers])]
+    count, layers = rounded.shape[:2]
+    half = forward.shape[0] // 2
+    theirs = half * (1 - tile) + half - count
+    for q in range(count):
+        rounded[q] = back[layers * q : layers * (q + 1)].astype(jnp.bfloat16)
+    copies = [pltpu.make_async_copy(rounded, adjoint.at[pl.ds(theirs, count)], sems.at[layers])]
     copies[0].start()
     pairs = []
-    for q, (source, at) in enumerate(rows):
+    for q in range(count):
         pairs.append((
             lambda i, q=q: forward[theirs + q, i].astype(jnp.float32),
-            lambda i, source=source, at=at: source[layers * at + i],
+            lambda i, q=q: back[layers * q + i],
         ))
     in_y, in_z = inner(shape, 0), inner(shape, 1)
     low = jnp.where(tile == 0, 0.0, 1.0)
@@ -602,15 +617,24 @@
         scratch=[V((half, *slab), jnp.bfloat16), dma],
         micros=3,
     )
+    added, joint = call(
+        gather_back,
+        (sums, back_first, forward, kept),
+        (V, V, V, H),
+        [f32(4, *slab), bf16(*forward.shape)],
+        [V, H],
+        scratch=[V((early, *slab), jnp.bfloat16), dma],
+        aliases={3: 1},
+        micros=1,
+    )
     adjoint, gradient = call(
         finish,
-        (sums, back_first, back_second, sent_second, forward, model, other, times, far, kept),
-        (V, V, V, V, V, V, V, V, V, H),
+        (added, back_second, sent_second, forward, model, other, times, far, joint),
+        (V, V, V, V, V, V, V, V, H),
         [bf16(*forward.shape), f32(*slab)],
         [H, H],
-        scratch=[V((half, *slab), jnp.bfloat16), V(slab, jnp.float32), dma((layers + 1,))],
-        aliases={9: 0},
-        micros=1,
+        scratch=[V((late, *slab), jnp.bfloat16), V(slab, jnp.float32), dma((layers + 1,))],
+        aliases={8: 0},
     )
     return adjoint, gradient
 

time: 38.3 us -> 37.8 us (0.987)
  waiting for transfers between devices: 15.7 us -> 14.8 us
  Pallas kernels: 7.8 us -> 8.31 us
    ppermute x8, waiting for transfers between devices: 15.7 us -> 14.8 us  [swap(): return lax.ppermute(x, 'space', links)]
    pallas_call x10 -> x11, Pallas kernels: 7.8 us -> 8.31 us  [call(): pl.pallas_call(kernel, out_shape=out_shapes if several else out_shapes[0]...]
  transfers between devices with their start and end apart: 8 -> 8, of which waited for: 5 -> 5; matrix products, arithmetic and copies ran while one was open for 0% -> 0% of each run, Pallas kernels for 17% -> 19%
where the time goes in v10:
time: 37.8 us; the launch traced here: 37.7 us
  waiting for transfers between devices  14.8 us (39%)
  starting transfers between devices  12.7 us (34%)
  Pallas kernels  8.31 us (22%)
  local copies, waits for them, and re-layouts  1.08 us (3%)
  between operations  0.78 us (2%)
    ppermute x8, waiting for transfers between devices, swap(): return lax.ppermute(x, 'space', links)  14.8 us
    ppermute x8, starting transfers between devices, swap(): return lax.ppermute(x, 'space', links)  12.7 us
    pallas_call x11, Pallas kernels, call(): pl.pallas_call(kernel, out_shape=out_shapes if several else out_shapes[0]...  8.31 us
    unnamed x14, local copies, waits for them, and re-layouts  1.08 us
  transfers between devices with their start and end apart: 8, of which 5 were waited for; matrix products, arithmetic and copies ran while one was open for 0% of the time, Pallas kernels for 19%

profile of v10, /device:TPU:1, one launch (start us, length us, event | category | flops | bytes accessed | tf_op | source)
XLA Modules:
  0.0 37.7 jit_solution(15163188319843880347)
XLA Ops:
  0.6 2.7 %collective-permute-start = (f32[4,64,128]{2,1,0:T(8,128)}, f32[4,64,128]{2,1,0:T(8,128)S(1)}, u32[]{:S(2)}, u32[]{:S(2)}) collective-permute-start(f32[4,64,128]{2,1,0:T(8,128)} %model.5), channel_id=1, source_target_pairs={{1,2},{2,1},{3,4},{4,3},{5,6},{6,5},{7,8},{8,7},{9,10},{10,9},{11,... | collective-permute-start | bytes 393224 | tf_op jit(solution)/shard_map/ppermute | solution.py:553
  3.3 0.0 copy-start
  3.3 1.0 %copy-done = bf16[8,4,64,128]{3,2,1,0:T(8,128)(2,1)S(1)} copy-done((bf16[8,4,64,128]{3,2,1,0:T(8,128)(2,1)S(1)}, bf16[8,4,64,128]{3,2,1,0:T(8,128)(2,1)}, u32[]{:S(2)}) %copy-start) | copy-done | bytes 524312
  4.4 0.0 copy-start.3
  4.4 0.0 copy-start.4
  4.4 0.0 copy-start.5
  4.4 0.0 copy-start.6
  4.4 0.1 collective-permute-start.1
  4.5 2.5 %collective-permute-done.other = f32[4,64,128]{2,1,0:T(8,128)S(1)} collective-permute-done((f32[4,64,128]{2,1,0:T(8,128)}, f32[4,64,128]{2,1,0:T(8,128)S(1)}, u32[]{:S(2)}, u32[]{:S(2)}) %collective-permute-start) | collective-permute-done | bytes 131104 | tf_op jit(solution)/shard_map/ppermute | solution.py:553
  7.0 2.2 %collective-permute-start.2 = (f32[4,64,128]{2,1,0:T(8,128)S(1)}, f32[4,64,128]{2,1,0:T(8,128)S(1)}, u32[]{:S(2)}, u32[]{:S(2)}) collective-permute-start(f32[4,64,128]{2,1,0:T(8,128)S(1)} %collective-permute-done.other), channel_id=1, source_target_pairs={{0,1},{1,0},{2,3},{3,2},{4,5},{5,4},{6,7},{7,6},{8,9},{9,8},{10,11... | collective-permute-start | bytes 393224 | tf_op jit(solution)/shard_map/ppermute | solution.py:553
  9.2 0.0 copy-done.3
  9.2 0.3 shard_map.77.coefs
  9.5 0.0 copy-done.4
  9.5 0.0 copy-done.5
  9.5 0.0 copy-done.6
  9.5 1.2 %shard_map.79 = (f32[4,8,64,128]{3,2,1,0:T(8,128)S(1)}, f32[8]{0:T(128)S(1)}) custom-call(s32[8]{0:T(128)S(1)} %copy-done.6, f32[8,8,256]{2,1,0:T(8,128)S(1)} %copy-done.4, s32[1,256]{1,0:T(1,128)S(1)} %bitcast.1, f32[7,8,64,128]{3,2,1,0:T(8,128)S(1)} %shard_map.77.coefs), custom_call_target="tpu_custom_call" | custom-call | flops 1000000000 | bytes 3000000 | tf_op jit(solution)/shard_map/pallas_call | solution.py:518
  10.7 0.0 collective-permute-done.2.beside
  10.7 0.0 copy-start.1
  10.8 0.0 copy-start.2
  10.8 0.6 %shard_map.81 = (f32[4,64,128]{2,1,0:T(8,128)S(1)}, f32[4,64,128]{2,1,0:T(8,128)S(1)}, f32[8,64,128]{2,1,0:T(8,128)S(1)}) custom-call(f32[8]{0:T(128)S(1)} %get-tuple-element.19.weights, f32[4,64,128]{2,1,0:T(8,128)S(1)} %copy-done.3, f32[4,64,128]{2,1,0:T(8,128)S(1)} %collective-permute-done.2.beside), custom_call_target="tpu_custom_call" | custom-call | flops 1000000000 | bytes 3000000 | tf_op jit(solution)/shard_map/pallas_call | solution.py:518
  11.4 4.1 %collective-permute-start.6 = (f32[8,64,128]{2,1,0:T(8,128)S(1)}, f32[8,64,128]{2,1,0:T(8,128)S(1)}, u32[]{:S(2)}, u32[]{:S(2)}) collective-permute-start(f32[8,64,128]{2,1,0:T(8,128)S(1)} %get-tuple-element.20.parts), channel_id=1, source_target_pairs={{0,4},{1,5},{2,6},{3,7},{4,0},{5,1},{6,2},{7,3},{8,12},{9,13},{10,... | collective-permute-start | bytes 786440 | tf_op jit(solution)/shard_map/ppermute | solution.py:553
  15.5 0.0 copy-done.1
  15.5 0.0 copy-done.2
  15.6 0.1 collective-permute-start.3
  15.6 1.3 %collective-permute-done.1.got = f32[3,4,64,128]{3,2,1,0:T(8,128)S(1)} collective-permute-done((f32[3,4,64,128]{3,2,1,0:T(8,128)S(1)}, f32[3,4,64,128]{3,2,1,0:T(8,128)S(1)}, u32[]{:S(2)}, u32[]{:S(2)}) %collective-permute-start.1) | collective-permute-done | bytes 393248 | tf_op jit(solution)/shard_map/ppermute | solution.py:553
  16.9 2.3 %shard_map.80 = (f32[3,4,64,128]{3,2,1,0:T(8,128)S(1)}, f32[12,64,128]{2,1,0:T(8,128)S(1)}) custom-call(f32[7,8,64,128]{3,2,1,0:T(8,128)S(1)} %shard_map.77.coefs, f32[3,4,64,128]{3,2,1,0:T(8,128)S(1)} %collective-permute-done.1.got, bf16[8,4,64,128]{3,2,1,0:T(8,128)(2,1)S(1)} %copy-done.1, f32[4,8,64,128]{3,2,1,0:T(8,128)S(1)} %get-tuple-element.17.rhs), custom_call_target="tpu_custom_call" | custom-call | flops 3000000000 | bytes 9000000 | tf_op jit(solution)/shard_map/pallas_call | solution.py:518
  19.2 0.9 %collective-permute-start.4 = (f32[12,64,128]{2,1,0:T(8,128)S(1)}, f32[12,64,128]{2,1,0:T(8,128)S(1)}, u32[]{:S(2)}, u32[]{:S(2)}) collective-permute-start(f32[12,64,128]{2,1,0:T(8,128)S(1)} %get-tuple-element.21.sent_first), channel_id=1, source_target_pairs={{1,2},{2,1},{3,4},{4,3},{5,6},{6,5},{7,8},{8,7},{9,10},{10,9},{11,... | collective-permute-start | bytes 1179656 | tf_op jit(solution)/shard_map/ppermute | solution.py:553
  20.1 1.6 %collective-permute-done.6.near = f32[8,64,128]{2,1,0:T(8,128)S(1)} collective-permute-done((f32[8,64,128]{2,1,0:T(8,128)S(1)}, f32[8,64,128]{2,1,0:T(8,128)S(1)}, u32[]{:S(2)}, u32[]{:S(2)}) %collective-permute-start.6) | collective-permute-done | bytes 262176 | tf_op jit(solution)/shard_map/ppermute | solution.py:553
  21.8 2.2 %collective-permute-start.7 = (f32[4,64,128]{2,1,0:T(8,128)S(1)}, f32[4,64,128]{2,1,0:T(8,128)S(1)}, u32[]{:S(2)}, u32[]{:S(2)}) collective-permute-start(f32[4,64,128]{2,1,0:T(8,128)S(1)} %get-tuple-element.30), channel_id=1, source_target_pairs={{0,8},{1,9},{2,10},{3,11},{4,12},{5,13},{6,14},{7,15},{8,0},{9,1},... | collective-permute-start | bytes 393224 | tf_op jit(solution)/shard_map/ppermute | solution.py:553
  24.0 0.0 collective-permute-done.3.got
  24.0 0.8 %shard_map.83 = (f32[1,4,64,128]{3,2,1,0:T(8,128)S(1)}, f32[5,64,128]{2,1,0:T(8,128)S(1)}) custom-call(f32[7,8,64,128]{3,2,1,0:T(8,128)S(1)} %shard_map.77.coefs, f32[8,64,128]{2,1,0:T(8,128)S(1)} %collective-permute-done.3.got, bf16[8,4,64,128]{3,2,1,0:T(8,128)(2,1)S(1)} %copy-done.1, f32[4,8,64,128]{3,2,1,0:T(8,128)S(1)} %get-tuple-element.17.rhs, ...), custom_call_target="tpu_custom_call" | custom-call | flops 3000000000 | bytes 9000000 | tf_op jit(solution)/shard_map/pallas_call | solution.py:518
  24.8 0.4 %collective-permute-start.5 = (f32[5,64,128]{2,1,0:T(8,128)S(1)}, f32[5,64,128]{2,1,0:T(8,128)S(1)}, u32[]{:S(2)}, u32[]{:S(2)}) collective-permute-start(f32[5,64,128]{2,1,0:T(8,128)S(1)} %get-tuple-element.26.sent), channel_id=1, source_target_pairs={{1,2},{2,1},{3,4},{4,3},{5,6},{6,5},{7,8},{8,7},{9,10},{10,9},{11,... | collective-permute-start | bytes 491528 | tf_op jit(solution)/shard_map/ppermute | solution.py:553
  25.2 1.1 %shard_map.84 = (f32[4,4,64,128]{3,2,1,0:T(8,128)S(1)}, bf16[8,4,64,128]{3,2,1,0:T(8,128)(2,1)}) custom-call(bf16[8,4,64,128]{3,2,1,0:T(8,128)(2,1)S(1)} %copy-done.2, f32[3,4,64,128]{3,2,1,0:T(8,128)S(1)} %get-tuple-element.18.own_first, f32[1,4,64,128]{3,2,1,0:T(8,128)S(1)} %get-tuple-element.22.own_second), custom_call_target="tpu_custom_call" | custom-call | flops 3000000000 | bytes 9000000 | tf_op jit(solution)/shard_map/pallas_call | solution.py:518
  26.3 8.7 %collective-permute-done.4.back = f32[12,64,128]{2,1,0:T(8,128)S(1)} collective-permute-done((f32[12,64,128]{2,1,0:T(8,128)S(1)}, f32[12,64,128]{2,1,0:T(8,128)S(1)}, u32[]{:S(2)}, u32[]{:S(2)}) %collective-permute-start.4) | collective-permute-done | bytes 393248 | tf_op jit(solution)/shard_map/ppermute | solution.py:553
  35.0 1.0 %shard_map.85 = (f32[4,4,64,128]{3,2,1,0:T(8,128)S(1)}, bf16[8,4,64,128]{3,2,1,0:T(8,128)(2,1)}) custom-call(f32[4,4,64,128]{3,2,1,0:T(8,128)S(1)} %get-tuple-element.23.sums, f32[12,64,128]{2,1,0:T(8,128)S(1)} %collective-permute-done.4.back, bf16[8,4,64,128]{3,2,1,0:T(8,128)(2,1)S(1)} %copy-done.2, ...), custom_call_target="tpu_custom_call", output_to_operand_aliasing={{1}: (3, {})} | custom-call | flops 1000000000 | bytes 3000000 | tf_op jit(solution)/shard_map/pallas_call | solution.py:518
  36.0 0.0 collective-permute-done.7.far
  36.0 0.7 %collective-permute-done.5.back = f32[5,64,128]{2,1,0:T(8,128)S(1)} collective-permute-done((f32[5,64,128]{2,1,0:T(8,128)S(1)}, f32[5,64,128]{2,1,0:T(8,128)S(1)}, u32[]{:S(2)}, u32[]{:S(2)}) %collective-permute-start.5) | collective-permute-done | bytes 163872 | tf_op jit(solution)/shard_map/ppermute | solution.py:553
  36.7 1.0 %shard_map.87 = (bf16[8,4,64,128]{3,2,1,0:T(8,128)(2,1)}, f32[4,64,128]{2,1,0:T(8,128)}) custom-call(f32[4,4,64,128]{3,2,1,0:T(8,128)S(1)} %get-tuple-element.25.sums, f32[5,64,128]{2,1,0:T(8,128)S(1)} %collective-permute-done.5.back, f32[5,64,128]{2,1,0:T(8,128)S(1)} %get-tuple-element.26.sent, ...), custom_call_target="tpu_custom_call", output_to_operand_aliasing={{0}: (8, {})} | custom-call | flops 1000000000 | bytes 3000000 | tf_op jit(solution)/shard_map/pallas_call | solution.py:518
  (3 shorter events, 0.1 us)
Async XLA Ops:
  0.6 6.4 %collective-permute-start = (f32[4,64,128]{2,1,0:T(8,128)}, f32[4,64,128]{2,1,0:T(8,128)S(1)}, u32[]{:S(2)}, u32[]{:S(2)}) collective-permute-start(f32[4,64,128]{2,1,0:T(8,128)} %model.5), channel_id=1, source_target_pairs={{1,2},{2,1},{3,4},{4,3},{5,6},{6,5},{7,8},{8,7},{9,10},{10,9},{11,... | collective-permute-start | bytes 393224 | tf_op jit(solution)/shard_map/ppermute | solution.py:553
  3.3 1.0 %copy-start = (bf16[8,4,64,128]{3,2,1,0:T(8,128)(2,1)S(1)}, bf16[8,4,64,128]{3,2,1,0:T(8,128)(2,1)}, u32[]{:S(2)}) copy-start(bf16[8,4,64,128]{3,2,1,0:T(8,128)(2,1)} %warm.7) | copy-start | bytes 1572868
  4.4 4.8 %copy-start.3 = (f32[4,64,128]{2,1,0:T(8,128)S(1)}, f32[4,64,128]{2,1,0:T(8,128)}, u32[]{:S(2)}) copy-start(f32[4,64,128]{2,1,0:T(8,128)} %model.5) | copy-start | bytes 393220
  4.4 5.1 %copy-start.4 = (f32[8,8,256]{2,1,0:T(8,128)S(1)}, f32[8,8,256]{2,1,0:T(8,128)}, u32[]{:S(2)}) copy-start(f32[8,8,256]{2,1,0:T(8,128)} %residual.1) | copy-start | bytes 196612
  4.4 5.1 %copy-start.5 = (s32[256]{0:T(256)S(1)}, s32[256]{0:T(256)}, u32[]{:S(2)}) copy-start(s32[256]{0:T(256)} %param.10) | copy-start | bytes 3076
  4.4 5.1 %copy-start.6 = (s32[8]{0:T(128)S(1)}, s32[8]{0:T(128)}, u32[]{:S(2)}) copy-start(s32[8]{0:T(128)} %order.1) | copy-start | bytes 100
  4.4 12.5 %collective-permute-start.1 = (f32[3,4,64,128]{3,2,1,0:T(8,128)S(1)}, f32[3,4,64,128]{3,2,1,0:T(8,128)S(1)}, u32[]{:S(2)}, u32[]{:S(2)}) collective-permute-start(f32[3,4,64,128]{3,2,1,0:T(8,128)S(1)} %shard_map.78), channel_id=1, source_target_pairs={{1,2},{2,1},{3,4},{4,3},{5,6},{6,5},{7,8},{8,7},{9,10},{10,9},{11,... | collective-permute-start | bytes 1179656 | tf_op jit(solution)/shard_map/ppermute | solution.py:553
  7.0 3.7 %collective-permute-start.2 = (f32[4,64,128]{2,1,0:T(8,128)S(1)}, f32[4,64,128]{2,1,0:T(8,128)S(1)}, u32[]{:S(2)}, u32[]{:S(2)}) collective-permute-start(f32[4,64,128]{2,1,0:T(8,128)S(1)} %collective-permute-done.other), channel_id=1, source_target_pairs={{0,1},{1,0},{2,3},{3,2},{4,5},{5,4},{6,7},{7,6},{8,9},{9,8},{10,11... | collective-permute-start | bytes 393224 | tf_op jit(solution)/shard_map/ppermute | solution.py:553
  10.7 4.8 %copy-start.1 = (bf16[8,4,64,128]{3,2,1,0:T(8,128)(2,1)S(1)}, bf16[8,4,64,128]{3,2,1,0:T(8,128)(2,1)}, u32[]{:S(2)}) copy-start(bf16[8,4,64,128]{3,2,1,0:T(8,128)(2,1)} %warm.7) | copy-start | bytes 1572868
  10.8 4.8 %copy-start.2 = (bf16[8,4,64,128]{3,2,1,0:T(8,128)(2,1)S(1)}, bf16[8,4,64,128]{3,2,1,0:T(8,128)(2,1)}, u32[]{:S(2)}) copy-start(bf16[8,4,64,128]{3,2,1,0:T(8,128)(2,1)} %forward.9) | copy-start | bytes 1572868
  11.4 10.4 %collective-permute-start.6 = (f32[8,64,128]{2,1,0:T(8,128)S(1)}, f32[8,64,128]{2,1,0:T(8,128)S(1)}, u32[]{:S(2)}, u32[]{:S(2)}) collective-permute-start(f32[8,64,128]{2,1,0:T(8,128)S(1)} %get-tuple-element.20.parts), channel_id=1, source_target_pairs={{0,4},{1,5},{2,6},{3,7},{4,0},{5,1},{6,2},{7,3},{8,12},{9,13},{10,... | collective-permute-start | bytes 786440 | tf_op jit(solution)/shard_map/ppermute | solution.py:553
  15.6 8.4 %collective-permute-start.3 = (f32[8,64,128]{2,1,0:T(8,128)S(1)}, f32[8,64,128]{2,1,0:T(8,128)S(1)}, u32[]{:S(2)}, u32[]{:S(2)}) collective-permute-start(f32[8,64,128]{2,1,0:T(8,128)S(1)} %shard_map.82), channel_id=1, source_target_pairs={{1,2},{2,1},{3,4},{4,3},{5,6},{6,5},{7,8},{8,7},{9,10},{10,9},{11,... | collective-permute-start | bytes 786440 | tf_op jit(solution)/shard_map/ppermute | solution.py:553
  19.2 15.8 %collective-permute-start.4 = (f32[12,64,128]{2,1,0:T(8,128)S(1)}, f32[12,64,128]{2,1,0:T(8,128)S(1)}, u32[]{:S(2)}, u32[]{:S(2)}) collective-permute-start(f32[12,64,128]{2,1,0:T(8,128)S(1)} %get-tuple-element.21.sent_first), channel_id=1, source_target_pairs={{1,2},{2,1},{3,4},{4,3},{5,6},{6,5},{7,8},{8,7},{9,10},{10,9},{11,... | collective-permute-start | bytes 1179656 | tf_op jit(solution)/shard_map/ppermute | solution.py:553
  21.8 14.2 %collective-permute-start.7 = (f32[4,64,128]{2,1,0:T(8,128)S(1)}, f32[4,64,128]{2,1,0:T(8,128)S(1)}, u32[]{:S(2)}, u32[]{:S(2)}) collective-permute-start(f32[4,64,128]{2,1,0:T(8,128)S(1)} %get-tuple-element.30), channel_id=1, source_target_pairs={{0,8},{1,9},{2,10},{3,11},{4,12},{5,13},{6,14},{7,15},{8,0},{9,1},... | collective-permute-start | bytes 393224 | tf_op jit(solution)/shard_map/ppermute | solution.py:553
  24.8 11.9 %collective-permute-start.5 = (f32[5,64,128]{2,1,0:T(8,128)S(1)}, f32[5,64,128]{2,1,0:T(8,128)S(1)}, u32[]{:S(2)}, u32[]{:S(2)}) collective-permute-start(f32[5,64,128]{2,1,0:T(8,128)S(1)} %get-tuple-element.26.sent), channel_id=1, source_target_pairs={{1,2},{2,1},{3,4},{4,3},{5,6},{6,5},{7,8},{8,7},{9,10},{10,9},{11,... | collective-permute-start | bytes 491528 | tf_op jit(solution)/shard_map/ppermute | solution.py:553

commit v11 on v10

--- a/solution.py
+++ b/solution.py
@@ -436,9 +436,26 @@
     copy.wait()
 
 
-def gather_back(sums, back, forward, kept, added, adjoint, rounded, sem):
+def spread(along_x, along_y, along_z, first, last, shape):
+    in_y, in_z = inner(shape, 0), inner(shape, 1)
+    products = [first] + along_x + [last]
+    terms = []
+    for i in range(len(along_y)):
+        total_y = jnp.where(in_y, along_y[i], 0.0)
+        total_z = jnp.where(in_z, along_z[i], 0.0)
+        sides = [p for p in products[i : i + 2] if p is not None]
+        total = (total_y + before(total_y, 0)) + (total_z + before(total_z, 1))
+        for side in sides:
+            total = total + side
+        terms.append(total)
+    return terms
+
+
+def gather_back(sums, back, forward, model, other, times, kept, base, sigma, adjoint, added, rounded, sem):
     early, layers = rounded.shape[:2]
-    theirs = forward.shape[0] // 2 * (1 - tile_of(lax.axis_index("space")))
+    tile = tile_of(lax.axis_index("space"))
+    theirs = forward.shape[0] // 2 * (1 - tile)
+    shape = model.shape[1:]
     for q in range(early):
         rounded[q] = back[layers * q : layers * (q + 1)].astype(jnp.bfloat16)
     copy = pltpu.make_async_copy(rounded, adjoint.at[pl.ds(theirs, early)], sem)
@@ -451,12 +468,26 @@
             lambda i, q=q: back[layers * q + i],
         ))
     data_sums(pairs, layers, added.at[0], added.at[1], added.at[2], added.at[3])
+    along = [[added[k, i] for i in range(layers)] for k in range(4)]
+    terms = spread(along[0][:-1], along[1], along[2], None, None, shape)
+    in_y, in_z = inner(shape, 0), inner(shape, 1)
+    low = jnp.where(tile == 0, 0.0, 1.0)
+    bridge = other[(layers - 1) * tile]
+    falls = [low * (bridge - model[0])]
+    falls += [model[i] - model[i + 1] for i in range(layers - 1)]
+    falls += [(1.0 - low) * (model[layers - 1] - bridge)]
+    for i in range(layers):
+        value = model[i]
+        sigma[i] = jnp.exp(value)
+        fall_y = jnp.where(in_y, value - after(value, 0), 0.0)
+        fall_z = jnp.where(in_z, value - after(value, 1), 0.0)
+        space = falls[i + 1] - falls[i] + (fall_y - before(fall_y, 0)) + (fall_z - before(fall_z, 1))
+        base[i] = space + times[i] - sigma[i] * (0.5 * terms[i] + GROUND * along[3][i])
     copy.wait()
 
 
-def finish(sums, back, sent, forward, model, other, times, far, kept, adjoint, gradient, rounded, result, sems):
+def finish(base, sigma, back, sent, forward, far, kept, adjoint, gradient, rounded, result, sems):
     tile = tile_of(lax.axis_index("space"))
-    shape = model.shape[1:]
     count, layers = rounded.shape[:2]
     half = forward.shape[0] // 2
     theirs = half * (1 - tile) + half - count
@@ -464,44 +495,23 @@
         rounded[q] = back[layers * q : layers * (q + 1)].astype(jnp.bfloat16)
     copies = [pltpu.make_async_copy(rounded, adjoint.at[pl.ds(theirs, count)], sems.at[layers])]
     copies[0].start()
-    pairs = []
+    along = [[None] * layers for _ in range(4)]
     for q in range(count):
-        pairs.append((
-            lambda i, q=q: forward[theirs + q, i].astype(jnp.float32),
-            lambda i, q=q: back[layers * q + i],
-        ))
-    in_y, in_z = inner(shape, 0), inner(shape, 1)
+        here = [forward[theirs + q, i].astype(jnp.float32) for i in range(layers)]
+        there = [back[layers * q + i] for i in range(layers)]
+        for i in range(layers):
+            values = [None, face_prod(here[i], there[i], 0), face_prod(here[i], there[i], 1), here[i] * there[i]]
+            if i + 1 < layers:
+                values[0] = (here[i] - here[i + 1]) * (there[i] - there[i + 1])
+            for k, value in enumerate(values):
+                if value is not None:
+                    along[k][i] = value if along[k][i] is None else along[k][i] + value
+    cross = back[count * layers] + sent[count * layers]
     low = jnp.where(tile == 0, 0.0, 1.0)
-    high = 1.0 - low
-    cross = back[count * layers] + sent[count * layers]
-    bridge = other[(layers - 1) * tile]
-    products, falls = [low * cross], [low * (bridge - model[0])]
+    terms = spread(along[0][:-1], along[1], along[2], low * cross, (1.0 - low) * cross, cross.shape)
     for i in range(layers):
-        if i + 1 < layers:
-            total = sums[0, i]
-            for f, l in pairs:
-                total = total + (f(i) - f(i + 1)) * (l(i) - l(i + 1))
-            products.append(total)
-            falls.append(model[i] - model[i + 1])
-        else:
-            products.append(high * cross)
-            falls.append(high * (model[i] - bridge))
-    for i in range(layers):
-        total_y, total_z, mass = sums[1, i], sums[2, i], sums[3, i]
-        for f, l in pairs:
-            here, there = f(i), l(i)
-            total_y = total_y + face_prod(here, there, 0)
-            total_z = total_z + face_prod(here, there, 1)
-            mass = mass + here * there
-        total_y = jnp.where(in_y, total_y, 0.0)
-        total_z = jnp.where(in_z, total_z, 0.0)
-        terms = products[i] + products[i + 1]
-        terms = terms + (total_y + before(total_y, 0)) + (total_z + before(total_z, 1))
-        value = model[i]
-        fall_y = jnp.where(in_y, value - after(value, 0), 0.0)
-        fall_z = jnp.where(in_z, value - after(value, 1), 0.0)
-        space = falls[i + 1] - falls[i] + (fall_y - before(fall_y, 0)) + (fall_z - before(fall_z, 1))
-        result[i] = space + (times[i] + far[i]) - jnp.exp(value) * (0.5 * terms + GROUND * mass)
+        change = sigma[i] * (0.5 * terms[i] + GROUND * along[3][i])
+        result[i] = (base[i] + far[i]) - change
         copies.append(pltpu.make_async_copy(result.at[i], gradient.at[i], sems.at[i]))
         copies[-1].start()
     for copy in copies:
@@ -617,24 +627,23 @@
         scratch=[V((half, *slab), jnp.bfloat16), dma],
         micros=3,
     )
-    added, joint = call(
+    base, sigma, joint = call(
         gather_back,
-        (sums, back_first, forward, kept),
-        (V, V, V, H),
-        [f32(4, *slab), bf16(*forward.shape)],
-        [V, H],
-        scratch=[V((early, *slab), jnp.bfloat16), dma],
-        aliases={3: 1},
-        micros=1,
+        (sums, back_first, forward, model, other, times, kept),
+        (V, V, V, V, V, V, H),
+        [f32(*slab), f32(*slab), bf16(*forward.shape)],
+        [V, V, H],
+        scratch=[V((4, *slab), jnp.float32), V((early, *slab), jnp.bfloat16), dma],
+        aliases={6: 2},
     )
     adjoint, gradient = call(
         finish,
-        (added, back_second, sent_second, forward, model, other, times, far, joint),
-        (V, V, V, V, V, V, V, V, H),
+        (base, sigma, back_second, sent_second, forward, far, joint),
+        (V, V, V, V, V, V, H),
         [bf16(*forward.shape), f32(*slab)],
         [H, H],
         scratch=[V((late, *slab), jnp.bfloat16), V(slab, jnp.float32), dma((layers + 1,))],
-        aliases={8: 0},
+        aliases={6: 0},
     )
     return adjoint, gradient
 

time: 37.8 us -> 37.7 us (level)
  transfers between devices with their start and end apart: 8 -> 8, of which waited for: 5 -> 5; matrix products, arithmetic and copies ran while one was open for 0% -> 0% of each run, Pallas kernels for 19% -> 20%
where the time goes in v11:
time: 37.7 us; the launch traced here: 37.6 us
  waiting for transfers between devices  14.6 us (39%)
  starting transfers between devices  12.7 us (34%)
  Pallas kernels  8.4 us (22%)
  local copies, waits for them, and re-layouts  1.08 us (3%)
  between operations  0.78 us (2%)
    ppermute x8, waiting for transfers between devices, swap(): return lax.ppermute(x, 'space', links)  14.6 us
    ppermute x8, starting transfers between devices, swap(): return lax.ppermute(x, 'space', links)  12.7 us
    pallas_call x11, Pallas kernels, call(): pl.pallas_call(kernel, out_shape=out_shapes if several else out_shapes[0]...  8.4 us
    unnamed x14, local copies, waits for them, and re-layouts  1.08 us
  transfers between devices with their start and end apart: 8, of which 5 were waited for; matrix products, arithmetic and copies ran while one was open for 0% of the time, Pallas kernels for 20%

profile of v11, /device:TPU:1, one launch (start us, length us, event | category | flops | bytes accessed | tf_op | source)
XLA Modules:
  0.0 37.6 jit_solution(11574623296012080440)
XLA Ops:
  0.6 2.7 %collective-permute-start = (f32[4,64,128]{2,1,0:T(8,128)}, f32[4,64,128]{2,1,0:T(8,128)S(1)}, u32[]{:S(2)}, u32[]{:S(2)}) collective-permute-start(f32[4,64,128]{2,1,0:T(8,128)} %model.5), channel_id=1, source_target_pairs={{1,2},{2,1},{3,4},{4,3},{5,6},{6,5},{7,8},{8,7},{9,10},{10,9},{11,... | collective-permute-start | bytes 393224 | tf_op jit(solution)/shard_map/ppermute | solution.py:563
  3.3 0.0 copy-start
  3.3 1.0 %copy-done = bf16[8,4,64,128]{3,2,1,0:T(8,128)(2,1)S(1)} copy-done((bf16[8,4,64,128]{3,2,1,0:T(8,128)(2,1)S(1)}, bf16[8,4,64,128]{3,2,1,0:T(8,128)(2,1)}, u32[]{:S(2)}) %copy-start) | copy-done | bytes 524312
  4.4 0.0 copy-start.3
  4.4 0.0 copy-start.4
  4.4 0.0 copy-start.5
  4.4 0.0 copy-start.6
  4.4 0.1 collective-permute-start.1
  4.5 2.5 %collective-permute-done.other = f32[4,64,128]{2,1,0:T(8,128)S(1)} collective-permute-done((f32[4,64,128]{2,1,0:T(8,128)}, f32[4,64,128]{2,1,0:T(8,128)S(1)}, u32[]{:S(2)}, u32[]{:S(2)}) %collective-permute-start) | collective-permute-done | bytes 131104 | tf_op jit(solution)/shard_map/ppermute | solution.py:563
  7.0 2.2 %collective-permute-start.2 = (f32[4,64,128]{2,1,0:T(8,128)S(1)}, f32[4,64,128]{2,1,0:T(8,128)S(1)}, u32[]{:S(2)}, u32[]{:S(2)}) collective-permute-start(f32[4,64,128]{2,1,0:T(8,128)S(1)} %collective-permute-done.other), channel_id=1, source_target_pairs={{0,1},{1,0},{2,3},{3,2},{4,5},{5,4},{6,7},{7,6},{8,9},{9,8},{10,11... | collective-permute-start | bytes 393224 | tf_op jit(solution)/shard_map/ppermute | solution.py:563
  9.2 0.0 copy-done.3
  9.2 0.3 shard_map.77.coefs
  9.5 0.0 copy-done.4
  9.5 0.0 copy-done.5
  9.5 0.0 copy-done.6
  9.5 1.2 %shard_map.79 = (f32[4,8,64,128]{3,2,1,0:T(8,128)S(1)}, f32[8]{0:T(128)S(1)}) custom-call(s32[8]{0:T(128)S(1)} %copy-done.6, f32[8,8,256]{2,1,0:T(8,128)S(1)} %copy-done.4, s32[1,256]{1,0:T(1,128)S(1)} %bitcast.1, f32[7,8,64,128]{3,2,1,0:T(8,128)S(1)} %shard_map.77.coefs), custom_call_target="tpu_custom_call" | custom-call | flops 1000000000 | bytes 3000000 | tf_op jit(solution)/shard_map/pallas_call | solution.py:528
  10.7 0.0 collective-permute-done.2.beside
  10.7 0.0 copy-start.1
  10.8 0.0 copy-start.2
  10.8 0.6 %shard_map.81 = (f32[4,64,128]{2,1,0:T(8,128)S(1)}, f32[4,64,128]{2,1,0:T(8,128)S(1)}, f32[8,64,128]{2,1,0:T(8,128)S(1)}) custom-call(f32[8]{0:T(128)S(1)} %get-tuple-element.20.weights, f32[4,64,128]{2,1,0:T(8,128)S(1)} %copy-done.3, f32[4,64,128]{2,1,0:T(8,128)S(1)} %collective-permute-done.2.beside), custom_call_target="tpu_custom_call" | custom-call | flops 1000000000 | bytes 3000000 | tf_op jit(solution)/shard_map/pallas_call | solution.py:528
  11.4 4.1 %collective-permute-start.5 = (f32[8,64,128]{2,1,0:T(8,128)S(1)}, f32[8,64,128]{2,1,0:T(8,128)S(1)}, u32[]{:S(2)}, u32[]{:S(2)}) collective-permute-start(f32[8,64,128]{2,1,0:T(8,128)S(1)} %get-tuple-element.21.parts), channel_id=1, source_target_pairs={{0,4},{1,5},{2,6},{3,7},{4,0},{5,1},{6,2},{7,3},{8,12},{9,13},{10,... | collective-permute-start | bytes 786440 | tf_op jit(solution)/shard_map/ppermute | solution.py:563
  15.5 0.0 copy-done.1
  15.5 0.0 copy-done.2
  15.6 0.1 collective-permute-start.3
  15.6 1.3 %collective-permute-done.1.got = f32[3,4,64,128]{3,2,1,0:T(8,128)S(1)} collective-permute-done((f32[3,4,64,128]{3,2,1,0:T(8,128)S(1)}, f32[3,4,64,128]{3,2,1,0:T(8,128)S(1)}, u32[]{:S(2)}, u32[]{:S(2)}) %collective-permute-start.1) | collective-permute-done | bytes 393248 | tf_op jit(solution)/shard_map/ppermute | solution.py:563
  16.9 2.3 %shard_map.80 = (f32[3,4,64,128]{3,2,1,0:T(8,128)S(1)}, f32[12,64,128]{2,1,0:T(8,128)S(1)}) custom-call(f32[7,8,64,128]{3,2,1,0:T(8,128)S(1)} %shard_map.77.coefs, f32[3,4,64,128]{3,2,1,0:T(8,128)S(1)} %collective-permute-done.1.got, bf16[8,4,64,128]{3,2,1,0:T(8,128)(2,1)S(1)} %copy-done.1, f32[4,8,64,128]{3,2,1,0:T(8,128)S(1)} %get-tuple-element.18.rhs), custom_call_target="tpu_custom_call" | custom-call | flops 3000000000 | bytes 9000000 | tf_op jit(solution)/shard_map/pallas_call | solution.py:528
  19.2 0.9 %collective-permute-start.4 = (f32[12,64,128]{2,1,0:T(8,128)S(1)}, f32[12,64,128]{2,1,0:T(8,128)S(1)}, u32[]{:S(2)}, u32[]{:S(2)}) collective-permute-start(f32[12,64,128]{2,1,0:T(8,128)S(1)} %get-tuple-element.22.sent_first), channel_id=1, source_target_pairs={{1,2},{2,1},{3,4},{4,3},{5,6},{6,5},{7,8},{8,7},{9,10},{10,9},{11,... | collective-permute-start | bytes 1179656 | tf_op jit(solution)/shard_map/ppermute | solution.py:563
  20.1 1.6 %collective-permute-done.5.near = f32[8,64,128]{2,1,0:T(8,128)S(1)} collective-permute-done((f32[8,64,128]{2,1,0:T(8,128)S(1)}, f32[8,64,128]{2,1,0:T(8,128)S(1)}, u32[]{:S(2)}, u32[]{:S(2)}) %collective-permute-start.5) | collective-permute-done | bytes 262176 | tf_op jit(solution)/shard_map/ppermute | solution.py:563
  21.8 2.2 %collective-permute-start.7 = (f32[4,64,128]{2,1,0:T(8,128)S(1)}, f32[4,64,128]{2,1,0:T(8,128)S(1)}, u32[]{:S(2)}, u32[]{:S(2)}) collective-permute-start(f32[4,64,128]{2,1,0:T(8,128)S(1)} %get-tuple-element.32), channel_id=1, source_target_pairs={{0,8},{1,9},{2,10},{3,11},{4,12},{5,13},{6,14},{7,15},{8,0},{9,1},... | collective-permute-start | bytes 393224 | tf_op jit(solution)/shard_map/ppermute | solution.py:563
  24.0 0.0 collective-permute-done.3.got
  24.0 0.8 %shard_map.83 = (f32[1,4,64,128]{3,2,1,0:T(8,128)S(1)}, f32[5,64,128]{2,1,0:T(8,128)S(1)}) custom-call(f32[7,8,64,128]{3,2,1,0:T(8,128)S(1)} %shard_map.77.coefs, f32[8,64,128]{2,1,0:T(8,128)S(1)} %collective-permute-done.3.got, bf16[8,4,64,128]{3,2,1,0:T(8,128)(2,1)S(1)} %copy-done.1, f32[4,8,64,128]{3,2,1,0:T(8,128)S(1)} %get-tuple-element.18.rhs, ...), custom_call_target="tpu_custom_call" | custom-call | flops 3000000000 | bytes 9000000 | tf_op jit(solution)/shard_map/pallas_call | solution.py:528
  24.8 0.4 %collective-permute-start.6 = (f32[5,64,128]{2,1,0:T(8,128)S(1)}, f32[5,64,128]{2,1,0:T(8,128)S(1)}, u32[]{:S(2)}, u32[]{:S(2)}) collective-permute-start(f32[5,64,128]{2,1,0:T(8,128)S(1)} %get-tuple-element.31.sent), channel_id=1, source_target_pairs={{1,2},{2,1},{3,4},{4,3},{5,6},{6,5},{7,8},{8,7},{9,10},{10,9},{11,... | collective-permute-start | bytes 491528 | tf_op jit(solution)/shard_map/ppermute | solution.py:563
  25.2 1.1 %shard_map.84 = (f32[4,4,64,128]{3,2,1,0:T(8,128)S(1)}, bf16[8,4,64,128]{3,2,1,0:T(8,128)(2,1)}) custom-call(bf16[8,4,64,128]{3,2,1,0:T(8,128)(2,1)S(1)} %copy-done.2, f32[3,4,64,128]{3,2,1,0:T(8,128)S(1)} %get-tuple-element.19.own_first, f32[1,4,64,128]{3,2,1,0:T(8,128)S(1)} %get-tuple-element.23.own_second), custom_call_target="tpu_custom_call" | custom-call | flops 3000000000 | bytes 9000000 | tf_op jit(solution)/shard_map/pallas_call | solution.py:528
  26.3 8.7 %collective-permute-done.4.back = f32[12,64,128]{2,1,0:T(8,128)S(1)} collective-permute-done((f32[12,64,128]{2,1,0:T(8,128)S(1)}, f32[12,64,128]{2,1,0:T(8,128)S(1)}, u32[]{:S(2)}, u32[]{:S(2)}) %collective-permute-start.4) | collective-permute-done | bytes 393248 | tf_op jit(solution)/shard_map/ppermute | solution.py:563
  35.0 1.2 %shard_map.86 = (f32[4,64,128]{2,1,0:T(8,128)S(1)}, f32[4,64,128]{2,1,0:T(8,128)S(1)}, bf16[8,4,64,128]{3,2,1,0:T(8,128)(2,1)}) custom-call(f32[4,4,64,128]{3,2,1,0:T(8,128)S(1)} %get-tuple-element.24.sums, f32[12,64,128]{2,1,0:T(8,128)S(1)} %collective-permute-done.4.back, bf16[8,4,64,128]{3,2,1,0:T(8,128)(2,1)S(1)} %copy-done.2, ...), custom_call_target="tpu_custom_call", output_to_operand_aliasing={{2}: (6, {})} | custom-call | flops 1000000000 | bytes 3000000 | tf_op jit(solution)/shard_map/pallas_call | solution.py:528
  36.2 0.0 collective-permute-done.7.far
  36.2 0.5 %collective-permute-done.6.back = f32[5,64,128]{2,1,0:T(8,128)S(1)} collective-permute-done((f32[5,64,128]{2,1,0:T(8,128)S(1)}, f32[5,64,128]{2,1,0:T(8,128)S(1)}, u32[]{:S(2)}, u32[]{:S(2)}) %collective-permute-start.6) | collective-permute-done | bytes 163872 | tf_op jit(solution)/shard_map/ppermute | solution.py:563
  36.7 0.9 %shard_map.87 = (bf16[8,4,64,128]{3,2,1,0:T(8,128)(2,1)}, f32[4,64,128]{2,1,0:T(8,128)}) custom-call(f32[4,64,128]{2,1,0:T(8,128)S(1)} %get-tuple-element.29.base, f32[4,64,128]{2,1,0:T(8,128)S(1)} %get-tuple-element.30.sigma, f32[5,64,128]{2,1,0:T(8,128)S(1)} %collective-permute-done.6.back, ...), custom_call_target="tpu_custom_call", output_to_operand_aliasing={{0}: (6, {})} | custom-call | flops 1000000000 | bytes 3000000 | tf_op jit(solution)/shard_map/pallas_call | solution.py:528
  (3 shorter events, 0.1 us)
Async XLA Ops:
  0.6 6.4 %collective-permute-start = (f32[4,64,128]{2,1,0:T(8,128)}, f32[4,64,128]{2,1,0:T(8,128)S(1)}, u32[]{:S(2)}, u32[]{:S(2)}) collective-permute-start(f32[4,64,128]{2,1,0:T(8,128)} %model.5), channel_id=1, source_target_pairs={{1,2},{2,1},{3,4},{4,3},{5,6},{6,5},{7,8},{8,7},{9,10},{10,9},{11,... | collective-permute-start | bytes 393224 | tf_op jit(solution)/shard_map/ppermute | solution.py:563
  3.3 1.0 %copy-start = (bf16[8,4,64,128]{3,2,1,0:T(8,128)(2,1)S(1)}, bf16[8,4,64,128]{3,2,1,0:T(8,128)(2,1)}, u32[]{:S(2)}) copy-start(bf16[8,4,64,128]{3,2,1,0:T(8,128)(2,1)} %warm.7) | copy-start | bytes 1572868
  4.4 4.8 %copy-start.3 = (f32[4,64,128]{2,1,0:T(8,128)S(1)}, f32[4,64,128]{2,1,0:T(8,128)}, u32[]{:S(2)}) copy-start(f32[4,64,128]{2,1,0:T(8,128)} %model.5) | copy-start | bytes 393220
  4.4 5.1 %copy-start.4 = (f32[8,8,256]{2,1,0:T(8,128)S(1)}, f32[8,8,256]{2,1,0:T(8,128)}, u32[]{:S(2)}) copy-start(f32[8,8,256]{2,1,0:T(8,128)} %residual.1) | copy-start | bytes 196612
  4.4 5.1 %copy-start.5 = (s32[256]{0:T(256)S(1)}, s32[256]{0:T(256)}, u32[]{:S(2)}) copy-start(s32[256]{0:T(256)} %param.10) | copy-start | bytes 3076
  4.4 5.1 %copy-start.6 = (s32[8]{0:T(128)S(1)}, s32[8]{0:T(128)}, u32[]{:S(2)}) copy-start(s32[8]{0:T(128)} %order.1) | copy-start | bytes 100
  4.4 12.5 %collective-permute-start.1 = (f32[3,4,64,128]{3,2,1,0:T(8,128)S(1)}, f32[3,4,64,128]{3,2,1,0:T(8,128)S(1)}, u32[]{:S(2)}, u32[]{:S(2)}) collective-permute-start(f32[3,4,64,128]{3,2,1,0:T(8,128)S(1)} %shard_map.78), channel_id=1, source_target_pairs={{1,2},{2,1},{3,4},{4,3},{5,6},{6,5},{7,8},{8,7},{9,10},{10,9},{11,... | collective-permute-start | bytes 1179656 | tf_op jit(solution)/shard_map/ppermute | solution.py:563
  7.0 3.7 %collective-permute-start.2 = (f32[4,64,128]{2,1,0:T(8,128)S(1)}, f32[4,64,128]{2,1,0:T(8,128)S(1)}, u32[]{:S(2)}, u32[]{:S(2)}) collective-permute-start(f32[4,64,128]{2,1,0:T(8,128)S(1)} %collective-permute-done.other), channel_id=1, source_target_pairs={{0,1},{1,0},{2,3},{3,2},{4,5},{5,4},{6,7},{7,6},{8,9},{9,8},{10,11... | collective-permute-start | bytes 393224 | tf_op jit(solution)/shard_map/ppermute | solution.py:563
  10.7 4.8 %copy-start.1 = (bf16[8,4,64,128]{3,2,1,0:T(8,128)(2,1)S(1)}, bf16[8,4,64,128]{3,2,1,0:T(8,128)(2,1)}, u32[]{:S(2)}) copy-start(bf16[8,4,64,128]{3,2,1,0:T(8,128)(2,1)} %warm.7) | copy-start | bytes 1572868
  10.8 4.8 %copy-start.2 = (bf16[8,4,64,128]{3,2,1,0:T(8,128)(2,1)S(1)}, bf16[8,4,64,128]{3,2,1,0:T(8,128)(2,1)}, u32[]{:S(2)}) copy-start(bf16[8,4,64,128]{3,2,1,0:T(8,128)(2,1)} %forward.9) | copy-start | bytes 1572868
  11.4 10.4 %collective-permute-start.5 = (f32[8,64,128]{2,1,0:T(8,128)S(1)}, f32[8,64,128]{2,1,0:T(8,128)S(1)}, u32[]{:S(2)}, u32[]{:S(2)}) collective-permute-start(f32[8,64,128]{2,1,0:T(8,128)S(1)} %get-tuple-element.21.parts), channel_id=1, source_target_pairs={{0,4},{1,5},{2,6},{3,7},{4,0},{5,1},{6,2},{7,3},{8,12},{9,13},{10,... | collective-permute-start | bytes 786440 | tf_op jit(solution)/shard_map/ppermute | solution.py:563
  15.6 8.4 %collective-permute-start.3 = (f32[8,64,128]{2,1,0:T(8,128)S(1)}, f32[8,64,128]{2,1,0:T(8,128)S(1)}, u32[]{:S(2)}, u32[]{:S(2)}) collective-permute-start(f32[8,64,128]{2,1,0:T(8,128)S(1)} %shard_map.82), channel_id=1, source_target_pairs={{1,2},{2,1},{3,4},{4,3},{5,6},{6,5},{7,8},{8,7},{9,10},{10,9},{11,... | collective-permute-start | bytes 786440 | tf_op jit(solution)/shard_map/ppermute | solution.py:563
  19.2 15.8 %collective-permute-start.4 = (f32[12,64,128]{2,1,0:T(8,128)S(1)}, f32[12,64,128]{2,1,0:T(8,128)S(1)}, u32[]{:S(2)}, u32[]{:S(2)}) collective-permute-start(f32[12,64,128]{2,1,0:T(8,128)S(1)} %get-tuple-element.22.sent_first), channel_id=1, source_target_pairs={{1,2},{2,1},{3,4},{4,3},{5,6},{6,5},{7,8},{8,7},{9,10},{10,9},{11,... | collective-permute-start | bytes 1179656 | tf_op jit(solution)/shard_map/ppermute | solution.py:563
  21.8 14.4 %collective-permute-start.7 = (f32[4,64,128]{2,1,0:T(8,128)S(1)}, f32[4,64,128]{2,1,0:T(8,128)S(1)}, u32[]{:S(2)}, u32[]{:S(2)}) collective-permute-start(f32[4,64,128]{2,1,0:T(8,128)S(1)} %get-tuple-element.32), channel_id=1, source_target_pairs={{0,8},{1,9},{2,10},{3,11},{4,12},{5,13},{6,14},{7,15},{8,0},{9,1},... | collective-permute-start | bytes 393224 | tf_op jit(solution)/shard_map/ppermute | solution.py:563
  24.8 11.9 %collective-permute-start.6 = (f32[5,64,128]{2,1,0:T(8,128)S(1)}, f32[5,64,128]{2,1,0:T(8,128)S(1)}, u32[]{:S(2)}, u32[]{:S(2)}) collective-permute-start(f32[5,64,128]{2,1,0:T(8,128)S(1)} %get-tuple-element.31.sent), channel_id=1, source_target_pairs={{1,2},{2,1},{3,4},{4,3},{5,6},{6,5},{7,8},{8,7},{9,10},{10,9},{11,... | collective-permute-start | bytes 491528 | tf_op jit(solution)/shard_map/ppermute | solution.py:563
